TPU v7x, 32 devices: a whole 2x2x4 slice. The times are simulated.
32 devices in a mesh: row: 2 (over x), col: 4 (over y, core), item: 4 (over z).
Axes of the slice: x: 2, y: 2, z: 4, core: 2. Of those that a mesh axis runs over, the one named last changes fastest.
Arguments:
- tokens: bfloat16 [4, 2, 64, 2432], P('item', 'row', 'col'), may hold values from -6 to 6
- text_keys_values: bfloat16 [4, 154, 2, 2048], P('item', None, None, 'row'), may hold values from -200 to 200
- text_length: int32 [4], P('item'), may hold values from 2 to 154, as said below
- modulation: float32 [4, 8, 2432], P('item'), may hold values from -4 to 4
- input_weight: bfloat16 [2432, 3, 2048], P(None, None, 'row'), may hold values from -0.125 to 0.125
- norm_gain: float32 [2, 64], replicated, may hold values from 1 to 3
- output_weight: bfloat16 [2048, 2432], P('row'), may hold values from -0.125 to 0.125
- up_weight: bfloat16 [2432, 9728], P(None, 'row'), may hold values from -0.125 to 0.125
- down_weight: bfloat16 [9728, 2432], P('row'), may hold values from -0.0625 to 0.0625
- final_weight: bfloat16 [2432, 64], replicated, may hold values from -0.125 to 0.125
- step_index: int32 [1], replicated, may hold values from 0 to 27
- latent: float32 [4, 2, 4096], P('item', 'row', 'col'), may hold values from -6 to 6
Outputs:
- tokens_out: bfloat16 [4, 2, 64, 2432], P('item', 'row', 'col')
- velocity: float32 [4, 2, 4096], P('item', 'row', 'col')
- latent_next: float32 [4, 2, 4096], P('item', 'row', 'col')
Inputs may be any that keep to these rules, and one draw needn't show every extreme that they name: `text_length`: at least one sequence has all 154 text tokens valid.
All inputs are finite; a program needn't handle non-finite values.
Results may differ from a plain program's by a relative error of at most 0.024.
Values may be sent and summed in bfloat16 or wider, within the bound.
No kernel may reach another device: no remote copies, remote signals or barrier semaphores. Data moves between devices by JAX's collectives and lax.ppermute only.
A program may use at most 128 MiB of HBM per device.

v0:
```python
import jax
import jax.numpy as jnp
from jax import lax
from jax.sharding import PartitionSpec as P

HD = 64
STEPS = 28


EPSILON = 1e-06
SHIFT_FACTOR = 3.0
GUIDANCE = 4.5
MASKED = -1e30


def partner_2(value, axis, apart):
    mask = 2**apart
    pairs = [(source, source ^ mask) for source in range(lax.axis_size(axis))]
    return lax.ppermute(value, axis, pairs)


def layer_norm(values):
    center = values - jnp.mean(values, axis=-1, keepdims=True)
    spread = jnp.mean(center * center, axis=-1, keepdims=True)
    return center * lax.rsqrt(spread + EPSILON)


def modulate(values, shift_term, scale_term):
    return (layer_norm(values) * (1.0 + scale_term) + shift_term).astype(jnp.bfloat16)


def root_norm(values, gain_row):
    return (
        values * lax.rsqrt(jnp.mean(values * values, axis=-1, keepdims=True) + EPSILON) * gain_row
    )


def noise_level(position):
    linear = 1.0 - position / STEPS
    return SHIFT_FACTOR * linear / (1.0 + (SHIFT_FACTOR - 1.0) * linear)


def on_device(
    tokens,
    text_keys_values,
    text_length,
    modulation,
    input_weight,
    norm_gain,
    output_weight,
    up_weight,
    down_weight,
    final_weight,
    step_index,
    latent,
):
    tile_rows = tokens.shape[1] * tokens.shape[2]
    model_width = tokens.shape[3]
    mod_rows = modulation[0]
    row_position = lax.axis_index("row")
    stripe_tokens = lax.all_gather(tokens, "row", axis=1, tiled=True)
    stripe_states = stripe_tokens.reshape(-1, model_width).astype(jnp.float32)
    stripe_rows = stripe_states.shape[0]
    local_width = input_weight.shape[2]
    local_heads = local_width // HD
    attn_input = modulate(stripe_states, mod_rows[0], mod_rows[1])
    projected = jnp.dot(
        attn_input,
        input_weight.reshape(model_width, 3 * local_width),
        preferred_element_type=jnp.float32,
    )
    projected = projected.reshape(stripe_rows, 3, local_heads, HD)
    queries = root_norm(projected[:, 0], norm_gain[0]).astype(jnp.bfloat16).transpose(1, 0, 2)
    keys_image = (
        root_norm(projected[:, 1], norm_gain[1])
        .astype(jnp.bfloat16)
        .reshape(stripe_rows, local_width)
    )
    values_image = projected[:, 2].astype(jnp.bfloat16).reshape(stripe_rows, local_width)
    text_pairs = text_keys_values[0]
    keys_text = text_pairs[:, 0].reshape(-1, local_heads, HD)
    values_text = text_pairs[:, 1].reshape(-1, local_heads, HD)
    text_valid = jnp.arange(keys_text.shape[0]) < text_length[0]
    text_scores = jnp.einsum(
        "hsd,thd->hst", queries, keys_text, preferred_element_type=jnp.float32
    ) * HD ** (-0.5)
    text_scores = jnp.where(text_valid[None, None, :], text_scores, MASKED)
    largest = jnp.max(text_scores, axis=-1)
    text_weights = jnp.exp(text_scores - largest[..., None])
    total_mass = jnp.sum(text_weights, axis=-1)
    weighted = jnp.einsum(
        "hst,thd->hsd",
        text_weights.astype(jnp.bfloat16),
        values_text,
        preferred_element_type=jnp.float32,
    )

    def one_block(running, block_pair):
        running_max, running_mass, running_sum = running
        key_block, value_block = block_pair
        scores = jnp.einsum(
            "hsd,khd->hsk", queries, key_block, preferred_element_type=jnp.float32
        ) * HD ** (-0.5)
        new_max = jnp.maximum(running_max, jnp.max(scores, axis=-1))
        factor = jnp.exp(running_max - new_max)
        weights = jnp.exp(scores - new_max[..., None])
        new_mass = running_mass * factor + jnp.sum(weights, axis=-1)
        new_sum = running_sum * factor[..., None] + jnp.einsum(
            "hsk,khd->hsd",
            weights.astype(jnp.bfloat16),
            value_block,
            preferred_element_type=jnp.float32,
        )
        return ((new_max, new_mass, new_sum), None)

    key_piece = lax.all_gather(keys_image, "col", axis=0, tiled=True)
    value_piece = lax.all_gather(values_image, "col", axis=0, tiled=True)
    blocks = key_piece.shape[0] // stripe_rows
    key_blocks = key_piece.reshape(blocks, stripe_rows, local_heads, HD)
    value_blocks = value_piece.reshape(blocks, stripe_rows, local_heads, HD)
    result, unused = lax.scan(
        one_block, (largest, total_mass, weighted), (key_blocks, value_blocks)
    )
    largest, total_mass, weighted = result
    attended = (
        (weighted / total_mass[..., None])
        .astype(jnp.bfloat16)
        .transpose(1, 0, 2)
        .reshape(stripe_rows, local_width)
    )
    attention = lax.psum(
        jnp.dot(attended, output_weight, preferred_element_type=jnp.float32).astype(jnp.bfloat16),
        "row",
    ).astype(jnp.float32)
    stripe_middle = stripe_states + mod_rows[2] * attention
    feed_input = modulate(stripe_middle, mod_rows[3], mod_rows[4])
    hidden = jax.nn.gelu(
        jnp.dot(feed_input, up_weight, preferred_element_type=jnp.float32), approximate=True
    ).astype(jnp.bfloat16)
    middle = lax.dynamic_slice_in_dim(stripe_middle, row_position * tile_rows, tile_rows, 0)
    feed = lax.psum_scatter(
        jnp.dot(hidden, down_weight, preferred_element_type=jnp.float32).astype(jnp.bfloat16),
        "row",
        scatter_dimension=0,
        tiled=True,
    ).astype(jnp.float32)
    leaving = middle + mod_rows[5] * feed
    tokens_out = leaving.astype(jnp.bfloat16).reshape(tokens.shape)
    final_input = modulate(leaving, mod_rows[6], mod_rows[7])
    raw_velocity = jnp.dot(final_input, final_weight, preferred_element_type=jnp.float32).reshape(
        1, tokens.shape[1], -1
    )
    partner = partner_2(raw_velocity, "item", 0)
    is_guided = lax.axis_index("item") % 2 == 0
    guided = jnp.where(is_guided, raw_velocity, partner)
    unguided = jnp.where(is_guided, partner, raw_velocity)
    velocity = unguided + GUIDANCE * (guided - unguided)
    position = step_index[0].astype(jnp.float32)
    step_size = noise_level(position + 1.0) - noise_level(position)
    return (tokens_out, velocity, latent + step_size * velocity)


def solution(mesh):
    in_specs = (
        P("item", "row", "col", None),
        P("item", None, None, "row"),
        P("item"),
        P("item", None, None),
        P(None, None, "row"),
        P(),
        P("row", None),
        P(None, "row"),
        P("row", None),
        P(),
        P(),
        P("item", "row", "col"),
    )
    out_specs = (P("item", "row", "col", None), P("item", "row", "col"), P("item", "row", "col"))
    return jax.shard_map(
        on_device, mesh=mesh, in_specs=in_specs, out_specs=out_specs, check_vma=False
    )
```

profile of v0, /device:TPU:0, one launch (start us, length us, event | category | flops | bytes accessed | tf_op | source)
XLA Modules:
  0.0 142.9 jit_solution(4607685740456688238)
XLA Ops:
  7.2 6.4 %all_gather.9 = bf16[1,2,16,2432]{3,2,0,1:T(8,128)(2,1)S(1)} all-gather(bf16[1,1,16,2432]{3,2,0,1:T(8,128)(2,1)} %bitcast.78), channel_id=1, replica_groups=mesh['row'=2,'col'=4,'item'=4] {'row'}, dimensions={1}, use_global_device_ids=true | all-gather | bytes 233472 | tf_op jit(solution)/shard_map/all_gather | solution.py:61
  13.9 1.8 %add_reduce_fusion = (f32[2432]{0:T(1024)S(1)}, f32[2432]{0:T(1024)S(1)}, f32[2432]{0:T(1024)S(1)}, f32[2432]{0:T(1024)S(1)}, f32[2432]{0:T(1024)S(1)}, /*index=...) fusion(f32[1,8,2432]{2,1,0:T(8,128)} %param.17), kind=kLoop, calls=%fused_computation.65 | loop fusion | flops 7296 | bytes 155648 | tf_op jit(solution)/shard_map/add | solution.py:29
  15.7 18.6 %copy.31 = bf16[2432,3,1024]{0,2,1:T(8,128)(2,1)} copy(bf16[2432,3,1024]{2,0,1:T(8,128)(2,1)} %param.18) | data formatting | bytes 29884416 | tf_op args[4]
  34.4 10.5 %fusion.49 = f32[32,3,16,64]{3,0,2,1:T(8,128)S(1)} fusion(bf16[32,2432,1,1]{1,0,3,2:T(8,128)(2,1)S(1)} %bitcast.77, bf16[3,16,64,2432]{3,2,1,0:T(8,128)(2,1)} %bitcast.73), kind=kOutput, calls=%fused_computation.98 | convolution fusion | flops 478150656 | bytes 15491072 | tf_op jit(solution)/shard_map/dot_general | solution.py:67
  45.0 0.7 multiply_reduce_fusion.2
  45.7 0.7 slice.93
  46.4 0.9 fusion.47
  50.4 1.1 copy.34
  51.7 6.3 %all_gather.10 = bf16[128,1024]{1,0:T(8,128)(2,1)S(1)} all-gather(bf16[32,1024]{1,0:T(8,128)(2,1)S(1)} %multiply_convert_fusion.1), channel_id=1, replica_groups=mesh['row'=2,'col'=4,'item'=4] {'col'}, dimensions={0}, use_global_device_ids=true | all-gather | bytes 327680 | tf_op jit(solution)/shard_map/all_gather | solution.py:116
  58.3 1.0 copy.36
  59.5 5.9 %all_gather.11 = bf16[128,1024]{1,0:T(8,128)(2,1)S(1)} all-gather(bf16[32,1024]{1,0:T(8,128)(2,1)S(1)} %convert_element_type.74), channel_id=1, replica_groups=mesh['row'=2,'col'=4,'item'=4] {'col'}, dimensions={0}, use_global_device_ids=true | all-gather | bytes 327680 | tf_op jit(solution)/shard_map/all_gather | solution.py:117
  65.7 2.7 %while.14 = (s32[]{:T(128)}, f32[16,32]{1,0:T(8,128)S(1)}, f32[16,32]{1,0:T(8,128)S(1)}, f32[16,32,64]{2,1,0:T(8,128)S(1)}, bf16[4,32,16,64]{3,2,1,0:T(8,128)(2,...) while((s32[]{:T(128)}, f32[16,32]{1,0:T(8,128)S(1)}, ...), condition=%wide.region_9.10_spmd, body=%wide.region_6.9_spmd.sunk | while | flops 4359170 | bytes 950361 | solution.py:121
  68.7 4.0 %convolution_convert_fusion.1 = bf16[32,2432]{1,0:T(8,128)(2,1)} fusion(bf16[32,1024]{1,0:T(8,128)(2,1)S(1)} %reshape.192, bf16[1024,2432]{1,0:T(8,128)(2,1)} %param.20), kind=kOutput, calls=%fused_computation.14 | convolution fusion | flops 159461376 | bytes 5201920 | tf_op jit(solution)/shard_map/dot_general | solution.py:132
  72.8 23.2 %all-reduce.2.cloned.1.call-done = bf16[32,2432]{1,0:T(8,128)(2,1)} async-done(((bf16[32,2432]{1,0:T(8,128)(2,1)}), bf16[32,2432]{1,0:T(8,128)(2,1)}) %all-reduce.2.cloned.1.call-update) | async-done | bytes 155664 | tf_op jit(solution)/shard_map/psum | solution.py:131
  95.9 1.1 fusion.45
  97.3 9.6 %fusion.24 = f32[32,4864]{1,0:T(8,128)S(1)} fusion(bf16[2432,4864]{1,0:T(8,128)(2,1)} %param.21, f32[32,2432]{1,0:T(8,128)S(1)} %get-tuple-element.84, f32[2432]{0:T(1024)S(1)} %get-tuple-element.58, f32[2432]{0:T(1024)S(1)} %get-tuple-element.59, f32[32]{0:T(128)S(1)} %add_rsqrt_fusion.4, f32[32]{0:T(128)S(1)} %broadcast_multiply_fusion.2), kind=kOutput, calls=%fused_computation.47 | convolution fusion | flops 757460992 | bytes 24612096 | tf_op jit(solution)/shard_map/dot_general | solution.py:138
  106.9 10.2 %convolution_convert_fusion = bf16[32,2432]{1,0:T(8,128)(2,1)} fusion(bf16[4864,2432]{1,0:T(8,128)(2,1)} %param.22, f32[32,4864]{1,0:T(8,128)S(1)} %fusion.24), kind=kOutput, calls=%fused_computation.13 | convolution fusion | flops 758550528 | bytes 24436736 | tf_op jit(solution)/shard_map/dot_general | solution.py:142
  117.1 10.8 %reduce-scatter.2.cloned.1.call-done = bf16[16,2432]{1,0:T(8,128)(2,1)} async-done(((bf16[32,2432]{1,0:T(8,128)(2,1)}), bf16[16,2432]{1,0:T(8,128)(2,1)}) %reduce-scatter.2.cloned.1.call-update) | async-done | bytes 77840 | tf_op jit(solution)/shard_map/reduce_scatter | solution.py:141
  127.9 1.0 fusion.43
  129.0 1.7 %multiply_reduce_fusion.4 = (f32[16]{0:T(128)S(1)}, bf16[1,1,16,2432]{3,2,1,0:T(8,128)(2,1)}) fusion(f32[16]{0:T(128)S(1)} %broadcast_multiply_fusion.1, bf16[16,2432]{1,0:T(8,128)(2,1)} %reduce-scatter.2.cloned.1.call-done, f32[2432]{0:T(1024)S(1)} %get-tuple-element.60, f32[32,2432]{1,0:T(8,128)S(1)} %get-tuple-element.84, s32[]{:T(128)S(6)} %select_n.27), kind=kLoop, calls=%fused_computation.49 | loop fusion | flops 272368 | bytes 321156 | tf_op jit(solution)/shard_map/reduce_sum | solution.py:24
  130.6 1.1 fusion.31
  131.8 1.5 %collective-permute-start = (f32[1,1,1024]{2,1,0:T(1,128)S(1)}, f32[1,1,1024]{2,1,0:T(1,128)S(1)}, u32[]{:S(2)}, u32[]{:S(2)}) collective-permute-start(f32[1,1,1024]{2,1,0:T(1,128)S(1)} %reshape.194), channel_id=1, source_target_pairs={{0,1},{1,0},{2,3},{3,2},{4,5},{5,4},{6,7},{7,6},{8,9},{9,8},{10,11... | collective-permute-start | bytes 12296 | tf_op jit(solution)/shard_map/ppermute | solution.py:19
  134.1 1.4 collective-permute-done
  135.5 0.6 multiply_add_fusion.2
  (75 shorter events, 7.2 us)
Async XLA Ops:
  7.2 123.5 %copy-start = (bf16[2432,64]{0,1:T(8,128)(2,1)S(1)}, bf16[2432,64]{0,1:T(8,128)(2,1)}, u32[]{:S(2)}) copy-start(bf16[2432,64]{0,1:T(8,128)(2,1)} %param.23) | copy-start | bytes 933892
  7.2 88.8 %all-reduce.2.cloned.1.call-start = ((), (), s32[]{:S(2)}) async-start(), calls=%async_computation.1 | async-start | bytes 311296 | tf_op jit(solution)/shard_map/psum | solution.py:131
  34.2 12.2 %copy-start.3 = (f32[2,64]{1,0:T(2,128)S(1)}, f32[2,64]{1,0:T(2,128)}, u32[]{:S(2)}) copy-start(f32[2,64]{1,0:T(2,128)} %param.19) | copy-start | bytes 1540
  34.2 12.2 %copy-start.1 = (bf16[1,154,2,1024]{3,2,1,0:T(2,128)(2,1)S(1)}, bf16[1,154,2,1024]{3,2,1,0:T(2,128)(2,1)}, u32[]{:S(2)}) copy-start(bf16[1,154,2,1024]{3,2,1,0:T(2,128)(2,1)} %param.15) | copy-start | bytes 1892356
  72.7 55.2 %reduce-scatter.2.cloned.1.call-start = ((), (), s32[]{:S(2)}) async-start(), calls=%async_computation.2 | async-start | bytes 233472 | tf_op jit(solution)/shard_map/reduce_scatter | solution.py:141
  106.9 28.6 %copy-start.2 = (f32[1,1,1024]{2,1,0:T(1,128)S(1)}, f32[1,1,1024]{2,1,0:T(1,128)}, u32[]{:S(2)}) copy-start(f32[1,1,1024]{2,1,0:T(1,128)} %param.25) | copy-start | bytes 12292
  131.8 3.6 %collective-permute-start = (f32[1,1,1024]{2,1,0:T(1,128)S(1)}, f32[1,1,1024]{2,1,0:T(1,128)S(1)}, u32[]{:S(2)}, u32[]{:S(2)}) collective-permute-start(f32[1,1,1024]{2,1,0:T(1,128)S(1)} %reshape.194), channel_id=1, source_target_pairs={{0,1},{1,0},{2,3},{3,2},{4,5},{5,4},{6,7},{7,6},{8,9},{9,8},{10,11... | collective-permute-start | bytes 12296 | tf_op jit(solution)/shard_map/ppermute | solution.py:19
Sparse Core Ops, SparseCore 0:
  72.8 23.0 all-reduce.1
  117.2 10.6 reduce-scatter.1
where the time goes:
time: 144 us; the launch traced here: 143 us
  matrix products  38 us (26%)
  waiting for transfers between devices  35.4 us (25%)
  local copies, waits for them, and re-layouts  25 us (17%)
  blocking collectives  18.5 us (13%)
  between operations  15.6 us (11%)
  other arithmetic  8.58 us (6%)
  starting transfers between devices  1.59 us (1%)
    psum x1, waiting for transfers between devices, on_device(): lax.psum(jnp.dot(attended, output_weight, preferred_element_type=jnp.floa...  23.2 us
    unnamed x9, local copies, waits for them, and re-layouts  18.6 us
    reduce_scatter x1, waiting for transfers between devices, on_device(): lax.psum_scatter(jnp.dot(hidden, down_weight, preferred_element_type=jnp....  10.8 us
    dot_general x1, matrix products, on_device(): jnp.dot(attn_input, input_weight.reshape(model_width, 3 * local_width), p...  10.5 us
    dot_general x1, matrix products, on_device(): jnp.dot(hidden, down_weight, preferred_element_type=jnp.float32)  10.2 us
    dot_general x1, matrix products, on_device(): jnp.dot(feed_input, up_weight, preferred_element_type=jnp.float32)  9.61 us
    all_gather x1, blocking collectives, on_device(): stripe_tokens = lax.all_gather(tokens, 'row', axis=1, tiled=True)  6.38 us
    all_gather x1, blocking collectives, on_device(): key_piece = lax.all_gather(keys_image, 'col', axis=0, tiled=True)  6.26 us
  transfers between devices with their start and end apart: 3, of which 3 were waited for; matrix products, arithmetic and copies ran while one was open for 0% of the time, Pallas kernels for 0%

commit v1 on v0

v1 whole, which is shorter than its diff:
```python
import functools

import jax
import jax.numpy as jnp
from jax import lax
from jax.experimental import pallas as pl
from jax.experimental.pallas import tpu as pltpu
from jax.sharding import PartitionSpec as P

HD = 64
STEPS = 28

EPSILON = 1e-06
SHIFT_FACTOR = 3.0
GUIDANCE = 4.5
MASKED = -1e30

LANES = 128
TILE = 256
ROWS = 16
SCOPED = 12 << 20

IN_VMEM = pl.BlockSpec(memory_space=pltpu.VMEM)
IN_SMEM = pl.BlockSpec(memory_space=pltpu.SMEM)
IN_PLACE = pl.BlockSpec(memory_space=pl.ANY)


def noise_level(position):
    linear = 1.0 - position / STEPS
    return SHIFT_FACTOR * linear / (1.0 + (SHIFT_FACTOR - 1.0) * linear)


def layer_norm(values):
    center = values - jnp.mean(values, axis=-1, keepdims=True)
    spread = jnp.mean(center * center, axis=-1, keepdims=True)
    return center * lax.rsqrt(spread + EPSILON)


def modulated(values, mod_ref, shift_row, scale_row):
    scale = 1.0 + mod_ref[scale_row : scale_row + 1, :]
    shift = mod_ref[shift_row : shift_row + 1, :]
    return (layer_norm(values) * scale + shift).astype(jnp.bfloat16)


def spans(width, step):
    return [(low, min(step, width - low)) for low in range(0, width, step)]


def for_rows(rows, step, body):
    if rows <= 2 * LANES:
        for low in range(0, rows, step):
            body(low)
    else:
        pl.loop(0, rows // step)(lambda at: body(pl.multiple_of(at * step, step)))


def in_hbm(array):
    return pltpu.with_memory_space_constraint(array, pltpu.HBM)


def in_vmem(array):
    return pltpu.with_memory_space_constraint(array, pltpu.VMEM)


def bytes_of(arrays):
    return sum(a.size * a.dtype.itemsize for a in arrays)


def fetch_kernel(parts, *refs):
    sources = refs[: len(refs) - len(parts) - 1]
    targets = refs[len(sources) : -1]
    sems = refs[-1]
    copies = [
        pltpu.make_async_copy(sources[at].at[pl.ds(low, size)], target, sems.at[index])
        for index, ((at, low, size), target) in enumerate(zip(parts, targets))
    ]
    for copy in copies:
        copy.start()
    for copy in copies:
        copy.wait()


def fetch(sources, parts):
    shapes = [(size,) + sources[at].shape[1:] for at, low, size in parts]
    moved = sum(2 * functools.reduce(lambda a, b: a * b, shape) for shape in shapes)
    return pl.pallas_call(
        functools.partial(fetch_kernel, parts),
        out_shape=[pltpu.VMEM(shape, jnp.bfloat16) for shape in shapes],
        in_specs=[IN_PLACE] * len(sources),
        out_specs=[IN_VMEM] * len(parts),
        scratch_shapes=[pltpu.SemaphoreType.DMA((len(parts),))],
        compiler_params=pltpu.CompilerParams(vmem_limit_bytes=SCOPED),
        cost_estimate=pl.CostEstimate(flops=0, bytes_accessed=2 * moved, transcendentals=0),
    )(*[in_hbm(source) for source in sources])


def attention_kernel(n_blocks, own_rows, up_low, *refs):
    blocks = refs[:n_blocks]
    (length, mod, gains, text, in_w, out_w, up_hbm, out, up_part) = refs[n_blocks : n_blocks + 9]
    normed, q_ref, k_ref, v_ref, att_ref, sem = refs[n_blocks + 9 :]
    up_copy = pltpu.make_async_copy(up_hbm.at[pl.ds(up_low, up_part.shape[0])], up_part, sem)
    up_copy.start()

    all_rows, width = normed.shape
    local = in_w.shape[2]
    low = 0
    for block in blocks:

        def norm_rows(at, block=block, low=low):
            values = block[pl.ds(at, ROWS), :].astype(jnp.float32)
            normed[pl.ds(low + at, ROWS), :] = modulated(values, mod, 0, 1)

        for_rows(block.shape[0], ROWS, norm_rows)
        low += block.shape[0]

    tile = min(TILE, local)
    head_of_row = lax.broadcasted_iota(jnp.int32, (tile, tile), 0) // HD
    head_of_col = lax.broadcasted_iota(jnp.int32, (tile, tile), 1) // HD
    same_head = (head_of_row == head_of_col).astype(jnp.bfloat16)

    def head_norm(values, gain):
        squares = values * values
        high = squares.astype(jnp.bfloat16)
        rest = (squares - high.astype(jnp.float32)).astype(jnp.bfloat16)
        total = jnp.dot(high, same_head, preferred_element_type=jnp.float32)
        total += jnp.dot(rest, same_head, preferred_element_type=jnp.float32)
        return values * lax.rsqrt(total * (1.0 / HD) + EPSILON) * gain

    for at, size in spans(local, tile):
        cols = slice(at, at + size)

        def project(first, rows, part):
            return jnp.dot(
                normed[pl.ds(first, rows), :],
                in_w[part, :, cols],
                preferred_element_type=jnp.float32,
            )

        def keys_values(first):
            rows = min(LANES, all_rows)
            k_ref[pl.ds(first, rows), cols] = head_norm(
                project(first, rows, 1), gains[1:2, :size]
            ).astype(jnp.bfloat16)
            v_ref[pl.ds(first, rows), cols] = project(first, rows, 2).astype(jnp.bfloat16)

        def queries(first):
            rows = min(LANES, own_rows)
            q_ref[pl.ds(first, rows), cols] = head_norm(
                project(first, rows, 0), gains[0:1, :size]
            ).astype(jnp.bfloat16)

        for_rows(own_rows, min(LANES, own_rows), queries)
        for_rows(all_rows, min(LANES, all_rows), keys_values)

    text_rows = text.shape[1]
    used = lax.broadcasted_iota(jnp.int32, (1, text_rows), 1) < length[0]
    first_head = lax.broadcasted_iota(jnp.int32, (1, LANES), 1) < HD
    contract = (((1,), (1,)), ((), ()))
    for at, size in spans(local, LANES):
        cols = slice(at, at + size)
        q = q_ref[:, cols]
        zero = jnp.zeros_like(q)
        pair = jnp.concatenate([jnp.where(first_head, q, zero), jnp.where(first_head, zero, q)], 0)
        scores = HD ** (-0.5) * lax.dot_general(
            pair, k_ref[:, cols], contract, preferred_element_type=jnp.float32
        )
        text_scores = HD ** (-0.5) * lax.dot_general(
            pair, text[0, :, cols], contract, preferred_element_type=jnp.float32
        )
        text_scores = jnp.where(used, text_scores, MASKED)
        largest = jnp.maximum(
            jnp.max(scores, axis=-1, keepdims=True), jnp.max(text_scores, axis=-1, keepdims=True)
        )
        weights = jnp.exp(scores - largest)
        text_weights = jnp.exp(text_scores - largest)
        total = jnp.sum(weights, axis=-1, keepdims=True)
        total += jnp.sum(text_weights, axis=-1, keepdims=True)
        mixed = jnp.dot(
            weights.astype(jnp.bfloat16), v_ref[:, cols], preferred_element_type=jnp.float32
        )
        mixed += jnp.dot(
            text_weights.astype(jnp.bfloat16), text[1, :, cols], preferred_element_type=jnp.float32
        )
        mixed = mixed / total
        att_ref[:, cols] = jnp.where(first_head, mixed[:own_rows], mixed[own_rows:]).astype(
            jnp.bfloat16
        )

    for at, size in spans(width, TILE):
        cols = slice(at, at + size)
        out[:, cols] = jnp.dot(
            att_ref[...], out_w[:, cols], preferred_element_type=jnp.float32
        ).astype(jnp.bfloat16)
    up_copy.wait()


def attention_half(blocks, own_rows, length, mod, gains, text, in_w, out_w, up, up_low):
    width, local = mod.shape[1], in_w.shape[2]
    all_rows = sum(block.shape[0] for block in blocks)
    up_rows = up.shape[0] - up_low
    scoped = SCOPED if all_rows <= LANES else 48 << 20
    return pl.pallas_call(
        functools.partial(attention_kernel, len(blocks), own_rows, up_low),
        out_shape=[
            jax.ShapeDtypeStruct((own_rows, width), jnp.bfloat16),
            pltpu.VMEM((up_rows, up.shape[1]), jnp.bfloat16),
        ],
        in_specs=[IN_VMEM] * len(blocks) + [IN_SMEM] + [IN_VMEM] * 5 + [IN_PLACE],
        out_specs=[IN_VMEM] * 2,
        scratch_shapes=[
            pltpu.VMEM((all_rows, width), jnp.bfloat16),
            pltpu.VMEM((own_rows, local), jnp.bfloat16),
            pltpu.VMEM((all_rows, local), jnp.bfloat16),
            pltpu.VMEM((all_rows, local), jnp.bfloat16),
            pltpu.VMEM((own_rows, local), jnp.bfloat16),
            pltpu.SemaphoreType.DMA,
        ],
        compiler_params=pltpu.CompilerParams(vmem_limit_bytes=scoped),
    )(*blocks, length, mod, gains, text, in_vmem(in_w), in_vmem(out_w), in_hbm(up))


def feed_kernel(n_blocks, paired, n_up, n_down, down_low, *refs):
    blocks = refs[:n_blocks]
    mine, theirs, mod = refs[n_blocks : n_blocks + 3]
    ups = refs[n_blocks + 3 : n_blocks + 3 + n_up]
    at = n_blocks + 3 + n_up
    downs = refs[at : at + n_down]
    down_hbm = refs[at + n_down]
    out, middle, fed, hidden, down_last, sem = refs[at + n_down + 1 :]
    down_copy = pltpu.make_async_copy(
        down_hbm.at[pl.ds(down_low, down_last.shape[0])], down_last, sem
    )
    down_copy.start()

    rows, width = fed.shape
    low = 0
    for block in blocks:

        def norm_rows(at, block=block, low=low):
            here = low + at
            attention = mine[pl.ds(here, ROWS), :].astype(jnp.float32)
            if paired:
                there = (here + rows // 2) % rows
                attention += theirs[pl.ds(there, ROWS), :].astype(jnp.float32)
            values = block[pl.ds(at, ROWS), :].astype(jnp.float32) + mod[2:3, :] * attention
            middle[pl.ds(here, ROWS), :] = values
            fed[pl.ds(here, ROWS), :] = modulated(values, mod, 3, 4)

        for_rows(block.shape[0], ROWS, norm_rows)
        low += block.shape[0]

    for at, size in spans(hidden.shape[1], TILE):
        cols = slice(at, at + size)
        total, low = None, 0
        for up in ups:
            high = low + up.shape[0]
            part = jnp.dot(fed[:, low:high], up[:, cols], preferred_element_type=jnp.float32)
            total, low = part if total is None else total + part, high
        hidden[:, cols] = jax.nn.gelu(total, approximate=True).astype(jnp.bfloat16)

    down_copy.wait()
    for at, size in spans(width, TILE):
        cols = slice(at, at + size)
        total, low = None, 0
        for down in (*downs, down_last):
            high = low + down.shape[0]
            part = jnp.dot(hidden[:, low:high], down[:, cols], preferred_element_type=jnp.float32)
            total, low = part if total is None else total + part, high
        out[:, cols] = total.astype(jnp.bfloat16)


def feed_half(blocks, mine, theirs, paired, mod, ups, downs, down, down_low):
    rows, width = mine.shape
    scoped = SCOPED if rows <= LANES else 32 << 20
    return pl.pallas_call(
        functools.partial(feed_kernel, len(blocks), paired, len(ups), len(downs), down_low),
        out_shape=[
            jax.ShapeDtypeStruct((rows, width), jnp.bfloat16),
            jax.ShapeDtypeStruct((rows, width), jnp.float32),
        ],
        in_specs=[IN_VMEM] * (len(blocks) + 3 + len(ups) + len(downs)) + [IN_PLACE],
        out_specs=[IN_VMEM] * 2,
        scratch_shapes=[
            pltpu.VMEM((rows, width), jnp.bfloat16),
            pltpu.VMEM((rows, down.shape[0]), jnp.bfloat16),
            pltpu.VMEM((down.shape[0] - down_low, width), jnp.bfloat16),
            pltpu.SemaphoreType.DMA,
        ],
        compiler_params=pltpu.CompilerParams(vmem_limit_bytes=scoped),
    )(
        *blocks,
        mine,
        theirs,
        mod,
        *[in_vmem(up) for up in ups],
        *[in_vmem(down_part) for down_part in downs],
        in_hbm(down),
    )


def final_kernel(paired, middle, mine, theirs, mod, final_w, leaving_out, velocity):
    feed = mine[:ROWS, :].astype(jnp.float32)
    if paired:
        feed += theirs[...].astype(jnp.float32)
    leaving = middle[:ROWS, :] + mod[5:6, :] * feed
    leaving_out[...] = leaving.astype(jnp.bfloat16)
    velocity[...] = lax.dot_general(
        modulated(leaving, mod, 6, 7),
        final_w[...],
        (((1,), (1,)), ((), ())),
        preferred_element_type=jnp.float32,
    )


def final_step(middle, mine, theirs, paired, mod, final_w):
    width = mod.shape[1]
    return pl.pallas_call(
        functools.partial(final_kernel, paired),
        out_shape=[
            jax.ShapeDtypeStruct((ROWS, width), jnp.bfloat16),
            jax.ShapeDtypeStruct((ROWS, final_w.shape[0]), jnp.float32),
        ],
        in_specs=[IN_VMEM] * 5,
        out_specs=[IN_VMEM] * 2,
        compiler_params=pltpu.CompilerParams(vmem_limit_bytes=SCOPED),
    )(middle, mine, theirs, mod, final_w)


def flipped(value, axes, mask, count):
    return lax.ppermute(value, axes, [(source, source ^ mask) for source in range(count)])


def on_device(
    tokens,
    text_keys_values,
    text_length,
    modulation,
    input_weight,
    norm_gain,
    output_weight,
    up_weight,
    down_weight,
    final_weight,
    step_index,
    latent,
):
    n_row, n_col = lax.axis_size("row"), lax.axis_size("col")
    width = tokens.shape[3]
    tile = tokens.reshape(-1, width)
    local = input_weight.shape[2]
    mod = modulation[0]
    in_w = input_weight.transpose(1, 0, 2)
    paired = n_row == 2
    both = ("row", "col")
    count = n_row * n_col
    tile_rows = tile.shape[0]
    own_rows = n_row * tile_rows

    if paired and n_col == 4:
        near = [tile] + [flipped(tile, both, mask, count) for mask in (n_col, 2, n_col + 2)]
        in_vm, out_vm = fetch((in_w, output_weight), ((0, 0, 3), (1, 0, local)))
        near = list(lax.optimization_barrier((*near, in_vm, out_vm)))
        in_vm, out_vm = near[4:]
        near = near[:4]
        far = [flipped(part, both, 1, count) for part in near]
        blocks = near + far
    else:
        gathered = lax.all_gather(tile, ("col", "row"), axis=0, tiled=True)
        blocks = [jnp.roll(gathered, -lax.axis_index("col") * own_rows, axis=0)]
        in_vm, out_vm = fetch((in_w, output_weight), ((0, 0, 3), (1, 0, local)))
    up_low = width // 4 // LANES * LANES
    (up_first,) = fetch((up_weight,), ((0, 0, up_low),))

    text = jnp.pad(text_keys_values[0].transpose(1, 0, 2), ((0, 0), (0, -text_keys_values.shape[1] % ROWS), (0, 0)))
    gains = jnp.tile(norm_gain, (1, TILE // HD))
    mine, up_last = attention_half(
        blocks, own_rows, text_length, mod, gains, text, in_vm, out_vm, up_weight, up_low
    )
    if paired:
        theirs = flipped(mine, "row", 1, n_row)
        own_blocks = blocks[:2] if len(blocks) > 1 else [blocks[0][:own_rows]]
    else:
        mine = lax.psum(mine.astype(jnp.float32), "row")
        theirs = mine
        own_blocks = [blocks[0][:own_rows]]
    downs = fetch((down_weight,), ((0, 0, 3 * local), (0, 3 * local, local)))
    feed, middle = feed_half(
        own_blocks, mine, theirs, paired, mod, (up_first, up_last), downs, down_weight, 4 * local
    )
    if paired:
        fed_there = flipped(feed[tile_rows:], "row", 1, n_row)
    else:
        feed = lax.psum_scatter(feed.astype(jnp.float32), "row", scatter_dimension=0, tiled=True)
        fed_there = feed
        middle = lax.dynamic_slice_in_dim(
            middle, lax.axis_index("row") * tile_rows, tile_rows, 0
        )
    leaving, raw_velocity = final_step(middle, feed, fed_there, paired, mod, final_weight.T)
    raw_velocity = raw_velocity.reshape(latent.shape)
    partner = flipped(raw_velocity, "item", 1, lax.axis_size("item"))
    is_guided = lax.axis_index("item") % 2 == 0
    guided = jnp.where(is_guided, raw_velocity, partner)
    unguided = jnp.where(is_guided, partner, raw_velocity)
    velocity = unguided + GUIDANCE * (guided - unguided)
    position = step_index[0].astype(jnp.float32)
    step_size = noise_level(position + 1.0) - noise_level(position)
    return (leaving.reshape(tokens.shape), velocity, latent + step_size * velocity)


def solution(mesh):
    in_specs = (
        P("item", "row", "col", None),
        P("item", None, None, "row"),
        P("item"),
        P("item", None, None),
        P(None, None, "row"),
        P(),
        P("row", None),
        P(None, "row"),
        P("row", None),
        P(),
        P(),
        P("item", "row", "col"),
    )
    out_specs = (P("item", "row", "col", None), P("item", "row", "col"), P("item", "row", "col"))
    return jax.shard_map(
        on_device, mesh=mesh, in_specs=in_specs, out_specs=out_specs, check_vma=False
    )
```

time: 144 us -> 91.6 us (0.64)
  Pallas kernels: 0 us -> 39 us
  matrix products: 38 us -> 0 us
  waiting for transfers between devices: 35.4 us -> 3.95 us
  blocking collectives: 18.5 us -> 0 us
  between operations: 15.6 us -> 2.27 us
  starting transfers between devices: 1.59 us -> 11.4 us
  local copies, waits for them, and re-layouts: 25 us -> 33.9 us
  other arithmetic: 8.58 us -> 0.61 us
    pallas_call x0 -> x6, Pallas kernels: none -> 39 us  [the longest x3 19.5 us: fetch(): pl.pallas_call(functools.partial(fetch_kernel, parts), out_shape=[pltpu.V...]
    dot_general x15 -> x0, matrix products: 38 us -> none  [the longest x1 10.5 us: on_device(): jnp.dot(attn_input, input_weight.reshape(model_width, 3 * local_width), p...]
    psum x1 -> x0, waiting for transfers between devices: 23.2 us -> none  [on_device(): lax.psum(jnp.dot(attended, output_weight, preferred_element_type=jnp.floa...]
    all_gather x3 -> x0, blocking collectives: 18.5 us -> none  [the longest x1 6.38 us: on_device(): stripe_tokens = lax.all_gather(tokens, 'row', axis=1, tiled=True)]
    unnamed x9 -> x35, local copies, waits for them, and re-layouts: 18.6 us -> 33.7 us
    reduce_scatter x1 -> x0, waiting for transfers between devices: 10.8 us -> none  [on_device(): lax.psum_scatter(jnp.dot(hidden, down_weight, preferred_element_type=jnp....]
    ppermute x1 -> x10, starting transfers between devices: 1.51 us -> 11.4 us  [flipped(): lax.ppermute(value, axes, [(source, source ^ mask) for source in range(co...]
    reduce_sum x13 -> x0, other arithmetic: 5.67 us -> none  [the longest x3 2.2 us: layer_norm(): center = values - jnp.mean(values, axis=-1, keepdims=True)]
  transfers between devices with their start and end apart: 3 -> 10, of which waited for: 3 -> 2; matrix products, arithmetic and copies ran while one was open for 0% -> 0% of each run, Pallas kernels for 0% -> 21%
where the time goes in v1:
time: 91.6 us; the launch traced here: 91.1 us
  Pallas kernels  39 us (43%)
  local copies, waits for them, and re-layouts  33.9 us (37%)
  starting transfers between devices  11.4 us (12%)
  waiting for transfers between devices  3.95 us (4%)
  between operations  2.27 us (2%)
    unnamed x35, local copies, waits for them, and re-layouts  33.7 us
    pallas_call x3, Pallas kernels, fetch(): pl.pallas_call(functools.partial(fetch_kernel, parts), out_shape=[pltpu.V...  19.5 us
    pallas_call x1, Pallas kernels, feed_half(): pl.pallas_call(functools.partial(feed_kernel, len(blocks), paired, len(up...  12.1 us
    ppermute x10, starting transfers between devices, flipped(): lax.ppermute(value, axes, [(source, source ^ mask) for source in range(co...  11.4 us
    pallas_call x1, Pallas kernels, attention_half(): pl.pallas_call(functools.partial(attention_kernel, len(blocks), own_rows,...  6.83 us
    ppermute x10, waiting for transfers between devices, flipped(): lax.ppermute(value, axes, [(source, source ^ mask) for source in range(co...  3.95 us
  transfers between devices with their start and end apart: 10, of which 2 were waited for; matrix products, arithmetic and copies ran while one was open for 0% of the time, Pallas kernels for 21%

profile of v1, /device:TPU:0, one launch (start us, length us, event | category | flops | bytes accessed | tf_op | source)
XLA Modules:
  0.0 91.1 jit_solution(16099767068228222407)
XLA Ops:
  0.7 3.0 %collective-permute-start = (bf16[16,2432]{1,0:T(8,128)(2,1)}, bf16[16,2432]{1,0:T(8,128)(2,1)S(1)}, u32[]{:S(2)}, u32[]{:S(2)}) collective-permute-start(bf16[16,2432]{1,0:T(8,128)(2,1)} %bitcast.14), channel_id=1, source_target_pairs={{0,16},{4,20},{8,24},{12,28},{16,0},{20,4},{24,8},{28,12},{1,17},{... | collective-permute-start | bytes 233480 | tf_op jit(solution)/shard_map/ppermute | solution.py:330
  3.7 1.5 %collective-permute-start.1 = (bf16[16,2432]{1,0:T(8,128)(2,1)}, bf16[16,2432]{1,0:T(8,128)(2,1)S(1)}, u32[]{:S(2)}, u32[]{:S(2)}) collective-permute-start(bf16[16,2432]{1,0:T(8,128)(2,1)} %bitcast.15), channel_id=1, source_target_pairs={{0,8},{4,12},{8,0},{12,4},{16,24},{20,28},{24,16},{28,20},{1,9},{5... | collective-permute-start | bytes 233480 | tf_op jit(solution)/shard_map/ppermute | solution.py:330
  5.2 6.7 %shard_map.139 = (bf16[3,2432,1024]{2,1,0:T(8,128)(2,1)S(1)}, bf16[1024,2432]{1,0:T(8,128)(2,1)S(1)}) custom-call(bf16[3,2432,1024]{2,1,0:T(8,128)(2,1)} %bitcast.21, bf16[1024,2432]{1,0:T(8,128)(2,1)} %refs_1_.1), custom_call_target="tpu_custom_call" | custom-call | bytes 39845888 | tf_op jit(solution)/shard_map/pallas_call | solution.py:86
  11.9 5.3 %copy-done.4 = bf16[3,2432,1024]{2,1,0:T(8,128)(2,1)} copy-done((bf16[3,2432,1024]{2,1,0:T(8,128)(2,1)}, bf16[3,2432,1024]{2,1,0:T(8,128)(2,1)S(1)}, u32[]{:S(2)}) %copy-start.4) | copy-done | bytes 14942232
  17.2 2.2 %copy-done.6 = bf16[1024,2432]{1,0:T(8,128)(2,1)} copy-done((bf16[1024,2432]{1,0:T(8,128)(2,1)}, bf16[1024,2432]{1,0:T(8,128)(2,1)S(1)}, u32[]{:S(2)}) %copy-start.6) | copy-done | bytes 4980760
  19.5 0.5 collective-permute-start.4
  21.5 5.2 %copy-done.5 = bf16[3,2432,1024]{2,1,0:T(8,128)(2,1)S(1)} copy-done((bf16[3,2432,1024]{2,1,0:T(8,128)(2,1)S(1)}, bf16[3,2432,1024]{2,1,0:T(8,128)(2,1)}, u32[]{:S(2)}) %copy-start.5) | copy-done | bytes 14942232
  26.8 2.4 %copy-done.7 = bf16[1024,2432]{1,0:T(8,128)(2,1)S(1)} copy-done((bf16[1024,2432]{1,0:T(8,128)(2,1)S(1)}, bf16[1024,2432]{1,0:T(8,128)(2,1)}, u32[]{:S(2)}) %copy-start.7) | copy-done | bytes 4980760
  29.2 6.8 %shard_map.140 = (bf16[32,2432]{1,0:T(8,128)(2,1)S(1)}, bf16[1920,4864]{1,0:T(8,128)(2,1)S(1)}) custom-call(bf16[16,2432]{1,0:T(8,128)(2,1)S(1)} %bitcast.18, bf16[16,2432]{1,0:T(8,128)(2,1)S(1)} %collective-permute-done.refs_1_, bf16[16,2432]{1,0:T(8,128)(2,1)S(1)} %collective-permute-done.1.refs_2_, bf16[16,2432]{1,0:T(8,128)(2,1)S(1)} %collective-permute-done.2.refs_3_, ...), custom_call_target="tpu_custom_call" | custom-call | tf_op jit(solution)/shard_map/pallas_call | solution.py:202
  36.0 2.0 %collective-permute-start.7 = (bf16[32,2432]{1,0:T(8,128)(2,1)S(1)}, bf16[32,2432]{1,0:T(8,128)(2,1)S(1)}, u32[]{:S(2)}, u32[]{:S(2)}) collective-permute-start(bf16[32,2432]{1,0:T(8,128)(2,1)S(1)} %get-tuple-element.27.refs_2_), channel_id=1, source_target_pairs={{0,16},{16,0},{1,17},{17,1},{2,18},{18,2},{3,19},{19,3},{4,20},{20... | collective-permute-start | bytes 466952 | tf_op jit(solution)/shard_map/ppermute | solution.py:330
  38.0 6.1 %shard_map.141.refs_5_ = bf16[512,4864]{1,0:T(8,128)(2,1)S(1)} custom-call(bf16[2432,4864]{1,0:T(8,128)(2,1)} %refs_0_.2), custom_call_target="tpu_custom_call" | custom-call | bytes 9961472 | tf_op jit(solution)/shard_map/pallas_call | solution.py:86
  44.2 6.7 %shard_map.142 = (bf16[3072,2432]{1,0:T(8,128)(2,1)S(1)}, bf16[1024,2432]{1,0:T(8,128)(2,1)S(1)}) custom-call(bf16[4864,2432]{1,0:T(8,128)(2,1)} %refs_9_.1), custom_call_target="tpu_custom_call" | custom-call | bytes 39845888 | tf_op jit(solution)/shard_map/pallas_call | solution.py:86
  50.9 5.2 %copy-done.2 = bf16[3072,2432]{1,0:T(8,128)(2,1)} copy-done((bf16[3072,2432]{1,0:T(8,128)(2,1)}, bf16[3072,2432]{1,0:T(8,128)(2,1)S(1)}, u32[]{:S(2)}) %copy-start.2) | copy-done | bytes 14942232
  56.1 0.7 copy-done.14
  56.7 6.3 %copy-done.1 = bf16[1920,4864]{1,0:T(8,128)(2,1)S(1)} copy-done((bf16[1920,4864]{1,0:T(8,128)(2,1)S(1)}, bf16[1920,4864]{1,0:T(8,128)(2,1)}, u32[]{:S(2)}) %copy-start.1) | copy-done | bytes 18677784
  63.1 5.2 %copy-done.3 = bf16[3072,2432]{1,0:T(8,128)(2,1)S(1)} copy-done((bf16[3072,2432]{1,0:T(8,128)(2,1)S(1)}, bf16[3072,2432]{1,0:T(8,128)(2,1)}, u32[]{:S(2)}) %copy-start.3) | copy-done | bytes 14942232
  68.3 12.1 %shard_map.143 = (bf16[32,2432]{1,0:T(8,128)(2,1)S(1)}, f32[32,2432]{1,0:T(8,128)}) custom-call(bf16[16,2432]{1,0:T(8,128)(2,1)S(1)} %bitcast.19, bf16[16,2432]{1,0:T(8,128)(2,1)S(1)} %collective-permute-done.refs_1_, bf16[32,2432]{1,0:T(8,128)(2,1)} %copy-done.12, bf16[32,2432]{1,0:T(8,128)(2,1)} %copy-done.14, f32[8,2432]{1,0:T(8,128)S(1)} %bitcast.12, ...), custom_call_target="tpu_custom_call" | custom-call | tf_op jit(solution)/shard_map/pallas_call | solution.py:275
  80.4 2.0 %collective-permute-start.8 = (bf16[16,2432]{1,0:T(8,128)(2,1)S(1)}, bf16[16,2432]{1,0:T(8,128)(2,1)S(1)}, u32[]{:S(2)}, u32[]{:S(2)}) collective-permute-start(bf16[16,2432]{1,0:T(8,128)(2,1)S(1)} %slice.3), channel_id=1, source_target_pairs={{0,16},{16,0},{1,17},{17,1},{2,18},{18,2},{3,19},{19,3},{4,20},{20... | collective-permute-start | bytes 233480 | tf_op jit(solution)/shard_map/ppermute | solution.py:330
  82.4 2.8 %collective-permute-done.8.theirs = bf16[16,2432]{1,0:T(8,128)(2,1)S(1)} collective-permute-done((bf16[16,2432]{1,0:T(8,128)(2,1)S(1)}, bf16[16,2432]{1,0:T(8,128)(2,1)S(1)}, u32[]{:S(2)}, u32[]{:S(2)}) %collective-permute-start.8) | collective-permute-done | bytes 77856 | tf_op jit(solution)/shard_map/ppermute | solution.py:330
  85.2 1.0 %copy-done.11 = f32[32,2432]{1,0:T(8,128)S(1)} copy-done((f32[32,2432]{1,0:T(8,128)S(1)}, f32[32,2432]{1,0:T(8,128)}, u32[]{:S(2)}) %copy-start.11) | copy-done | bytes 311320
  86.2 0.7 shard_map.144
  86.9 1.7 %collective-permute-start.9 = (f32[1,1,1024]{2,1,0:T(1,128)S(1)}, f32[1,1,1024]{2,1,0:T(1,128)S(1)}, u32[]{:S(2)}, u32[]{:S(2)}) collective-permute-start(f32[1,1,1024]{2,1,0:T(1,128)S(1)} %reshape.36), channel_id=1, source_target_pairs={{0,1},{1,0},{2,3},{3,2},{4,5},{5,4},{6,7},{7,6},{8,9},{9,8},{10,11... | collective-permute-start | bytes 12296 | tf_op jit(solution)/shard_map/ppermute | solution.py:330
  89.4 1.1 %collective-permute-done.9 = f32[1,1,1024]{2,1,0:T(1,128)S(1)} collective-permute-done((f32[1,1,1024]{2,1,0:T(1,128)S(1)}, f32[1,1,1024]{2,1,0:T(1,128)S(1)}, u32[]{:S(2)}, u32[]{:S(2)}) %collective-permute-start.9) | collective-permute-done | bytes 4128 | tf_op jit(solution)/shard_map/ppermute | solution.py:330
  90.5 0.6 multiply_add_fusion
  (43 shorter events, 1.0 us)
Async XLA Ops:
  0.6 18.8 %copy-start.9 = (bf16[1,1,16,2432]{3,2,1,0:T(8,128)(2,1)S(1)}, bf16[1,1,16,2432]{3,2,1,0:T(8,128)(2,1)}, u32[]{:S(2)}) copy-start(bf16[1,1,16,2432]{3,2,1,0:T(8,128)(2,1)} %param.12) | copy-start | bytes 233476
  0.6 19.8 %copy-start.13 = (bf16[1,154,2,1024]{3,2,1,0:T(2,128)(2,1)S(1)}, bf16[1,154,2,1024]{3,2,1,0:T(2,128)(2,1)}, u32[]{:S(2)}) copy-start(bf16[1,154,2,1024]{3,2,1,0:T(2,128)(2,1)} %param.13) | copy-start | bytes 1892356
  0.7 20.0 %copy-start.16 = (f32[2,64]{1,0:T(2,128)S(1)}, f32[2,64]{1,0:T(2,128)}, u32[]{:S(2)}) copy-start(f32[2,64]{1,0:T(2,128)} %param.17) | copy-start | bytes 1540
  0.7 20.8 %copy-start.8 = (f32[1,8,2432]{2,1,0:T(8,128)S(1)}, f32[1,8,2432]{2,1,0:T(8,128)}, u32[]{:S(2)}) copy-start(f32[1,8,2432]{2,1,0:T(8,128)} %param.15) | copy-start | bytes 233476
  0.7 18.7 %collective-permute-start = (bf16[16,2432]{1,0:T(8,128)(2,1)}, bf16[16,2432]{1,0:T(8,128)(2,1)S(1)}, u32[]{:S(2)}, u32[]{:S(2)}) collective-permute-start(bf16[16,2432]{1,0:T(8,128)(2,1)} %bitcast.14), channel_id=1, source_target_pairs={{0,16},{4,20},{8,24},{12,28},{16,0},{20,4},{24,8},{28,12},{1,17},{... | collective-permute-start | bytes 233480 | tf_op jit(solution)/shard_map/ppermute | solution.py:330
  3.7 15.7 %collective-permute-start.1 = (bf16[16,2432]{1,0:T(8,128)(2,1)}, bf16[16,2432]{1,0:T(8,128)(2,1)S(1)}, u32[]{:S(2)}, u32[]{:S(2)}) collective-permute-start(bf16[16,2432]{1,0:T(8,128)(2,1)} %bitcast.15), channel_id=1, source_target_pairs={{0,8},{4,12},{8,0},{12,4},{16,24},{20,28},{24,16},{28,20},{1,9},{5... | collective-permute-start | bytes 233480 | tf_op jit(solution)/shard_map/ppermute | solution.py:330
  5.2 14.2 %collective-permute-start.2 = (bf16[16,2432]{1,0:T(8,128)(2,1)}, bf16[16,2432]{1,0:T(8,128)(2,1)S(1)}, u32[]{:S(2)}, u32[]{:S(2)}) collective-permute-start(bf16[16,2432]{1,0:T(8,128)(2,1)} %bitcast.16), channel_id=1, source_target_pairs={{0,24},{4,28},{8,16},{12,20},{16,8},{20,12},{24,0},{28,4},{1,25},{... | collective-permute-start | bytes 233480 | tf_op jit(solution)/shard_map/ppermute | solution.py:330
  11.9 5.3 %copy-start.4 = (bf16[3,2432,1024]{2,1,0:T(8,128)(2,1)}, bf16[3,2432,1024]{2,1,0:T(8,128)(2,1)S(1)}, u32[]{:S(2)}) copy-start(bf16[3,2432,1024]{2,1,0:T(8,128)(2,1)S(1)} %get-tuple-element.25.refs_12_) | copy-start | bytes 44826628
  19.4 2.1 %collective-permute-start.3 = (bf16[16,2432]{1,0:T(8,128)(2,1)S(1)}, bf16[16,2432]{1,0:T(8,128)(2,1)S(1)}, u32[]{:S(2)}, u32[]{:S(2)}) collective-permute-start(bf16[16,2432]{1,0:T(8,128)(2,1)S(1)} %bitcast.17), channel_id=1, source_target_pairs={{0,4},{4,0},{8,12},{12,8},{16,20},{20,16},{24,28},{28,24},{1,5},{5... | collective-permute-start | bytes 233480 | tf_op jit(solution)/shard_map/ppermute | solution.py:330
  19.5 2.0 %collective-permute-start.4 = (bf16[16,2432]{1,0:T(8,128)(2,1)S(1)}, bf16[16,2432]{1,0:T(8,128)(2,1)S(1)}, u32[]{:S(2)}, u32[]{:S(2)}) collective-permute-start(bf16[16,2432]{1,0:T(8,128)(2,1)S(1)} %collective-permute-done.refs_1_), channel_id=1, source_target_pairs={{0,4},{4,0},{8,12},{12,8},{16,20},{20,16},{24,28},{28,24},{1,5},{5... | collective-permute-start | bytes 233480 | tf_op jit(solution)/shard_map/ppermute | solution.py:330
  20.0 1.5 %collective-permute-start.5 = (bf16[16,2432]{1,0:T(8,128)(2,1)S(1)}, bf16[16,2432]{1,0:T(8,128)(2,1)S(1)}, u32[]{:S(2)}, u32[]{:S(2)}) collective-permute-start(bf16[16,2432]{1,0:T(8,128)(2,1)S(1)} %collective-permute-done.1.refs_2_), channel_id=1, source_target_pairs={{0,4},{4,0},{8,12},{12,8},{16,20},{20,16},{24,28},{28,24},{1,5},{5... | collective-permute-start | bytes 233480 | tf_op jit(solution)/shard_map/ppermute | solution.py:330
  20.1 1.4 %collective-permute-start.6 = (bf16[16,2432]{1,0:T(8,128)(2,1)S(1)}, bf16[16,2432]{1,0:T(8,128)(2,1)S(1)}, u32[]{:S(2)}, u32[]{:S(2)}) collective-permute-start(bf16[16,2432]{1,0:T(8,128)(2,1)S(1)} %collective-permute-done.2.refs_3_), channel_id=1, source_target_pairs={{0,4},{4,0},{8,12},{12,8},{16,20},{20,16},{24,28},{28,24},{1,5},{5... | collective-permute-start | bytes 233480 | tf_op jit(solution)/shard_map/ppermute | solution.py:330
  21.5 5.2 %copy-start.5 = (bf16[3,2432,1024]{2,1,0:T(8,128)(2,1)S(1)}, bf16[3,2432,1024]{2,1,0:T(8,128)(2,1)}, u32[]{:S(2)}) copy-start(bf16[3,2432,1024]{2,1,0:T(8,128)(2,1)} %copy-done.4) | copy-start | bytes 44826628
  26.8 2.4 %copy-start.7 = (bf16[1024,2432]{1,0:T(8,128)(2,1)S(1)}, bf16[1024,2432]{1,0:T(8,128)(2,1)}, u32[]{:S(2)}) copy-start(bf16[1024,2432]{1,0:T(8,128)(2,1)} %copy-done.6) | copy-start | bytes 14942212
  36.0 14.9 %copy-start = (bf16[1920,4864]{1,0:T(8,128)(2,1)}, bf16[1920,4864]{1,0:T(8,128)(2,1)S(1)}, u32[]{:S(2)}) copy-start(bf16[1920,4864]{1,0:T(8,128)(2,1)S(1)} %get-tuple-element.28.refs_6_) | copy-start | bytes 56033284
  36.0 14.9 %copy-start.12 = (bf16[32,2432]{1,0:T(8,128)(2,1)}, bf16[32,2432]{1,0:T(8,128)(2,1)S(1)}, u32[]{:S(2)}) copy-start(bf16[32,2432]{1,0:T(8,128)(2,1)S(1)} %get-tuple-element.27.refs_2_) | copy-start | bytes 466948
  36.0 20.1 %collective-permute-start.7 = (bf16[32,2432]{1,0:T(8,128)(2,1)S(1)}, bf16[32,2432]{1,0:T(8,128)(2,1)S(1)}, u32[]{:S(2)}, u32[]{:S(2)}) collective-permute-start(bf16[32,2432]{1,0:T(8,128)(2,1)S(1)} %get-tuple-element.27.refs_2_), channel_id=1, source_target_pairs={{0,16},{16,0},{1,17},{17,1},{2,18},{18,2},{3,19},{19,3},{4,20},{20... | collective-permute-start | bytes 466952 | tf_op jit(solution)/shard_map/ppermute | solution.py:330
  50.9 5.2 %copy-start.2 = (bf16[3072,2432]{1,0:T(8,128)(2,1)}, bf16[3072,2432]{1,0:T(8,128)(2,1)S(1)}, u32[]{:S(2)}) copy-start(bf16[3072,2432]{1,0:T(8,128)(2,1)S(1)} %get-tuple-element.29.refs_7_) | copy-start | bytes 44826628
  56.7 6.3 %copy-start.1 = (bf16[1920,4864]{1,0:T(8,128)(2,1)S(1)}, bf16[1920,4864]{1,0:T(8,128)(2,1)}, u32[]{:S(2)}) copy-start(bf16[1920,4864]{1,0:T(8,128)(2,1)} %copy-done) | copy-start | bytes 56033284
  63.1 5.2 %copy-start.3 = (bf16[3072,2432]{1,0:T(8,128)(2,1)S(1)}, bf16[3072,2432]{1,0:T(8,128)(2,1)}, u32[]{:S(2)}) copy-start(bf16[3072,2432]{1,0:T(8,128)(2,1)} %copy-done.2) | copy-start | bytes 44826628
  68.3 16.9 %copy-start.10 = (bf16[2432,64]{0,1:T(8,128)(2,1)S(1)}, bf16[2432,64]{0,1:T(8,128)(2,1)}, u32[]{:S(2)}) copy-start(bf16[2432,64]{0,1:T(8,128)(2,1)} %param.21) | copy-start | bytes 933892
  68.3 22.2 %copy-start.15 = (f32[1,1,1024]{2,1,0:T(1,128)S(1)}, f32[1,1,1024]{2,1,0:T(1,128)}, u32[]{:S(2)}) copy-start(f32[1,1,1024]{2,1,0:T(1,128)} %param.23) | copy-start | bytes 12292
  80.4 4.8 %collective-permute-start.8 = (bf16[16,2432]{1,0:T(8,128)(2,1)S(1)}, bf16[16,2432]{1,0:T(8,128)(2,1)S(1)}, u32[]{:S(2)}, u32[]{:S(2)}) collective-permute-start(bf16[16,2432]{1,0:T(8,128)(2,1)S(1)} %slice.3), channel_id=1, source_target_pairs={{0,16},{16,0},{1,17},{17,1},{2,18},{18,2},{3,19},{19,3},{4,20},{20... | collective-permute-start | bytes 233480 | tf_op jit(solution)/shard_map/ppermute | solution.py:330
  86.9 3.6 %collective-permute-start.9 = (f32[1,1,1024]{2,1,0:T(1,128)S(1)}, f32[1,1,1024]{2,1,0:T(1,128)S(1)}, u32[]{:S(2)}, u32[]{:S(2)}) collective-permute-start(f32[1,1,1024]{2,1,0:T(1,128)S(1)} %reshape.36), channel_id=1, source_target_pairs={{0,1},{1,0},{2,3},{3,2},{4,5},{5,4},{6,7},{7,6},{8,9},{9,8},{10,11... | collective-permute-start | bytes 12296 | tf_op jit(solution)/shard_map/ppermute | solution.py:330
  (3 other events, 3.8 us)

commit v2 on v1

--- a/solution.py
+++ b/solution.py
@@ -18,7 +18,8 @@
 LANES = 128
 TILE = 256
 ROWS = 16
-SCOPED = 12 << 20
+SCOPED = 16 << 20
+SCOPED_FETCH = 17 << 20
 
 IN_VMEM = pl.BlockSpec(memory_space=pltpu.VMEM)
 IN_SMEM = pl.BlockSpec(memory_space=pltpu.SMEM)
@@ -66,10 +67,11 @@
     return sum(a.size * a.dtype.itemsize for a in arrays)
 
 
-def fetch_kernel(parts, *refs):
-    sources = refs[: len(refs) - len(parts) - 1]
-    targets = refs[len(sources) : -1]
-    sems = refs[-1]
+def fetch_kernel(parts, n_sources, *refs):
+    sources = refs[:n_sources]
+    targets = refs[-len(parts) - 2 : -2]
+    done, sems = refs[-2:]
+    done[...] = jnp.zeros_like(done)
     copies = [
         pltpu.make_async_copy(sources[at].at[pl.ds(low, size)], target, sems.at[index])
         for index, ((at, low, size), target) in enumerate(zip(parts, targets))
@@ -80,29 +82,37 @@
         copy.wait()
 
 
-def fetch(sources, parts):
+def fetch(sources, parts, after=()):
     shapes = [(size,) + sources[at].shape[1:] for at, low, size in parts]
     moved = sum(2 * functools.reduce(lambda a, b: a * b, shape) for shape in shapes)
     return pl.pallas_call(
-        functools.partial(fetch_kernel, parts),
-        out_shape=[pltpu.VMEM(shape, jnp.bfloat16) for shape in shapes],
-        in_specs=[IN_PLACE] * len(sources),
-        out_specs=[IN_VMEM] * len(parts),
+        functools.partial(fetch_kernel, parts, len(sources)),
+        out_shape=[pltpu.VMEM(shape, jnp.bfloat16) for shape in shapes]
+        + [jax.ShapeDtypeStruct((8, LANES), jnp.float32)],
+        in_specs=[IN_PLACE] * (len(sources) + len(after)),
+        out_specs=[IN_VMEM] * (len(parts) + 1),
         scratch_shapes=[pltpu.SemaphoreType.DMA((len(parts),))],
-        compiler_params=pltpu.CompilerParams(vmem_limit_bytes=SCOPED),
+        compiler_params=pltpu.CompilerParams(vmem_limit_bytes=SCOPED_FETCH),
         cost_estimate=pl.CostEstimate(flops=0, bytes_accessed=2 * moved, transcendentals=0),
-    )(*[in_hbm(source) for source in sources])
-
-
-def attention_kernel(n_blocks, own_rows, up_low, *refs):
+    )(*[in_hbm(source) for source in sources], *after)
+
+
+def attention_kernel(n_blocks, own_rows, *refs):
     blocks = refs[:n_blocks]
-    (length, mod, gains, text, in_w, out_w, up_hbm, out, up_part) = refs[n_blocks : n_blocks + 9]
-    normed, q_ref, k_ref, v_ref, att_ref, sem = refs[n_blocks + 9 :]
-    up_copy = pltpu.make_async_copy(up_hbm.at[pl.ds(up_low, up_part.shape[0])], up_part, sem)
-    up_copy.start()
+    length, mod, gains, text, *in_ws, out_hbm, up_hbm = refs[n_blocks : n_blocks + 9]
+    out, *ups = refs[n_blocks + 10 : -8]
+    normed, q_ref, k_ref, v_ref, att_ref, out_w, out_sem, up_sems = refs[-8:]
+    out_copy = pltpu.make_async_copy(out_hbm, out_w, out_sem)
+    out_copy.start()
+    up_copies, low = [], 0
+    for at, up in enumerate(ups):
+        rows = pl.ds(low, up.shape[0])
+        up_copies.append(pltpu.make_async_copy(up_hbm.at[rows], up, up_sems.at[at]))
+        up_copies[-1].start()
+        low += up.shape[0]
 
     all_rows, width = normed.shape
-    local = in_w.shape[2]
+    local = in_ws[0].shape[1]
     low = 0
     for block in blocks:
 
@@ -116,15 +126,16 @@
     tile = min(TILE, local)
     head_of_row = lax.broadcasted_iota(jnp.int32, (tile, tile), 0) // HD
     head_of_col = lax.broadcasted_iota(jnp.int32, (tile, tile), 1) // HD
+    gain = jnp.concatenate([gains[...]] * (tile // HD), axis=1)
     same_head = (head_of_row == head_of_col).astype(jnp.bfloat16)
 
-    def head_norm(values, gain):
+    def head_norm(values, gain_row):
         squares = values * values
         high = squares.astype(jnp.bfloat16)
         rest = (squares - high.astype(jnp.float32)).astype(jnp.bfloat16)
         total = jnp.dot(high, same_head, preferred_element_type=jnp.float32)
         total += jnp.dot(rest, same_head, preferred_element_type=jnp.float32)
-        return values * lax.rsqrt(total * (1.0 / HD) + EPSILON) * gain
+        return values * lax.rsqrt(total * (1.0 / HD) + EPSILON) * gain_row
 
     for at, size in spans(local, tile):
         cols = slice(at, at + size)
@@ -132,21 +143,21 @@
         def project(first, rows, part):
             return jnp.dot(
                 normed[pl.ds(first, rows), :],
-                in_w[part, :, cols],
+                in_ws[part][:, cols],
                 preferred_element_type=jnp.float32,
             )
 
         def keys_values(first):
             rows = min(LANES, all_rows)
             k_ref[pl.ds(first, rows), cols] = head_norm(
-                project(first, rows, 1), gains[1:2, :size]
+                project(first, rows, 1), gain[1:2, :size]
             ).astype(jnp.bfloat16)
             v_ref[pl.ds(first, rows), cols] = project(first, rows, 2).astype(jnp.bfloat16)
 
         def queries(first):
             rows = min(LANES, own_rows)
             q_ref[pl.ds(first, rows), cols] = head_norm(
-                project(first, rows, 0), gains[0:1, :size]
+                project(first, rows, 0), gain[0:1, :size]
             ).astype(jnp.bfloat16)
 
         for_rows(own_rows, min(LANES, own_rows), queries)
@@ -186,53 +197,63 @@
             jnp.bfloat16
         )
 
+    out_copy.wait()
     for at, size in spans(width, TILE):
         cols = slice(at, at + size)
         out[:, cols] = jnp.dot(
             att_ref[...], out_w[:, cols], preferred_element_type=jnp.float32
         ).astype(jnp.bfloat16)
-    up_copy.wait()
-
-
-def attention_half(blocks, own_rows, length, mod, gains, text, in_w, out_w, up, up_low):
-    width, local = mod.shape[1], in_w.shape[2]
+    for copy in up_copies:
+        copy.wait()
+
+
+def attention_half(blocks, own_rows, length, mod, gains, text, in_ws, out_w, up, up_rows, after):
+    width, local = mod.shape[1], out_w.shape[0]
     all_rows = sum(block.shape[0] for block in blocks)
-    up_rows = up.shape[0] - up_low
-    scoped = SCOPED if all_rows <= LANES else 48 << 20
+    scoped = SCOPED_FETCH if all_rows <= LANES else 48 << 20
     return pl.pallas_call(
-        functools.partial(attention_kernel, len(blocks), own_rows, up_low),
+        functools.partial(attention_kernel, len(blocks), own_rows),
         out_shape=[
             jax.ShapeDtypeStruct((own_rows, width), jnp.bfloat16),
-            pltpu.VMEM((up_rows, up.shape[1]), jnp.bfloat16),
+            *[pltpu.VMEM((rows, up.shape[1]), jnp.bfloat16) for rows in up_rows],
         ],
-        in_specs=[IN_VMEM] * len(blocks) + [IN_SMEM] + [IN_VMEM] * 5 + [IN_PLACE],
-        out_specs=[IN_VMEM] * 2,
+        in_specs=[IN_VMEM] * len(blocks) + [IN_SMEM] + [IN_VMEM] * 6 + [IN_PLACE] * 3,
+        out_specs=[IN_VMEM] * (1 + len(up_rows)),
         scratch_shapes=[
             pltpu.VMEM((all_rows, width), jnp.bfloat16),
             pltpu.VMEM((own_rows, local), jnp.bfloat16),
             pltpu.VMEM((all_rows, local), jnp.bfloat16),
             pltpu.VMEM((all_rows, local), jnp.bfloat16),
             pltpu.VMEM((own_rows, local), jnp.bfloat16),
+            pltpu.VMEM((local, width), jnp.bfloat16),
             pltpu.SemaphoreType.DMA,
+            pltpu.SemaphoreType.DMA((len(up_rows),)),
         ],
         compiler_params=pltpu.CompilerParams(vmem_limit_bytes=scoped),
-    )(*blocks, length, mod, gains, text, in_vmem(in_w), in_vmem(out_w), in_hbm(up))
-
-
-def feed_kernel(n_blocks, paired, n_up, n_down, down_low, *refs):
+    )(
+        *blocks,
+        length,
+        mod,
+        gains,
+        text,
+        *[in_vmem(part) for part in in_ws],
+        in_hbm(out_w),
+        in_hbm(up),
+        after,
+    )
+
+
+def feed_kernel(n_blocks, n_ups, n_downs, paired, *refs):
     blocks = refs[:n_blocks]
     mine, theirs, mod = refs[n_blocks : n_blocks + 3]
-    ups = refs[n_blocks + 3 : n_blocks + 3 + n_up]
-    at = n_blocks + 3 + n_up
-    downs = refs[at : at + n_down]
-    down_hbm = refs[at + n_down]
-    out, middle, fed, hidden, down_last, sem = refs[at + n_down + 1 :]
-    down_copy = pltpu.make_async_copy(
-        down_hbm.at[pl.ds(down_low, down_last.shape[0])], down_last, sem
-    )
+    ups = refs[n_blocks + 3 : n_blocks + 3 + n_ups]
+    downs = refs[n_blocks + 3 + n_ups : n_blocks + 3 + n_ups + n_downs]
+    down_hbm, out, middle, fed, hidden, down_last, sem = refs[-7:]
+    rows, width = fed.shape
+    units, last = hidden.shape[1], down_last.shape[0]
+    down_copy = pltpu.make_async_copy(down_hbm.at[pl.ds(units - last, last)], down_last, sem)
     down_copy.start()
 
-    rows, width = fed.shape
     low = 0
     for block in blocks:
 
@@ -249,31 +270,30 @@
         for_rows(block.shape[0], ROWS, norm_rows)
         low += block.shape[0]
 
-    for at, size in spans(hidden.shape[1], TILE):
+    def product(left, parts, cols):
+        sums, low = 0.0, 0
+        for part in parts:
+            here = slice(low, low + part.shape[0])
+            sums += jnp.dot(left[:, here], part[:, cols], preferred_element_type=jnp.float32)
+            low = here.stop
+        return sums
+
+    for at, size in spans(units, TILE):
         cols = slice(at, at + size)
-        total, low = None, 0
-        for up in ups:
-            high = low + up.shape[0]
-            part = jnp.dot(fed[:, low:high], up[:, cols], preferred_element_type=jnp.float32)
-            total, low = part if total is None else total + part, high
-        hidden[:, cols] = jax.nn.gelu(total, approximate=True).astype(jnp.bfloat16)
+        hidden[:, cols] = jax.nn.gelu(product(fed, ups, cols), approximate=True).astype(jnp.bfloat16)
 
     down_copy.wait()
     for at, size in spans(width, TILE):
         cols = slice(at, at + size)
-        total, low = None, 0
-        for down in (*downs, down_last):
-            high = low + down.shape[0]
-            part = jnp.dot(hidden[:, low:high], down[:, cols], preferred_element_type=jnp.float32)
-            total, low = part if total is None else total + part, high
-        out[:, cols] = total.astype(jnp.bfloat16)
-
-
-def feed_half(blocks, mine, theirs, paired, mod, ups, downs, down, down_low):
+        out[:, cols] = product(hidden, (*downs, down_last), cols).astype(jnp.bfloat16)
+
+
+def feed_half(blocks, mine, theirs, paired, mod, ups, downs, down):
     rows, width = mine.shape
-    scoped = SCOPED if rows <= LANES else 32 << 20
+    units = down.shape[0]
+    last = units - sum(part.shape[0] for part in downs)
     return pl.pallas_call(
-        functools.partial(feed_kernel, len(blocks), paired, len(ups), len(downs), down_low),
+        functools.partial(feed_kernel, len(blocks), len(ups), len(downs), paired),
         out_shape=[
             jax.ShapeDtypeStruct((rows, width), jnp.bfloat16),
             jax.ShapeDtypeStruct((rows, width), jnp.float32),
@@ -282,20 +302,12 @@
         out_specs=[IN_VMEM] * 2,
         scratch_shapes=[
             pltpu.VMEM((rows, width), jnp.bfloat16),
-            pltpu.VMEM((rows, down.shape[0]), jnp.bfloat16),
-            pltpu.VMEM((down.shape[0] - down_low, width), jnp.bfloat16),
+            pltpu.VMEM((rows, units), jnp.bfloat16),
+            pltpu.VMEM((last, width), jnp.bfloat16),
             pltpu.SemaphoreType.DMA,
         ],
-        compiler_params=pltpu.CompilerParams(vmem_limit_bytes=scoped),
-    )(
-        *blocks,
-        mine,
-        theirs,
-        mod,
-        *[in_vmem(up) for up in ups],
-        *[in_vmem(down_part) for down_part in downs],
-        in_hbm(down),
-    )
+        compiler_params=pltpu.CompilerParams(vmem_limit_bytes=SCOPED),
+    )(*blocks, mine, theirs, mod, *[in_vmem(part) for part in (*ups, *downs)], in_hbm(down))
 
 
 def final_kernel(paired, middle, mine, theirs, mod, final_w, leaving_out, velocity):
@@ -349,32 +361,43 @@
     tile = tokens.reshape(-1, width)
     local = input_weight.shape[2]
     mod = modulation[0]
-    in_w = input_weight.transpose(1, 0, 2)
+    in_w = input_weight.transpose(1, 0, 2).reshape(3 * width, local)
     paired = n_row == 2
     both = ("row", "col")
     count = n_row * n_col
     tile_rows = tile.shape[0]
     own_rows = n_row * tile_rows
 
+    text = text_keys_values[0].transpose(1, 0, 2)
+    text = jnp.pad(text, ((0, 0), (0, -text.shape[1] % ROWS), (0, 0)))
+
+    thirds = [(0, part * width, width) for part in range(3)]
     if paired and n_col == 4:
         near = [tile] + [flipped(tile, both, mask, count) for mask in (n_col, 2, n_col + 2)]
-        in_vm, out_vm = fetch((in_w, output_weight), ((0, 0, 3), (1, 0, local)))
-        near = list(lax.optimization_barrier((*near, in_vm, out_vm)))
-        in_vm, out_vm = near[4:]
-        near = near[:4]
-        far = [flipped(part, both, 1, count) for part in near]
-        blocks = near + far
+        *in_ws, done = fetch((in_w,), thirds[:2], (text,))
+        *near, done = lax.optimization_barrier((*near, done))
+        blocks = near + [flipped(part, both, 1, count) for part in near]
     else:
         gathered = lax.all_gather(tile, ("col", "row"), axis=0, tiled=True)
         blocks = [jnp.roll(gathered, -lax.axis_index("col") * own_rows, axis=0)]
-        in_vm, out_vm = fetch((in_w, output_weight), ((0, 0, 3), (1, 0, local)))
-    up_low = width // 4 // LANES * LANES
-    (up_first,) = fetch((up_weight,), ((0, 0, up_low),))
-
-    text = jnp.pad(text_keys_values[0].transpose(1, 0, 2), ((0, 0), (0, -text_keys_values.shape[1] % ROWS), (0, 0)))
-    gains = jnp.tile(norm_gain, (1, TILE // HD))
-    mine, up_last = attention_half(
-        blocks, own_rows, text_length, mod, gains, text, in_vm, out_vm, up_weight, up_low
+        *in_ws, done = fetch((in_w,), thirds[:2], (text,))
+    in_last, done = fetch((in_w,), thirds[2:], (blocks[0], done))
+    in_ws.append(in_last)
+    step = 6 * LANES
+    up_parts = spans(width, step)
+    early = 2
+    mine, *ups = attention_half(
+        blocks,
+        own_rows,
+        text_length,
+        mod,
+        norm_gain,
+        text,
+        in_ws,
+        output_weight,
+        up_weight,
+        [size for low, size in up_parts[:early]],
+        done,
     )
     if paired:
         theirs = flipped(mine, "row", 1, n_row)
@@ -383,9 +406,19 @@
         mine = lax.psum(mine.astype(jnp.float32), "row")
         theirs = mine
         own_blocks = [blocks[0][:own_rows]]
-    downs = fetch((down_weight,), ((0, 0, 3 * local), (0, 3 * local, local)))
+    edge = up_parts[early][0]
+    late = [(0, edge + low, size) for low, size in spans(width - edge, 2 * LANES)]
+    late_down = [(1, part * local // 2, local // 2) for part in range(4)]
+    *rest, done = fetch((up_weight, down_weight), late + late_down, (mine,))
     feed, middle = feed_half(
-        own_blocks, mine, theirs, paired, mod, (up_first, up_last), downs, down_weight, 4 * local
+        own_blocks,
+        mine,
+        theirs,
+        paired,
+        mod,
+        ups + rest[: len(late)],
+        rest[len(late) :],
+        down_weight,
     )
     if paired:
         fed_there = flipped(feed[tile_rows:], "row", 1, n_row)

time: 91.6 us -> 55.4 us (0.60)
  local copies, waits for them, and re-layouts: 33.9 us -> 1.39 us
  Pallas kernels: 39 us -> 35.9 us
  starting transfers between devices: 11.4 us -> 9.3 us
  waiting for transfers between devices: 3.95 us -> 5.7 us
    unnamed x35 -> x11, local copies, waits for them, and re-layouts: 33.7 us -> 1.26 us
    pallas_call x5, Pallas kernels: 38.4 us -> 35.2 us  [the longest x3 13.5 us: fetch(): pl.pallas_call(functools.partial(fetch_kernel, parts, len(sources)), out_...]
    ppermute x10, starting transfers between devices: 11.4 us -> 9.3 us  [flipped(): lax.ppermute(value, axes, [(source, source ^ mask) for source in range(co...]
    ppermute x10, waiting for transfers between devices: 3.95 us -> 5.7 us  [flipped(): lax.ppermute(value, axes, [(source, source ^ mask) for source in range(co...]
  transfers between devices with their start and end apart: 10 -> 10, of which waited for: 2 -> 3; matrix products, arithmetic and copies ran while one was open for 0% -> 2% of each run, Pallas kernels for 21% -> 24%
where the time goes in v2:
time: 55.4 us; the launch traced here: 55.1 us
  Pallas kernels  35.9 us (65%)
  starting transfers between devices  9.3 us (17%)
  waiting for transfers between devices  5.7 us (10%)
  between operations  2.21 us (4%)
  local copies, waits for them, and re-layouts  1.39 us (3%)
  other arithmetic  0.61 us (1%)
    pallas_call x3, Pallas kernels, fetch(): pl.pallas_call(functools.partial(fetch_kernel, parts, len(sources)), out_...  13.5 us
    pallas_call x1, Pallas kernels, feed_half(): pl.pallas_call(functools.partial(feed_kernel, len(blocks), len(ups), len(...  13.4 us
    ppermute x10, starting transfers between devices, flipped(): lax.ppermute(value, axes, [(source, source ^ mask) for source in range(co...  9.3 us
    pallas_call x1, Pallas kernels, attention_half(): pl.pallas_call(functools.partial(attention_kernel, len(blocks), own_rows)...  8.33 us
    ppermute x10, waiting for transfers between devices, flipped(): lax.ppermute(value, axes, [(source, source ^ mask) for source in range(co...  5.7 us
    unnamed x11, local copies, waits for them, and re-layouts  1.26 us
  transfers between devices with their start and end apart: 10, of which 3 were waited for; matrix products, arithmetic and copies ran while one was open for 2% of the time, Pallas kernels for 24%

profile of v2, /device:TPU:0, one launch (start us, length us, event | category | flops | bytes accessed | tf_op | source)
XLA Modules:
  0.0 55.1 jit_solution(915771295041449714)
XLA Ops:
  0.6 3.0 %collective-permute-start = (bf16[16,2432]{1,0:T(8,128)(2,1)}, bf16[16,2432]{1,0:T(8,128)(2,1)S(1)}, u32[]{:S(2)}, u32[]{:S(2)}) collective-permute-start(bf16[16,2432]{1,0:T(8,128)(2,1)} %bitcast.13), channel_id=1, source_target_pairs={{0,16},{4,20},{8,24},{12,28},{16,0},{20,4},{24,8},{28,12},{1,17},{... | collective-permute-start | bytes 233480 | tf_op jit(solution)/shard_map/ppermute | solution.py:342
  3.6 1.5 %collective-permute-start.1 = (bf16[16,2432]{1,0:T(8,128)(2,1)}, bf16[16,2432]{1,0:T(8,128)(2,1)S(1)}, u32[]{:S(2)}, u32[]{:S(2)}) collective-permute-start(bf16[16,2432]{1,0:T(8,128)(2,1)} %bitcast.14), channel_id=1, source_target_pairs={{0,8},{4,12},{8,0},{12,4},{16,24},{20,28},{24,16},{28,20},{1,9},{5... | collective-permute-start | bytes 233480 | tf_op jit(solution)/shard_map/ppermute | solution.py:342
  5.2 0.0 collective-permute-start.2
  5.2 1.2 %copy.17 = bf16[1,154,2,1024]{3,1,2,0:T(8,128)(2,1)S(1)} copy(bf16[1,154,2,1024]{3,2,1,0:T(2,128)(2,1)} %param.13) | data formatting | bytes 1261568 | tf_op args[1]
  6.5 0.0 copy-start
  6.5 4.0 %shard_map.139 = (bf16[2432,1024]{1,0:T(8,128)(2,1)S(1)}, bf16[2432,1024]{1,0:T(8,128)(2,1)S(1)}, f32[8,128]{1,0:T(8,128)S(1)}) custom-call(bf16[7296,1024]{1,0:T(8,128)(2,1)} %bitcast.24, bf16[2,160,1024]{2,1,0:T(8,128)(2,1)S(1)} %pad.4.refs_1_.refs_11_), custom_call_target="tpu_custom_call" | custom-call | bytes 19922944 | tf_op jit(solution)/shard_map/pallas_call | solution.py:88
  10.5 0.2 collective-permute-done.2.refs_3_
  10.7 0.5 collective-permute-start.4
  11.2 0.5 collective-permute-start.6
  12.3 0.0 copy-start.1
  12.3 0.0 copy-start.3
  12.4 2.5 %shard_map.140 = (bf16[2432,1024]{1,0:T(8,128)(2,1)S(1)}, f32[8,128]{1,0:T(8,128)S(1)}) custom-call(bf16[7296,1024]{1,0:T(8,128)(2,1)} %bitcast.25, bf16[16,2432]{1,0:T(8,128)(2,1)S(1)} %bitcast.17, f32[8,128]{1,0:T(8,128)S(1)} %get-tuple-element.35.refs_2_), custom_call_target="tpu_custom_call" | custom-call | bytes 9961472 | tf_op jit(solution)/shard_map/pallas_call | solution.py:88
  14.9 8.3 %shard_map.141 = (bf16[32,2432]{1,0:T(8,128)(2,1)S(1)}, bf16[768,4864]{1,0:T(8,128)(2,1)S(1)}, bf16[768,4864]{1,0:T(8,128)(2,1)S(1)}) custom-call(bf16[16,2432]{1,0:T(8,128)(2,1)S(1)} %bitcast.18, bf16[16,2432]{1,0:T(8,128)(2,1)S(1)} %collective-permute-done.refs_1_, bf16[16,2432]{1,0:T(8,128)(2,1)S(1)} %collective-permute-done.1.refs_2_, ...), custom_call_target="tpu_custom_call" | custom-call | tf_op jit(solution)/shard_map/pallas_call | solution.py:214
  23.2 1.9 %collective-permute-start.7 = (bf16[32,2432]{1,0:T(8,128)(2,1)S(1)}, bf16[32,2432]{1,0:T(8,128)(2,1)S(1)}, u32[]{:S(2)}, u32[]{:S(2)}) collective-permute-start(bf16[32,2432]{1,0:T(8,128)(2,1)S(1)} %get-tuple-element.38.refs_2_), channel_id=1, source_target_pairs={{0,16},{16,0},{1,17},{17,1},{2,18},{18,2},{3,19},{19,3},{4,20},{20... | collective-permute-start | bytes 466952 | tf_op jit(solution)/shard_map/ppermute | solution.py:342
  25.1 7.1 %shard_map.142 = (bf16[256,4864]{1,0:T(8,128)(2,1)S(1)}, bf16[256,4864]{1,0:T(8,128)(2,1)S(1)}, bf16[256,4864]{1,0:T(8,128)(2,1)S(1)}, bf16[128,4864]{1,0:T(8,12...) custom-call(bf16[2432,4864]{1,0:T(8,128)(2,1)} %refs_0_.1, ...), custom_call_target="tpu_custom_call" | custom-call | bytes 37355520 | tf_op jit(solution)/shard_map/pallas_call | solution.py:88
  32.2 0.0 copy-start.2
  32.2 13.4 %shard_map.143 = (bf16[32,2432]{1,0:T(8,128)(2,1)S(1)}, f32[32,2432]{1,0:T(8,128)S(1)}) custom-call(bf16[16,2432]{1,0:T(8,128)(2,1)S(1)} %bitcast.19, bf16[16,2432]{1,0:T(8,128)(2,1)S(1)} %collective-permute-done.refs_1_, bf16[32,2432]{1,0:T(8,128)(2,1)S(1)} %get-tuple-element.38.refs_2_, bf16[32,2432]{1,0:T(8,128)(2,1)S(1)} %collective-permute-done.7.refs_3_, ...), custom_call_target="tpu_custom_call" | custom-call | tf_op jit(solution)/shard_map/pallas_call | solution.py:295
  45.7 0.3 collective-permute-start.8
  45.9 4.2 %collective-permute-done.8.theirs = bf16[16,2432]{1,0:T(8,128)(2,1)S(1)} collective-permute-done((bf16[16,2432]{1,0:T(8,128)(2,1)S(1)}, bf16[16,2432]{1,0:T(8,128)(2,1)S(1)}, u32[]{:S(2)}, u32[]{:S(2)}) %collective-permute-start.8) | collective-permute-done | bytes 77856 | tf_op jit(solution)/shard_map/ppermute | solution.py:342
  50.1 0.7 %shard_map.144 = (bf16[16,2432]{1,0:T(8,128)(2,1)}, f32[16,64]{1,0:T(8,128)S(1)}) custom-call(f32[32,2432]{1,0:T(8,128)S(1)} %get-tuple-element.49.middle, bf16[32,2432]{1,0:T(8,128)(2,1)S(1)} %get-tuple-element.50.mine, bf16[16,2432]{1,0:T(8,128)(2,1)S(1)} %collective-permute-done.8.theirs, f32[8,2432]{1,0:T(8,128)S(1)} %bitcast.22, ...), custom_call_target="tpu_custom_call" | custom-call | tf_op jit(solution)/shard_map/pallas_call | solution.py:329
  50.8 0.1 reshape.36
  50.9 1.6 %collective-permute-start.9 = (f32[1,1,1024]{2,1,0:T(1,128)S(1)}, f32[1,1,1024]{2,1,0:T(1,128)S(1)}, u32[]{:S(2)}, u32[]{:S(2)}) collective-permute-start(f32[1,1,1024]{2,1,0:T(1,128)S(1)} %reshape.36), channel_id=1, source_target_pairs={{0,1},{1,0},{2,3},{3,2},{4,5},{5,4},{6,7},{7,6},{8,9},{9,8},{10,11... | collective-permute-start | bytes 12296 | tf_op jit(solution)/shard_map/ppermute | solution.py:342
  53.2 1.3 %collective-permute-done.9 = f32[1,1,1024]{2,1,0:T(1,128)S(1)} collective-permute-done((f32[1,1,1024]{2,1,0:T(1,128)S(1)}, f32[1,1,1024]{2,1,0:T(1,128)S(1)}, u32[]{:S(2)}, u32[]{:S(2)}) %collective-permute-start.9) | collective-permute-done | bytes 4128 | tf_op jit(solution)/shard_map/ppermute | solution.py:342
  54.5 0.6 %multiply_add_fusion = (f32[1,1,1024]{2,1,0:T(1,128)}, f32[1,1,1024]{2,1,0:T(1,128)}) fusion(f32[1,1,1024]{2,1,0:T(1,128)S(1)} %copy-done.4, f32[]{:T(128)} %bitcast.9, f32[1,1,1024]{2,1,0:T(1,128)S(1)} %reshape.36, f32[1,1,1024]{2,1,0:T(1,128)S(1)} %collective-permute-done.9, pred[]{:T(512)S(6)} %eq.5), kind=kLoop, calls=%fused_computation.6 | loop fusion | flops 7168 | bytes 20485 | tf_op jit(solution)/shard_map/add | solution.py:440
  (17 shorter events, 0.1 us)
Async XLA Ops:
  0.6 9.8 %collective-permute-start = (bf16[16,2432]{1,0:T(8,128)(2,1)}, bf16[16,2432]{1,0:T(8,128)(2,1)S(1)}, u32[]{:S(2)}, u32[]{:S(2)}) collective-permute-start(bf16[16,2432]{1,0:T(8,128)(2,1)} %bitcast.13), channel_id=1, source_target_pairs={{0,16},{4,20},{8,24},{12,28},{16,0},{20,4},{24,8},{28,12},{1,17},{... | collective-permute-start | bytes 233480 | tf_op jit(solution)/shard_map/ppermute | solution.py:342
  3.6 6.8 %collective-permute-start.1 = (bf16[16,2432]{1,0:T(8,128)(2,1)}, bf16[16,2432]{1,0:T(8,128)(2,1)S(1)}, u32[]{:S(2)}, u32[]{:S(2)}) collective-permute-start(bf16[16,2432]{1,0:T(8,128)(2,1)} %bitcast.14), channel_id=1, source_target_pairs={{0,8},{4,12},{8,0},{12,4},{16,24},{20,28},{24,16},{28,20},{1,9},{5... | collective-permute-start | bytes 233480 | tf_op jit(solution)/shard_map/ppermute | solution.py:342
  5.2 5.5 %collective-permute-start.2 = (bf16[16,2432]{1,0:T(8,128)(2,1)}, bf16[16,2432]{1,0:T(8,128)(2,1)S(1)}, u32[]{:S(2)}, u32[]{:S(2)}) collective-permute-start(bf16[16,2432]{1,0:T(8,128)(2,1)} %bitcast.15), channel_id=1, source_target_pairs={{0,24},{4,28},{8,16},{12,20},{16,8},{20,12},{24,0},{28,4},{1,25},{... | collective-permute-start | bytes 233480 | tf_op jit(solution)/shard_map/ppermute | solution.py:342
  6.5 4.2 %copy-start = (bf16[1,1,16,2432]{3,2,1,0:T(8,128)(2,1)S(1)}, bf16[1,1,16,2432]{3,2,1,0:T(8,128)(2,1)}, u32[]{:S(2)}) copy-start(bf16[1,1,16,2432]{3,2,1,0:T(8,128)(2,1)} %param.12) | copy-start | bytes 233476
  10.7 4.2 %collective-permute-start.3 = (bf16[16,2432]{1,0:T(8,128)(2,1)S(1)}, bf16[16,2432]{1,0:T(8,128)(2,1)S(1)}, u32[]{:S(2)}, u32[]{:S(2)}) collective-permute-start(bf16[16,2432]{1,0:T(8,128)(2,1)S(1)} %bitcast.16), channel_id=1, source_target_pairs={{0,4},{4,0},{8,12},{12,8},{16,20},{20,16},{24,28},{28,24},{1,5},{5... | collective-permute-start | bytes 233480 | tf_op jit(solution)/shard_map/ppermute | solution.py:342
  10.7 4.2 %collective-permute-start.4 = (bf16[16,2432]{1,0:T(8,128)(2,1)S(1)}, bf16[16,2432]{1,0:T(8,128)(2,1)S(1)}, u32[]{:S(2)}, u32[]{:S(2)}) collective-permute-start(bf16[16,2432]{1,0:T(8,128)(2,1)S(1)} %collective-permute-done.refs_1_), channel_id=1, source_target_pairs={{0,4},{4,0},{8,12},{12,8},{16,20},{20,16},{24,28},{28,24},{1,5},{5... | collective-permute-start | bytes 233480 | tf_op jit(solution)/shard_map/ppermute | solution.py:342
  11.2 3.7 %collective-permute-start.5 = (bf16[16,2432]{1,0:T(8,128)(2,1)S(1)}, bf16[16,2432]{1,0:T(8,128)(2,1)S(1)}, u32[]{:S(2)}, u32[]{:S(2)}) collective-permute-start(bf16[16,2432]{1,0:T(8,128)(2,1)S(1)} %collective-permute-done.1.refs_2_), channel_id=1, source_target_pairs={{0,4},{4,0},{8,12},{12,8},{16,20},{20,16},{24,28},{28,24},{1,5},{5... | collective-permute-start | bytes 233480 | tf_op jit(solution)/shard_map/ppermute | solution.py:342
  11.2 3.7 %collective-permute-start.6 = (bf16[16,2432]{1,0:T(8,128)(2,1)S(1)}, bf16[16,2432]{1,0:T(8,128)(2,1)S(1)}, u32[]{:S(2)}, u32[]{:S(2)}) collective-permute-start(bf16[16,2432]{1,0:T(8,128)(2,1)S(1)} %collective-permute-done.2.refs_3_), channel_id=1, source_target_pairs={{0,4},{4,0},{8,12},{12,8},{16,20},{20,16},{24,28},{28,24},{1,5},{5... | collective-permute-start | bytes 233480 | tf_op jit(solution)/shard_map/ppermute | solution.py:342
  12.3 2.5 %copy-start.1 = (f32[1,8,2432]{2,1,0:T(8,128)S(1)}, f32[1,8,2432]{2,1,0:T(8,128)}, u32[]{:S(2)}) copy-start(f32[1,8,2432]{2,1,0:T(8,128)} %param.15) | copy-start | bytes 233476
  12.3 2.5 %copy-start.3 = (f32[2,64]{1,0:T(2,128)S(1)}, f32[2,64]{1,0:T(2,128)}, u32[]{:S(2)}) copy-start(f32[2,64]{1,0:T(2,128)} %refs_10_.1) | copy-start | bytes 1540
  23.2 9.0 %collective-permute-start.7 = (bf16[32,2432]{1,0:T(8,128)(2,1)S(1)}, bf16[32,2432]{1,0:T(8,128)(2,1)S(1)}, u32[]{:S(2)}, u32[]{:S(2)}) collective-permute-start(bf16[32,2432]{1,0:T(8,128)(2,1)S(1)} %get-tuple-element.38.refs_2_), channel_id=1, source_target_pairs={{0,16},{16,0},{1,17},{17,1},{2,18},{18,2},{3,19},{19,3},{4,20},{20... | collective-permute-start | bytes 466952 | tf_op jit(solution)/shard_map/ppermute | solution.py:342
  32.2 17.9 %copy-start.2 = (bf16[2432,64]{0,1:T(8,128)(2,1)S(1)}, bf16[2432,64]{0,1:T(8,128)(2,1)}, u32[]{:S(2)}) copy-start(bf16[2432,64]{0,1:T(8,128)(2,1)} %param.21) | copy-start | bytes 933892
  32.2 22.3 %copy-start.4 = (f32[1,1,1024]{2,1,0:T(1,128)S(1)}, f32[1,1,1024]{2,1,0:T(1,128)}, u32[]{:S(2)}) copy-start(f32[1,1,1024]{2,1,0:T(1,128)} %param.23) | copy-start | bytes 12292
  45.7 4.5 %collective-permute-start.8 = (bf16[16,2432]{1,0:T(8,128)(2,1)S(1)}, bf16[16,2432]{1,0:T(8,128)(2,1)S(1)}, u32[]{:S(2)}, u32[]{:S(2)}) collective-permute-start(bf16[16,2432]{1,0:T(8,128)(2,1)S(1)} %slice.3), channel_id=1, source_target_pairs={{0,16},{16,0},{1,17},{17,1},{2,18},{18,2},{3,19},{19,3},{4,20},{20... | collective-permute-start | bytes 233480 | tf_op jit(solution)/shard_map/ppermute | solution.py:342
  50.9 3.6 %collective-permute-start.9 = (f32[1,1,1024]{2,1,0:T(1,128)S(1)}, f32[1,1,1024]{2,1,0:T(1,128)S(1)}, u32[]{:S(2)}, u32[]{:S(2)}) collective-permute-start(f32[1,1,1024]{2,1,0:T(1,128)S(1)} %reshape.36), channel_id=1, source_target_pairs={{0,1},{1,0},{2,3},{3,2},{4,5},{5,4},{6,7},{7,6},{8,9},{9,8},{10,11... | collective-permute-start | bytes 12296 | tf_op jit(solution)/shard_map/ppermute | solution.py:342

commit v3 on v2

v3 whole, which is shorter than its diff:
```python
import functools

import jax
import jax.numpy as jnp
from jax import lax
from jax.experimental import pallas as pl
from jax.experimental.pallas import tpu as pltpu
from jax.sharding import PartitionSpec as P

HD = 64
STEPS = 28

EPSILON = 1e-06
SHIFT_FACTOR = 3.0
GUIDANCE = 4.5
MASKED = -1e30

LANES = 128
TILE = 256
ROWS = 16
SCOPED = 16 << 20
SCOPED_FETCH = 17 << 20
EARLY = 1

IN_VMEM = pl.BlockSpec(memory_space=pltpu.VMEM)
IN_PLACE = pl.BlockSpec(memory_space=pl.ANY)


def noise_level(position):
    linear = 1.0 - position / STEPS
    return SHIFT_FACTOR * linear / (1.0 + (SHIFT_FACTOR - 1.0) * linear)


def layer_norm(values):
    center = values - jnp.mean(values, axis=-1, keepdims=True)
    spread = jnp.mean(center * center, axis=-1, keepdims=True)
    return center * lax.rsqrt(spread + EPSILON)


def modulated(values, mod_ref, shift_row, scale_row):
    scale = 1.0 + mod_ref[scale_row : scale_row + 1, :]
    shift = mod_ref[shift_row : shift_row + 1, :]
    return (layer_norm(values) * scale + shift).astype(jnp.bfloat16)


def spans(width, step):
    return [(low, min(step, width - low)) for low in range(0, width, step)]


def for_rows(rows, step, body):
    if rows <= 2 * LANES:
        for low in range(0, rows, step):
            body(low)
    else:
        pl.loop(0, rows // step)(lambda at: body(pl.multiple_of(at * step, step)))


def in_hbm(array):
    return pltpu.with_memory_space_constraint(array, pltpu.HBM)


def in_vmem(array):
    return pltpu.with_memory_space_constraint(array, pltpu.VMEM)


def bytes_of(arrays):
    return sum(a.size * a.dtype.itemsize for a in arrays)


def copies_of(parts, sources, targets, sems, shares):
    share = lax.axis_index("col") % shares
    copies = []
    for index, ((at, low, rows, width), target) in enumerate(zip(parts, targets)):
        source = sources[at]
        if source.shape[1] == width:
            first = low + share * (source.shape[0] // shares)
            piece = source.at[pl.ds(pl.multiple_of(first, ROWS), rows)]
        else:
            piece = source.at[pl.ds(low, rows), pl.ds(pl.multiple_of(share * width, LANES), width)]
        copies.append(pltpu.make_async_copy(piece, target, sems.at[index]))
    return copies


def fetch_kernel(parts, shares, n_sources, n_after, *refs):
    sources, refs = refs[:n_sources], refs[n_sources + n_after :]
    targets, done, sems = refs[: len(parts)], refs[-2], refs[-1]
    copies = copies_of(parts, sources, targets, sems, shares)
    for copy in copies:
        copy.start()
    done[...] = jnp.zeros_like(done)
    for copy in copies:
        copy.wait()


def first_kernel(parts, text_hbm, source, *refs):
    *targets, split, text, text_sem, sems = refs
    text_copy = pltpu.make_async_copy(text_hbm, text, text_sem)
    text_copy.start()
    copies = copies_of(parts, (source,), targets, sems, 1)
    for copy in copies:
        copy.start()
    count = text.shape[0]
    split[...] = jnp.zeros_like(split)
    text_copy.wait()
    split[0, :count, :] = text[:, 0, :]
    split[1, :count, :] = text[:, 1, :]
    for copy in copies:
        copy.wait()


def first_step(text, source, parts):
    rows = -(-text.shape[0] // ROWS) * ROWS
    moved = sum(2 * size * width for at, low, size, width in parts)
    return pl.pallas_call(
        functools.partial(first_kernel, parts),
        out_shape=[pltpu.VMEM((size, width), jnp.bfloat16) for at, low, size, width in parts]
        + [jax.ShapeDtypeStruct((2, rows, text.shape[2]), jnp.bfloat16)],
        in_specs=[IN_PLACE] * 2,
        out_specs=[IN_VMEM] * (len(parts) + 1),
        scratch_shapes=[
            pltpu.VMEM(text.shape, jnp.bfloat16),
            pltpu.SemaphoreType.DMA,
            pltpu.SemaphoreType.DMA((len(parts),)),
        ],
        compiler_params=pltpu.CompilerParams(vmem_limit_bytes=SCOPED_FETCH),
        cost_estimate=pl.CostEstimate(flops=0, bytes_accessed=2 * moved, transcendentals=0),
    )(in_hbm(text), in_hbm(source))


def fetch(sources, parts, after=(), shares=1):
    shapes = [(rows, width) for at, low, rows, width in parts]
    moved = sum(2 * rows * width for rows, width in shapes)
    return pl.pallas_call(
        functools.partial(fetch_kernel, parts, shares, len(sources), len(after)),
        out_shape=[pltpu.VMEM(shape, jnp.bfloat16) for shape in shapes]
        + [jax.ShapeDtypeStruct((8, LANES), jnp.float32)],
        in_specs=[IN_PLACE] * (len(sources) + len(after)),
        out_specs=[IN_VMEM] * (len(parts) + 1),
        scratch_shapes=[pltpu.SemaphoreType.DMA((len(parts),))],
        compiler_params=pltpu.CompilerParams(vmem_limit_bytes=SCOPED_FETCH),
        cost_estimate=pl.CostEstimate(flops=0, bytes_accessed=2 * moved, transcendentals=0),
    )(*[in_hbm(source) for source in sources], *after)


def norm_kernel(n_blocks, *refs):
    blocks, mod, normed = refs[:n_blocks], refs[n_blocks], refs[-1]
    for at, block in enumerate(blocks):
        rows = block.shape[0]
        values = block[...].astype(jnp.float32)
        normed[at * rows : (at + 1) * rows, :] = modulated(values, mod, 0, 1)


def norm_step(blocks, mod):
    rows, width = sum(block.shape[0] for block in blocks), mod.shape[1]
    return pl.pallas_call(
        functools.partial(norm_kernel, len(blocks)),
        out_shape=jax.ShapeDtypeStruct((rows, width), jnp.bfloat16),
        in_specs=[IN_VMEM] * (len(blocks) + 1),
        out_specs=IN_VMEM,
        compiler_params=pltpu.CompilerParams(vmem_limit_bytes=SCOPED_FETCH),
        cost_estimate=pl.CostEstimate(
            flops=10 * rows * width, bytes_accessed=4 * rows * width, transcendentals=0
        ),
    )(*blocks, mod)


def attention_kernel(n_normed, n_blocks, own_rows, *refs):
    ready, refs = refs[:n_normed], refs[n_normed:]
    blocks = refs[:n_blocks]
    length, mod, gains, text, *in_ws, out_w = refs[n_blocks : n_blocks + 8]
    out, normed, q_ref, k_ref, v_ref, att_ref = refs[-6:]

    all_rows, width = normed.shape
    local = in_ws[0].shape[1]
    low = 0
    for part in ready:
        normed[low : low + part.shape[0], :] = part[...]
        low += part.shape[0]
    for block in blocks:

        def norm_rows(at, block=block, low=low):
            values = block[pl.ds(at, ROWS), :].astype(jnp.float32)
            normed[pl.ds(low + at, ROWS), :] = modulated(values, mod, 0, 1)

        for_rows(block.shape[0], ROWS, norm_rows)
        low += block.shape[0]

    tile = min(TILE, local)
    head_of_row = lax.broadcasted_iota(jnp.int32, (tile, tile), 0) // HD
    head_of_col = lax.broadcasted_iota(jnp.int32, (tile, tile), 1) // HD
    gain = jnp.concatenate([gains[...]] * (tile // HD), axis=1)
    same_head = (head_of_row == head_of_col).astype(jnp.bfloat16)

    def head_norm(values, gain_row):
        squares = values * values
        high = squares.astype(jnp.bfloat16)
        rest = (squares - high.astype(jnp.float32)).astype(jnp.bfloat16)
        total = jnp.dot(high, same_head, preferred_element_type=jnp.float32)
        total += jnp.dot(rest, same_head, preferred_element_type=jnp.float32)
        return values * lax.rsqrt(total * (1.0 / HD) + EPSILON) * gain_row

    for at, size in spans(local, tile):
        cols = slice(at, at + size)

        def project(first, rows, part):
            return jnp.dot(
                normed[pl.ds(first, rows), :],
                in_ws[part][:, cols],
                preferred_element_type=jnp.float32,
            )

        def keys_values(first):
            rows = min(LANES, all_rows)
            k_ref[pl.ds(first, rows), cols] = head_norm(
                project(first, rows, 1), gain[1:2, :size]
            ).astype(jnp.bfloat16)
            v_ref[pl.ds(first, rows), cols] = project(first, rows, 2).astype(jnp.bfloat16)

        def queries(first):
            rows = min(LANES, own_rows)
            q_ref[pl.ds(first, rows), cols] = head_norm(
                project(first, rows, 0), gain[0:1, :size]
            ).astype(jnp.bfloat16)

        for_rows(own_rows, min(LANES, own_rows), queries)
        for_rows(all_rows, min(LANES, all_rows), keys_values)

    used = lax.broadcasted_iota(jnp.int32, (1, text.shape[1]), 1) < length[...]
    first_head = lax.broadcasted_iota(jnp.int32, (1, LANES), 1) < HD
    contract = (((1,), (1,)), ((), ()))
    for at, size in spans(local, LANES):
        cols = slice(at, at + size)
        q = q_ref[:, cols]
        zero = jnp.zeros_like(q)
        pair = jnp.concatenate([jnp.where(first_head, q, zero), jnp.where(first_head, zero, q)], 0)
        scores = HD ** (-0.5) * lax.dot_general(
            pair, k_ref[:, cols], contract, preferred_element_type=jnp.float32
        )
        text_scores = HD ** (-0.5) * lax.dot_general(
            pair, text[0, :, cols], contract, preferred_element_type=jnp.float32
        )
        text_scores = jnp.where(used, text_scores, MASKED)
        largest = jnp.maximum(
            jnp.max(scores, axis=-1, keepdims=True), jnp.max(text_scores, axis=-1, keepdims=True)
        )
        weights = jnp.exp(scores - largest)
        text_weights = jnp.exp(text_scores - largest)
        total = jnp.sum(weights, axis=-1, keepdims=True)
        total += jnp.sum(text_weights, axis=-1, keepdims=True)
        mixed = jnp.dot(
            weights.astype(jnp.bfloat16), v_ref[:, cols], preferred_element_type=jnp.float32
        )
        mixed += jnp.dot(
            text_weights.astype(jnp.bfloat16), text[1, :, cols], preferred_element_type=jnp.float32
        )
        mixed = mixed / total
        att_ref[:, cols] = jnp.where(first_head, mixed[:own_rows], mixed[own_rows:]).astype(
            jnp.bfloat16
        )

    for at, size in spans(width, TILE):
        cols = slice(at, at + size)
        out[:, cols] = jnp.dot(
            att_ref[...], out_w[:, cols], preferred_element_type=jnp.float32
        ).astype(jnp.bfloat16)


def attention_half(ready, blocks, own_rows, length, mod, gains, text, in_ws, out_w, after):
    width, local = mod.shape[1], out_w.shape[0]
    all_rows = sum(part.shape[0] for part in (*ready, *blocks))
    scoped = SCOPED_FETCH if all_rows <= LANES else 48 << 20
    return pl.pallas_call(
        functools.partial(attention_kernel, len(ready), len(blocks), own_rows),
        out_shape=jax.ShapeDtypeStruct((own_rows, width), jnp.bfloat16),
        in_specs=[IN_VMEM] * (len(ready) + len(blocks)) + [IN_VMEM] * 8 + [IN_PLACE],
        out_specs=IN_VMEM,
        scratch_shapes=[
            pltpu.VMEM((all_rows, width), jnp.bfloat16),
            pltpu.VMEM((own_rows, local), jnp.bfloat16),
            pltpu.VMEM((all_rows, local), jnp.bfloat16),
            pltpu.VMEM((all_rows, local), jnp.bfloat16),
            pltpu.VMEM((own_rows, local), jnp.bfloat16),
        ],
        compiler_params=pltpu.CompilerParams(vmem_limit_bytes=scoped),
    )(
        *ready,
        *blocks,
        length,
        mod,
        gains,
        text,
        *[in_vmem(part) for part in in_ws],
        in_vmem(out_w),
        after,
    )


def middle_kernel(n_blocks, paired, *refs):
    blocks = refs[:n_blocks]
    mine, theirs, mod, after, fed, middle = refs[n_blocks:]
    rows = fed.shape[0]
    tile = rows // n_blocks
    step = tile if tile <= LANES else ROWS
    for at, block in enumerate(blocks):

        def norm_rows(low, at=at, block=block):
            here = pl.ds(at * tile + low, step)
            attention = mine[here, :].astype(jnp.float32)
            if paired:
                there = pl.ds((at * tile + low + rows // 2) % rows, step)
                attention += theirs[there, :].astype(jnp.float32)
            values = block[pl.ds(low, step), :].astype(jnp.float32) + mod[2:3, :] * attention
            middle[here, :] = values
            fed[here, :] = modulated(values, mod, 3, 4)

        for_rows(tile, step, norm_rows)


def middle_step(blocks, mine, theirs, paired, mod, after):
    rows, width = mine.shape
    return pl.pallas_call(
        functools.partial(middle_kernel, len(blocks), paired),
        out_shape=[
            jax.ShapeDtypeStruct((rows, width), jnp.bfloat16),
            jax.ShapeDtypeStruct((rows, width), jnp.float32),
        ],
        in_specs=[IN_VMEM] * (len(blocks) + 3) + [IN_PLACE],
        out_specs=[IN_VMEM] * 2,
        compiler_params=pltpu.CompilerParams(vmem_limit_bytes=SCOPED),
    )(*blocks, mine, theirs, mod, after)


def feed_kernel(n_fed, n_ups, n_downs, n_outs, *refs):
    feds, refs = refs[:n_fed], refs[n_fed:]
    ups, refs = refs[:n_ups], refs[n_ups:]
    downs, outs = refs[:n_downs], refs[n_downs : n_downs + n_outs]
    fed, hidden = refs[-2:]
    rows, width = fed.shape
    units = hidden.shape[1]
    for at, part in enumerate(feds):
        fed[at * part.shape[0] : (at + 1) * part.shape[0], :] = part[...]

    def product(left, parts, cols):
        sums, low = 0.0, 0
        for part in parts:
            here = slice(low, low + part.shape[0])
            sums += jnp.dot(left[:, here], part[:, cols], preferred_element_type=jnp.float32)
            low = here.stop
        return sums

    for at, size in spans(units, TILE):
        cols = slice(at, at + size)
        hidden[:, cols] = jax.nn.gelu(product(fed, ups, cols), approximate=True).astype(jnp.bfloat16)

    each = rows // n_outs
    for at, size in spans(width, TILE):
        cols = slice(at, at + size)
        sums = product(hidden, downs, cols).astype(jnp.bfloat16)
        for index, out in enumerate(outs):
            out[:, cols] = sums[index * each : (index + 1) * each]


def feed_half(feds, ups, downs, n_outs):
    rows = sum(fed.shape[0] for fed in feds)
    width, units = downs[0].shape[1], ups[0].shape[1]
    scoped = SCOPED if rows <= LANES else 32 << 20
    return pl.pallas_call(
        functools.partial(feed_kernel, len(feds), len(ups), len(downs), n_outs),
        out_shape=[jax.ShapeDtypeStruct((rows // n_outs, width), jnp.bfloat16)] * n_outs,
        in_specs=[IN_VMEM] * (len(feds) + len(ups) + len(downs)),
        out_specs=[IN_VMEM] * n_outs,
        scratch_shapes=[
            pltpu.VMEM((rows, width), jnp.bfloat16),
            pltpu.VMEM((rows, units), jnp.bfloat16),
        ],
        compiler_params=pltpu.CompilerParams(vmem_limit_bytes=scoped),
    )(*feds, *[in_vmem(part) for part in (*ups, *downs)])


def final_kernel(n_feeds, middle, *refs):
    feeds = refs[:n_feeds]
    mod, final_w, leaving_out, velocity = refs[n_feeds:]
    feed = feeds[0][...].astype(jnp.float32)
    for other in feeds[1:]:
        feed += other[...].astype(jnp.float32)
    leaving = middle[: feed.shape[0], :] + mod[5:6, :] * feed
    leaving_out[...] = leaving.astype(jnp.bfloat16)
    raw = lax.dot_general(
        modulated(leaving, mod, 6, 7),
        final_w[...],
        (((1,), (1,)), ((), ())),
        preferred_element_type=jnp.float32,
    )
    velocity[...] = jnp.concatenate([raw[at : at + 1, :] for at in range(raw.shape[0])], axis=1)


def final_step(middle, feeds, mod, final_w):
    rows, width = feeds[0].shape
    return pl.pallas_call(
        functools.partial(final_kernel, len(feeds)),
        out_shape=[
            jax.ShapeDtypeStruct((rows, width), jnp.bfloat16),
            jax.ShapeDtypeStruct((1, rows * final_w.shape[0]), jnp.float32),
        ],
        in_specs=[IN_VMEM] * (3 + len(feeds)),
        out_specs=[IN_VMEM] * 2,
        compiler_params=pltpu.CompilerParams(vmem_limit_bytes=SCOPED),
    )(middle, *feeds, mod, final_w)


def guided_kernel(raw, partner, latent, index, velocity, latent_next):
    position = index[...].astype(jnp.float32)
    step_size = noise_level(position + 1.0) - noise_level(position)
    is_guided = lax.axis_index("item") % 2 == 0
    guided = jnp.where(is_guided, raw[...], partner[...])
    unguided = jnp.where(is_guided, partner[...], raw[...])
    combined = unguided + GUIDANCE * (guided - unguided)
    velocity[...] = combined
    latent_next[...] = latent[...] + step_size * combined


def guided_step(raw, partner, latent, index):
    return pl.pallas_call(
        guided_kernel,
        out_shape=[jax.ShapeDtypeStruct(raw.shape, jnp.float32)] * 2,
        in_specs=[IN_VMEM] * 4,
        out_specs=[IN_VMEM] * 2,
        compiler_params=pltpu.CompilerParams(vmem_limit_bytes=SCOPED),
    )(raw, partner, latent, index)


def flipped(value, axes, mask, count):
    return lax.ppermute(value, axes, [(source, source ^ mask) for source in range(count)])


def on_device(
    tokens,
    text_keys_values,
    text_length,
    modulation,
    input_weight,
    norm_gain,
    output_weight,
    up_weight,
    down_weight,
    final_weight,
    step_index,
    latent,
):
    n_row, n_col = lax.axis_size("row"), lax.axis_size("col")
    width = tokens.shape[3]
    tile = tokens.reshape(-1, width)
    local = input_weight.shape[2]
    mod = modulation[0]
    in_w = input_weight.transpose(1, 0, 2).reshape(3 * width, local)
    paired = n_row == 2
    both = ("row", "col")
    count = n_row * n_col
    tile_rows = tile.shape[0]
    own_rows = n_row * tile_rows

    split = paired and n_col == 4
    shares = 2 if split else 1
    units = down_weight.shape[0] // shares
    up_parts = [(0, low, size, units) for low, size in spans(width, 3 * TILE)]
    thirds = [(0, part * width, width, local) for part in range(3)]
    step = max(LANES, units // 4 // TILE * TILE)
    down_parts = [(0, low, size, width) for low, size in spans(units, step)]
    if split:
        near = [tile] + [flipped(tile, both, mask, count) for mask in (n_col, 2, n_col + 2)]
        *in_ws, text = first_step(text_keys_values[0], in_w, thirds)
        *near, text = lax.optimization_barrier((*near, text))
        own_blocks = near[:2]
        normed = norm_step(near, mod)
        ready, far = [normed, flipped(normed, both, 1, count)], []
    else:
        gathered = lax.all_gather(tile, ("col", "row"), axis=0, tiled=True)
        far = [jnp.roll(gathered, -lax.axis_index("col") * own_rows, axis=0)]
        own_blocks = [far[0][:own_rows]]
        ready, normed = [], tile
        *in_ws, text = first_step(text_keys_values[0], in_w, thirds)
    *early, done = fetch((down_weight,), down_parts[:EARLY], (normed,), shares)
    mine = attention_half(
        ready,
        far,
        own_rows,
        text_length.reshape(1, 1),
        mod,
        norm_gain,
        text,
        in_ws,
        output_weight,
        done,
    )
    if paired:
        theirs = flipped(mine, "row", 1, n_row)
    else:
        mine = lax.psum(mine.astype(jnp.float32), "row")
        theirs = mine
    *ups, done = fetch((up_weight,), up_parts, (mine,), shares)
    fed, middle = middle_step(own_blocks, mine, theirs, paired, mod, done)
    *late, done = fetch((down_weight,), down_parts[EARLY:], (fed,), shares)
    downs = early + late
    if split:
        feds = [fed, flipped(fed, both, 1, count)]
        feed, *others = feed_half(feds, ups, downs, 4)
        feeds = [feed] + [
            flipped(part, both, mask, count) for part, mask in zip(others, (n_col, 1, n_col + 1))
        ]
    else:
        (feed,) = feed_half([fed], ups, downs, 1)
        if paired:
            feeds = [feed[:tile_rows], flipped(feed[tile_rows:], "row", 1, n_row)]
        else:
            feeds = [
                lax.psum_scatter(feed.astype(jnp.float32), "row", scatter_dimension=0, tiled=True)
            ]
            middle = lax.dynamic_slice_in_dim(
                middle, lax.axis_index("row") * tile_rows, tile_rows, 0
            )
    leaving, raw_velocity = final_step(middle, feeds, mod, final_weight.T)
    partner = flipped(raw_velocity, "item", 1, lax.axis_size("item"))
    velocity, latent_next = guided_step(
        raw_velocity, partner, latent.reshape(raw_velocity.shape), step_index.reshape(1, 1)
    )
    return (
        leaving.reshape(tokens.shape),
        velocity.reshape(latent.shape),
        latent_next.reshape(latent.shape),
    )


def solution(mesh):
    in_specs = (
        P("item", "row", "col", None),
        P("item", None, None, "row"),
        P("item"),
        P("item", None, None),
        P(None, None, "row"),
        P(),
        P("row", None),
        P(None, "row"),
        P("row", None),
        P(),
        P(),
        P("item", "row", "col"),
    )
    out_specs = (P("item", "row", "col", None), P("item", "row", "col"), P("item", "row", "col"))
    return jax.shard_map(
        on_device, mesh=mesh, in_specs=in_specs, out_specs=out_specs, check_vma=False
    )
```

time: 55.4 us -> 47.5 us (0.86)
  Pallas kernels: 35.9 us -> 28.9 us
  starting transfers between devices: 9.3 us -> 10.5 us
  local copies, waits for them, and re-layouts: 1.39 us -> 0.3 us
  other arithmetic: 0.61 us -> 0.01 us
    pallas_call x6 -> x10, Pallas kernels: 35.9 us -> 28.9 us  [the longest x3 10.7 us: fetch(): pl.pallas_call(functools.partial(fetch_kernel, parts, shares, len(sources...]
    ppermute x10, starting transfers between devices: 9.3 us -> 10.5 us  [flipped(): lax.ppermute(value, axes, [(source, source ^ mask) for source in range(co...]
    unnamed x11 -> x14, local copies, waits for them, and re-layouts: 1.26 us -> 0.3 us
    add x1 -> x0, other arithmetic: 0.61 us -> none  [on_device(): latent + step_size * velocity]
  transfers between devices with their start and end apart: 10 -> 10, of which waited for: 3 -> 3; matrix products, arithmetic and copies ran while one was open for 2% -> 0% of each run, Pallas kernels for 24% -> 34%
where the time goes in v3:
time: 47.5 us; the launch traced here: 47.3 us
  Pallas kernels  28.9 us (61%)
  starting transfers between devices  10.5 us (22%)
  waiting for transfers between devices  5.32 us (11%)
  between operations  2.33 us (5%)
    pallas_call x3, Pallas kernels, fetch(): pl.pallas_call(functools.partial(fetch_kernel, parts, shares, len(sources...  10.7 us
    ppermute x10, starting transfers between devices, flipped(): lax.ppermute(value, axes, [(source, source ^ mask) for source in range(co...  10.5 us
    pallas_call x1, Pallas kernels, attention_half(): pl.pallas_call(functools.partial(attention_kernel, len(ready), len(blocks...  6.63 us
    pallas_call x1, Pallas kernels, first_step(): pl.pallas_call(functools.partial(first_kernel, parts), out_shape=[pltpu.V...  5.58 us
    ppermute x10, waiting for transfers between devices, flipped(): lax.ppermute(value, axes, [(source, source ^ mask) for source in range(co...  5.32 us
    pallas_call x1, Pallas kernels, feed_half(): pl.pallas_call(functools.partial(feed_kernel, len(feds), len(ups), len(do...  4.03 us
  transfers between devices with their start and end apart: 10, of which 3 were waited for; matrix products, arithmetic and copies ran while one was open for 0% of the time, Pallas kernels for 34%

profile of v3, /device:TPU:0, one launch (start us, length us, event | category | flops | bytes accessed | tf_op | source)
XLA Modules:
  0.0 47.3 jit_solution(11784897494635141534)
XLA Ops:
  0.6 3.0 %collective-permute-start = (bf16[16,2432]{1,0:T(8,128)(2,1)}, bf16[16,2432]{1,0:T(8,128)(2,1)S(1)}, u32[]{:S(2)}, u32[]{:S(2)}) collective-permute-start(bf16[16,2432]{1,0:T(8,128)(2,1)} %bitcast.22), channel_id=1, source_target_pairs={{0,16},{4,20},{8,24},{12,28},{16,0},{20,4},{24,8},{28,12},{1,17},{... | collective-permute-start | bytes 233480 | tf_op jit(solution)/shard_map/ppermute | solution.py:433
  3.6 1.5 %collective-permute-start.1 = (bf16[16,2432]{1,0:T(8,128)(2,1)}, bf16[16,2432]{1,0:T(8,128)(2,1)S(1)}, u32[]{:S(2)}, u32[]{:S(2)}) collective-permute-start(bf16[16,2432]{1,0:T(8,128)(2,1)} %bitcast.23), channel_id=1, source_target_pairs={{0,8},{4,12},{8,0},{12,4},{16,24},{20,28},{24,16},{28,20},{1,9},{5... | collective-permute-start | bytes 233480 | tf_op jit(solution)/shard_map/ppermute | solution.py:433
  5.2 0.0 collective-permute-start.2
  5.2 5.6 %shard_map.139 = (bf16[2432,1024]{1,0:T(8,128)(2,1)S(1)}, bf16[2432,1024]{1,0:T(8,128)(2,1)S(1)}, bf16[2432,1024]{1,0:T(8,128)(2,1)S(1)}, bf16[2,160,1024]{2,1,0:T(8,128)(2,1)S(1)}) custom-call(bf16[154,2,1024]{2,1,0:T(2,128)(2,1)} %bitcast.29, bf16[7296,1024]{1,0:T(8,128)(2,1)} %bitcast.28), custom_call_target="tpu_custom_call" | custom-call | bytes 29884416 | tf_op jit(solution)/shard_map/pallas_call | solution.py:114
  10.8 0.3 shard_map.140.refs_1_.refs_0_
  11.2 0.1 collective-permute-start.3
  12.1 1.8 %shard_map.141 = (bf16[512,2432]{1,0:T(8,128)(2,1)S(1)}, f32[8,128]{1,0:T(8,128)S(1)}) custom-call(bf16[4864,2432]{1,0:T(8,128)(2,1)} %refs_0_.5, bf16[64,2432]{1,0:T(8,128)(2,1)S(1)} %shard_map.140.refs_1_.refs_0_), custom_call_target="tpu_custom_call" | custom-call | bytes 4980736 | tf_op jit(solution)/shard_map/pallas_call | solution.py:133
  14.0 0.3 slice-done.1
  14.2 6.6 %shard_map.142.refs_1_.refs_2_ = bf16[32,2432]{1,0:T(8,128)(2,1)S(1)} custom-call(bf16[64,2432]{1,0:T(8,128)(2,1)S(1)} %shard_map.140.refs_1_.refs_0_, bf16[64,2432]{1,0:T(8,128)(2,1)S(1)} %collective-permute-done.3.refs_1_, s32[1,1]{1,0:T(1,128)} %bitcast.13.refs_2_, f32[8,2432]{1,0:T(8,128)S(1)} %bitcast.18, f32[2,64]{1,0:T(2,128)S(1)} %copy-done.4, ...), custom_call_target="tpu_custom_call" | custom-call | tf_op jit(solution)/shard_map/pallas_call | solution.py:272
  20.9 2.0 %collective-permute-start.4 = (bf16[32,2432]{1,0:T(8,128)(2,1)S(1)}, bf16[32,2432]{1,0:T(8,128)(2,1)S(1)}, u32[]{:S(2)}, u32[]{:S(2)}) collective-permute-start(bf16[32,2432]{1,0:T(8,128)(2,1)S(1)} %shard_map.142.refs_1_.refs_2_), channel_id=1, source_target_pairs={{0,16},{16,0},{1,17},{17,1},{2,18},{18,2},{3,19},{19,3},{4,20},{20... | collective-permute-start | bytes 466952 | tf_op jit(solution)/shard_map/ppermute | solution.py:433
  22.8 4.5 %shard_map.143 = (bf16[768,2432]{1,0:T(8,128)(2,1)S(1)}, bf16[768,2432]{1,0:T(8,128)(2,1)S(1)}, bf16[768,2432]{1,0:T(8,128)(2,1)S(1)}, bf16[128,2432]{1,0:T(8,128)(2,1)S(1)}, f32[8,128]{1,0:T(8,128)S(1)}) custom-call(bf16[2432,4864]{1,0:T(8,128)(2,1)} %refs_0_.4, bf16[32,2432]{1,0:T(8,128)(2,1)S(1)} %shard_map.142.refs_1_.refs_2_), custom_call_target="tpu_custom_call" | custom-call | bytes 23658496 | tf_op jit(solution)/shard_map/pallas_call | solution.py:133
  27.4 0.3 shard_map.144
  27.7 0.1 collective-permute-start.5
  27.7 4.4 %shard_map.145 = (bf16[512,2432]{1,0:T(8,128)(2,1)S(1)}, bf16[512,2432]{1,0:T(8,128)(2,1)S(1)}, bf16[512,2432]{1,0:T(8,128)(2,1)S(1)}, bf16[384,2432]{1,0:T(8,128)(2,1)S(1)}, f32[8,128]{1,0:T(8,128)}) custom-call(bf16[4864,2432]{1,0:T(8,128)(2,1)} %refs_0_.5, bf16[32,2432]{1,0:T(8,128)(2,1)S(1)} %get-tuple-element.45.refs_1_.refs_0_), custom_call_target="tpu_custom_call" | custom-call | bytes 18677760 | tf_op jit(solution)/shard_map/pallas_call | solution.py:133
  32.1 4.0 %shard_map.146 = (bf16[16,2432]{1,0:T(8,128)(2,1)S(1)}, bf16[16,2432]{1,0:T(8,128)(2,1)S(1)}, bf16[16,2432]{1,0:T(8,128)(2,1)S(1)}, bf16[16,2432]{1,0:T(8,128)(2,1)S(1)}) custom-call(bf16[32,2432]{1,0:T(8,128)(2,1)S(1)} %get-tuple-element.45.refs_1_.refs_0_, bf16[32,2432]{1,0:T(8,128)(2,1)S(1)} %collective-permute-done.5.refs_1_, ...), custom_call_target="tpu_custom_call" | custom-call | tf_op jit(solution)/shard_map/pallas_call | solution.py:367
  36.2 1.5 %collective-permute-start.6 = (bf16[16,2432]{1,0:T(8,128)(2,1)S(1)}, bf16[16,2432]{1,0:T(8,128)(2,1)S(1)}, u32[]{:S(2)}, u32[]{:S(2)}) collective-permute-start(bf16[16,2432]{1,0:T(8,128)(2,1)S(1)} %get-tuple-element.56), channel_id=1, source_target_pairs={{0,16},{4,20},{8,24},{12,28},{16,0},{20,4},{24,8},{28,12},{1,17},{... | collective-permute-start | bytes 233480 | tf_op jit(solution)/shard_map/ppermute | solution.py:433
  37.7 0.2 collective-permute-start.7
  37.9 0.5 collective-permute-start.8
  38.4 2.7 %collective-permute-done.6.refs_1_ = bf16[16,2432]{1,0:T(8,128)(2,1)S(1)} collective-permute-done((bf16[16,2432]{1,0:T(8,128)(2,1)S(1)}, bf16[16,2432]{1,0:T(8,128)(2,1)S(1)}, u32[]{:S(2)}, u32[]{:S(2)}) %collective-permute-start.6) | collective-permute-done | bytes 77856 | tf_op jit(solution)/shard_map/ppermute | solution.py:433
  41.1 1.3 %collective-permute-done.8.refs_3_ = bf16[16,2432]{1,0:T(8,128)(2,1)S(1)} collective-permute-done((bf16[16,2432]{1,0:T(8,128)(2,1)S(1)}, bf16[16,2432]{1,0:T(8,128)(2,1)S(1)}, u32[]{:S(2)}, u32[]{:S(2)}) %collective-permute-start.8) | collective-permute-done | bytes 77856 | tf_op jit(solution)/shard_map/ppermute | solution.py:433
  42.3 0.7 %shard_map.147 = (bf16[16,2432]{1,0:T(8,128)(2,1)}, f32[1,1024]{1,0:T(1,128)S(1)}) custom-call(f32[32,2432]{1,0:T(8,128)S(1)} %get-tuple-element.44.middle, bf16[16,2432]{1,0:T(8,128)(2,1)S(1)} %get-tuple-element.55.refs_0_, bf16[16,2432]{1,0:T(8,128)(2,1)S(1)} %collective-permute-done.6.refs_1_, bf16[16,2432]{1,0:T(8,128)(2,1)S(1)} %collective-permute-done.7.refs_2_, ...), custom_call_target="tpu_custom_call" | custom-call | tf_op jit(solution)/shard_map/pallas_call | solution.py:399
  43.0 1.6 %collective-permute-start.9 = (f32[1,1024]{1,0:T(1,128)S(1)}, f32[1,1024]{1,0:T(1,128)S(1)}, u32[]{:S(2)}, u32[]{:S(2)}) collective-permute-start(f32[1,1024]{1,0:T(1,128)S(1)} %get-tuple-element.60.raw), channel_id=1, source_target_pairs={{0,1},{1,0},{2,3},{3,2},{4,5},{5,4},{6,7},{7,6},{8,9},{9,8},{10,11... | collective-permute-start | bytes 12296 | tf_op jit(solution)/shard_map/ppermute | solution.py:433
  45.2 1.4 %collective-permute-done.9.partner = f32[1,1024]{1,0:T(1,128)S(1)} collective-permute-done((f32[1,1024]{1,0:T(1,128)S(1)}, f32[1,1024]{1,0:T(1,128)S(1)}, u32[]{:S(2)}, u32[]{:S(2)}) %collective-permute-start.9) | collective-permute-done | bytes 4128 | tf_op jit(solution)/shard_map/ppermute | solution.py:433
  46.6 0.7 %shard_map.148 = (f32[1,1024]{1,0:T(1,128)}, f32[1,1024]{1,0:T(1,128)}) custom-call(f32[1,1024]{1,0:T(1,128)S(1)} %get-tuple-element.60.raw, f32[1,1024]{1,0:T(1,128)S(1)} %collective-permute-done.9.partner, f32[1,1024]{1,0:T(1,128)S(1)} %bitcast.27, s32[1,1]{1,0:T(1,128)} %bitcast.14.index), custom_call_target="tpu_custom_call" | custom-call | tf_op jit(solution)/shard_map/pallas_call | solution.py:423
  (21 shorter events, 0.1 us)
Async XLA Ops:
  0.6 10.1 %collective-permute-start = (bf16[16,2432]{1,0:T(8,128)(2,1)}, bf16[16,2432]{1,0:T(8,128)(2,1)S(1)}, u32[]{:S(2)}, u32[]{:S(2)}) collective-permute-start(bf16[16,2432]{1,0:T(8,128)(2,1)} %bitcast.22), channel_id=1, source_target_pairs={{0,16},{4,20},{8,24},{12,28},{16,0},{20,4},{24,8},{28,12},{1,17},{... | collective-permute-start | bytes 233480 | tf_op jit(solution)/shard_map/ppermute | solution.py:433
  3.6 7.1 %collective-permute-start.1 = (bf16[16,2432]{1,0:T(8,128)(2,1)}, bf16[16,2432]{1,0:T(8,128)(2,1)S(1)}, u32[]{:S(2)}, u32[]{:S(2)}) collective-permute-start(bf16[16,2432]{1,0:T(8,128)(2,1)} %bitcast.23), channel_id=1, source_target_pairs={{0,8},{4,12},{8,0},{12,4},{16,24},{20,28},{24,16},{28,20},{1,9},{5... | collective-permute-start | bytes 233480 | tf_op jit(solution)/shard_map/ppermute | solution.py:433
  5.2 5.6 %collective-permute-start.2 = (bf16[16,2432]{1,0:T(8,128)(2,1)}, bf16[16,2432]{1,0:T(8,128)(2,1)S(1)}, u32[]{:S(2)}, u32[]{:S(2)}) collective-permute-start(bf16[16,2432]{1,0:T(8,128)(2,1)} %bitcast.24), channel_id=1, source_target_pairs={{0,24},{4,28},{8,16},{12,20},{16,8},{20,12},{24,0},{28,4},{1,25},{... | collective-permute-start | bytes 233480 | tf_op jit(solution)/shard_map/ppermute | solution.py:433
  5.2 5.6 %copy-start = (f32[1,8,2432]{2,1,0:T(8,128)S(1)}, f32[1,8,2432]{2,1,0:T(8,128)}, u32[]{:S(2)}) copy-start(f32[1,8,2432]{2,1,0:T(8,128)} %param.15) | copy-start | bytes 233476
  5.2 5.6 %copy-start.2 = (bf16[1,1,16,2432]{3,2,1,0:T(8,128)(2,1)S(1)}, bf16[1,1,16,2432]{3,2,1,0:T(8,128)(2,1)}, u32[]{:S(2)}) copy-start(bf16[1,1,16,2432]{3,2,1,0:T(8,128)(2,1)} %param.12) | copy-start | bytes 233476
  10.8 3.1 %slice-start = ((s8[4980736]{0:T(1024)(128)(4,1)}), s8[4194304]{0:T(1024)(128)(4,1)S(1)}, s32[]{:S(2)}) async-start(s8[4980736]{0:T(1024)(128)(4,1)} %bitcast.15), calls=%async_computation | async-start | bytes 8388608
  11.2 2.8 %collective-permute-start.3 = (bf16[64,2432]{1,0:T(8,128)(2,1)S(1)}, bf16[64,2432]{1,0:T(8,128)(2,1)S(1)}, u32[]{:S(2)}, u32[]{:S(2)}) collective-permute-start(bf16[64,2432]{1,0:T(8,128)(2,1)S(1)} %shard_map.140.refs_1_.refs_0_), channel_id=1, source_target_pairs={{0,4},{4,0},{8,12},{12,8},{16,20},{20,16},{24,28},{28,24},{1,5},{5... | collective-permute-start | bytes 933896 | tf_op jit(solution)/shard_map/ppermute | solution.py:433
  12.1 2.1 %slice-start.1 = ((s8[4980736]{0:T(1024)(128)(4,1)}), s8[786432]{0:T(1024)(128)(4,1)S(1)}, s32[]{:S(2)}) async-start(s8[4980736]{0:T(1024)(128)(4,1)} %bitcast.15), calls=%async_computation.1 | async-start | bytes 1572864
  12.1 2.1 %copy-start.4 = (f32[2,64]{1,0:T(2,128)S(1)}, f32[2,64]{1,0:T(2,128)}, u32[]{:S(2)}) copy-start(f32[2,64]{1,0:T(2,128)} %refs_4_.1) | copy-start | bytes 1540
  20.9 6.5 %collective-permute-start.4 = (bf16[32,2432]{1,0:T(8,128)(2,1)S(1)}, bf16[32,2432]{1,0:T(8,128)(2,1)S(1)}, u32[]{:S(2)}, u32[]{:S(2)}) collective-permute-start(bf16[32,2432]{1,0:T(8,128)(2,1)S(1)} %shard_map.142.refs_1_.refs_2_), channel_id=1, source_target_pairs={{0,16},{16,0},{1,17},{17,1},{2,18},{18,2},{3,19},{19,3},{4,20},{20... | collective-permute-start | bytes 466952 | tf_op jit(solution)/shard_map/ppermute | solution.py:433
  27.7 4.5 %collective-permute-start.5 = (bf16[32,2432]{1,0:T(8,128)(2,1)S(1)}, bf16[32,2432]{1,0:T(8,128)(2,1)S(1)}, u32[]{:S(2)}, u32[]{:S(2)}) collective-permute-start(bf16[32,2432]{1,0:T(8,128)(2,1)S(1)} %get-tuple-element.45.refs_1_.refs_0_), channel_id=1, source_target_pairs={{0,4},{4,0},{8,12},{12,8},{16,20},{20,16},{24,28},{28,24},{1,5},{5... | collective-permute-start | bytes 466952 | tf_op jit(solution)/shard_map/ppermute | solution.py:433
  32.1 10.2 %copy-start.1 = (bf16[2432,64]{0,1:T(8,128)(2,1)S(1)}, bf16[2432,64]{0,1:T(8,128)(2,1)}, u32[]{:S(2)}) copy-start(bf16[2432,64]{0,1:T(8,128)(2,1)} %param.21) | copy-start | bytes 933892
  32.1 14.5 %copy-start.3 = (f32[1,1,1024]{2,1,0:T(1,128)S(1)}, f32[1,1,1024]{2,1,0:T(1,128)}, u32[]{:S(2)}) copy-start(f32[1,1,1024]{2,1,0:T(1,128)} %param.23) | copy-start | bytes 12292
  36.2 4.9 %collective-permute-start.6 = (bf16[16,2432]{1,0:T(8,128)(2,1)S(1)}, bf16[16,2432]{1,0:T(8,128)(2,1)S(1)}, u32[]{:S(2)}, u32[]{:S(2)}) collective-permute-start(bf16[16,2432]{1,0:T(8,128)(2,1)S(1)} %get-tuple-element.56), channel_id=1, source_target_pairs={{0,16},{4,20},{8,24},{12,28},{16,0},{20,4},{24,8},{28,12},{1,17},{... | collective-permute-start | bytes 233480 | tf_op jit(solution)/shard_map/ppermute | solution.py:433
  37.7 3.3 %collective-permute-start.7 = (bf16[16,2432]{1,0:T(8,128)(2,1)S(1)}, bf16[16,2432]{1,0:T(8,128)(2,1)S(1)}, u32[]{:S(2)}, u32[]{:S(2)}) collective-permute-start(bf16[16,2432]{1,0:T(8,128)(2,1)S(1)} %get-tuple-element.57), channel_id=1, source_target_pairs={{0,4},{4,0},{8,12},{12,8},{16,20},{20,16},{24,28},{28,24},{1,5},{5... | collective-permute-start | bytes 233480 | tf_op jit(solution)/shard_map/ppermute | solution.py:433
  37.9 4.4 %collective-permute-start.8 = (bf16[16,2432]{1,0:T(8,128)(2,1)S(1)}, bf16[16,2432]{1,0:T(8,128)(2,1)S(1)}, u32[]{:S(2)}, u32[]{:S(2)}) collective-permute-start(bf16[16,2432]{1,0:T(8,128)(2,1)S(1)} %get-tuple-element.58), channel_id=1, source_target_pairs={{0,20},{4,16},{8,28},{12,24},{16,4},{20,0},{24,12},{28,8},{1,21},{... | collective-permute-start | bytes 233480 | tf_op jit(solution)/shard_map/ppermute | solution.py:433
  43.0 3.6 %collective-permute-start.9 = (f32[1,1024]{1,0:T(1,128)S(1)}, f32[1,1024]{1,0:T(1,128)S(1)}, u32[]{:S(2)}, u32[]{:S(2)}) collective-permute-start(f32[1,1024]{1,0:T(1,128)S(1)} %get-tuple-element.60.raw), channel_id=1, source_target_pairs={{0,1},{1,0},{2,3},{3,2},{4,5},{5,4},{6,7},{7,6},{8,9},{9,8},{10,11... | collective-permute-start | bytes 12296 | tf_op jit(solution)/shard_map/ppermute | solution.py:433

commit v4 on v3

--- a/solution.py
+++ b/solution.py
@@ -20,7 +20,6 @@
 ROWS = 16
 SCOPED = 16 << 20
 SCOPED_FETCH = 17 << 20
-EARLY = 1
 
 IN_VMEM = pl.BlockSpec(memory_space=pltpu.VMEM)
 IN_PLACE = pl.BlockSpec(memory_space=pl.ANY)
@@ -191,72 +190,84 @@
     gain = jnp.concatenate([gains[...]] * (tile // HD), axis=1)
     same_head = (head_of_row == head_of_col).astype(jnp.bfloat16)
 
-    def head_norm(values, gain_row):
-        squares = values * values
-        high = squares.astype(jnp.bfloat16)
-        rest = (squares - high.astype(jnp.float32)).astype(jnp.bfloat16)
-        total = jnp.dot(high, same_head, preferred_element_type=jnp.float32)
-        total += jnp.dot(rest, same_head, preferred_element_type=jnp.float32)
-        return values * lax.rsqrt(total * (1.0 / HD) + EPSILON) * gain_row
-
-    for at, size in spans(local, tile):
-        cols = slice(at, at + size)
-
-        def project(first, rows, part):
-            return jnp.dot(
-                normed[pl.ds(first, rows), :],
-                in_ws[part][:, cols],
-                preferred_element_type=jnp.float32,
-            )
-
-        def keys_values(first):
-            rows = min(LANES, all_rows)
-            k_ref[pl.ds(first, rows), cols] = head_norm(
-                project(first, rows, 1), gain[1:2, :size]
-            ).astype(jnp.bfloat16)
-            v_ref[pl.ds(first, rows), cols] = project(first, rows, 2).astype(jnp.bfloat16)
-
-        def queries(first):
-            rows = min(LANES, own_rows)
-            q_ref[pl.ds(first, rows), cols] = head_norm(
-                project(first, rows, 0), gain[0:1, :size]
-            ).astype(jnp.bfloat16)
-
-        for_rows(own_rows, min(LANES, own_rows), queries)
-        for_rows(all_rows, min(LANES, all_rows), keys_values)
+    def head_norm(values, gain_rows):
+        squares = (values * values).astype(jnp.bfloat16)
+        total = jnp.dot(squares, same_head, preferred_element_type=jnp.float32)
+        return (values * lax.rsqrt(total * (1.0 / HD) + EPSILON) * gain_rows).astype(jnp.bfloat16)
+
+    def project(first, rows, part, cols):
+        return jnp.dot(
+            normed[pl.ds(first, rows), :], in_ws[part][:, cols], preferred_element_type=jnp.float32
+        )
+
+    def project_rows(first, rows, part, target, columns):
+        raws = [project(first, rows, part, cols) for cols in columns]
+        normals = [head_norm(raw, gain[part : part + 1, :]) for raw in raws]
+        for cols, normal in zip(columns, normals):
+            target[pl.ds(first, rows), cols] = normal
+
+    columns = [slice(at, at + size) for at, size in spans(local, tile)]
+    own_step, all_step = min(LANES, own_rows), min(LANES, all_rows)
+
+    def keys_values(first):
+        project_rows(first, all_step, 1, k_ref, columns)
+        for cols in columns:
+            values = project(first, all_step, 2, cols)
+            v_ref[pl.ds(first, all_step), cols] = values.astype(jnp.bfloat16)
+
+    for_rows(own_rows, own_step, lambda first: project_rows(first, own_step, 0, q_ref, columns))
+    for_rows(all_rows, all_step, keys_values)
 
     used = lax.broadcasted_iota(jnp.int32, (1, text.shape[1]), 1) < length[...]
     first_head = lax.broadcasted_iota(jnp.int32, (1, LANES), 1) < HD
     contract = (((1,), (1,)), ((), ()))
-    for at, size in spans(local, LANES):
-        cols = slice(at, at + size)
-        q = q_ref[:, cols]
-        zero = jnp.zeros_like(q)
-        pair = jnp.concatenate([jnp.where(first_head, q, zero), jnp.where(first_head, zero, q)], 0)
-        scores = HD ** (-0.5) * lax.dot_general(
-            pair, k_ref[:, cols], contract, preferred_element_type=jnp.float32
-        )
-        text_scores = HD ** (-0.5) * lax.dot_general(
-            pair, text[0, :, cols], contract, preferred_element_type=jnp.float32
-        )
-        text_scores = jnp.where(used, text_scores, MASKED)
-        largest = jnp.maximum(
-            jnp.max(scores, axis=-1, keepdims=True), jnp.max(text_scores, axis=-1, keepdims=True)
-        )
-        weights = jnp.exp(scores - largest)
-        text_weights = jnp.exp(text_scores - largest)
-        total = jnp.sum(weights, axis=-1, keepdims=True)
-        total += jnp.sum(text_weights, axis=-1, keepdims=True)
-        mixed = jnp.dot(
-            weights.astype(jnp.bfloat16), v_ref[:, cols], preferred_element_type=jnp.float32
-        )
-        mixed += jnp.dot(
-            text_weights.astype(jnp.bfloat16), text[1, :, cols], preferred_element_type=jnp.float32
-        )
-        mixed = mixed / total
-        att_ref[:, cols] = jnp.where(first_head, mixed[:own_rows], mixed[own_rows:]).astype(
-            jnp.bfloat16
-        )
+    def attend(group):
+        scores = []
+        for cols in group:
+            q = q_ref[:, cols]
+            zero = jnp.zeros_like(q)
+            pair = jnp.concatenate(
+                [jnp.where(first_head, q, zero), jnp.where(first_head, zero, q)], 0
+            )
+            image = lax.dot_general(
+                pair, k_ref[:, cols], contract, preferred_element_type=jnp.float32
+            )
+            other = lax.dot_general(
+                pair, text[0, :, cols], contract, preferred_element_type=jnp.float32
+            )
+            scores.append(
+                (HD ** (-0.5) * image, jnp.where(used, HD ** (-0.5) * other, MASKED))
+            )
+        largest = [
+            jnp.maximum(
+                jnp.max(image, axis=-1, keepdims=True), jnp.max(other, axis=-1, keepdims=True)
+            )
+            for image, other in scores
+        ]
+        weights = [
+            (jnp.exp(image - top), jnp.exp(other - top))
+            for (image, other), top in zip(scores, largest)
+        ]
+        totals = [
+            jnp.sum(image, axis=-1, keepdims=True) + jnp.sum(other, axis=-1, keepdims=True)
+            for image, other in weights
+        ]
+        for cols, (image, other), total in zip(group, weights, totals):
+            mixed = jnp.dot(
+                image.astype(jnp.bfloat16), v_ref[:, cols], preferred_element_type=jnp.float32
+            )
+            mixed += jnp.dot(
+                other.astype(jnp.bfloat16), text[1, :, cols], preferred_element_type=jnp.float32
+            )
+            mixed = mixed / total
+            att_ref[:, cols] = jnp.where(first_head, mixed[:own_rows], mixed[own_rows:]).astype(
+                jnp.bfloat16
+            )
+
+    pairs = [slice(at, at + size) for at, size in spans(local, LANES)]
+    group = len(pairs) if all_rows <= LANES else 1
+    for first in range(0, len(pairs), group):
+        attend(pairs[first : first + group])
 
     for at, size in spans(width, TILE):
         cols = slice(at, at + size)
@@ -479,7 +490,6 @@
         own_blocks = [far[0][:own_rows]]
         ready, normed = [], tile
         *in_ws, text = first_step(text_keys_values[0], in_w, thirds)
-    *early, done = fetch((down_weight,), down_parts[:EARLY], (normed,), shares)
     mine = attention_half(
         ready,
         far,
@@ -490,7 +500,7 @@
         text,
         in_ws,
         output_weight,
-        done,
+        normed,
     )
     if paired:
         theirs = flipped(mine, "row", 1, n_row)
@@ -499,8 +509,7 @@
         theirs = mine
     *ups, done = fetch((up_weight,), up_parts, (mine,), shares)
     fed, middle = middle_step(own_blocks, mine, theirs, paired, mod, done)
-    *late, done = fetch((down_weight,), down_parts[EARLY:], (fed,), shares)
-    downs = early + late
+    *downs, done = fetch((down_weight,), down_parts, (fed,), shares)
     if split:
         feds = [fed, flipped(fed, both, 1, count)]
         feed, *others = feed_half(feds, ups, downs, 4)

time: 47.5 us -> 44.3 us (0.933)
  Pallas kernels: 28.9 us -> 25.4 us
  waiting for transfers between devices: 5.32 us -> 6.11 us
    pallas_call x1, Pallas kernels: 6.63 us -> 4.11 us  [attention_half(): pl.pallas_call(functools.partial(attention_kernel, len(ready), len(blocks...]
    pallas_call x3 -> x2, Pallas kernels: 10.7 us -> 9.58 us  [fetch(): pl.pallas_call(functools.partial(fetch_kernel, parts, shares, len(sources...]
    ppermute x10, waiting for transfers between devices: 5.32 us -> 6.11 us  [flipped(): lax.ppermute(value, axes, [(source, source ^ mask) for source in range(co...]
  transfers between devices with their start and end apart: 10 -> 10, of which waited for: 3 -> 4; matrix products, arithmetic and copies ran while one was open for 0% -> 0% of each run, Pallas kernels for 34% -> 35%
where the time goes in v4:
time: 44.3 us; the launch traced here: 44.2 us
  Pallas kernels  25.4 us (57%)
  starting transfers between devices  10.5 us (24%)
  waiting for transfers between devices  6.11 us (14%)
  between operations  2.1 us (5%)
    ppermute x10, starting transfers between devices, flipped(): lax.ppermute(value, axes, [(source, source ^ mask) for source in range(co...  10.5 us
    pallas_call x2, Pallas kernels, fetch(): pl.pallas_call(functools.partial(fetch_kernel, parts, shares, len(sources...  9.58 us
    ppermute x10, waiting for transfers between devices, flipped(): lax.ppermute(value, axes, [(source, source ^ mask) for source in range(co...  6.11 us
    pallas_call x1, Pallas kernels, first_step(): pl.pallas_call(functools.partial(first_kernel, parts), out_shape=[pltpu.V...  5.68 us
    pallas_call x1, Pallas kernels, attention_half(): pl.pallas_call(functools.partial(attention_kernel, len(ready), len(blocks...  4.11 us
    pallas_call x1, Pallas kernels, feed_half(): pl.pallas_call(functools.partial(feed_kernel, len(feds), len(ups), len(do...  4.06 us
  transfers between devices with their start and end apart: 10, of which 4 were waited for; matrix products, arithmetic and copies ran while one was open for 0% of the time, Pallas kernels for 35%

profile of v4, /device:TPU:0, one launch (start us, length us, event | category | flops | bytes accessed | tf_op | source)
XLA Modules:
  0.0 44.2 jit_solution(8061747957670493701)
XLA Ops:
  0.6 3.0 %collective-permute-start = (bf16[16,2432]{1,0:T(8,128)(2,1)}, bf16[16,2432]{1,0:T(8,128)(2,1)S(1)}, u32[]{:S(2)}, u32[]{:S(2)}) collective-permute-start(bf16[16,2432]{1,0:T(8,128)(2,1)} %bitcast.22), channel_id=1, source_target_pairs={{0,16},{4,20},{8,24},{12,28},{16,0},{20,4},{24,8},{28,12},{1,17},{... | collective-permute-start | bytes 233480 | tf_op jit(solution)/shard_map/ppermute | solution.py:444
  3.6 1.5 %collective-permute-start.1 = (bf16[16,2432]{1,0:T(8,128)(2,1)}, bf16[16,2432]{1,0:T(8,128)(2,1)S(1)}, u32[]{:S(2)}, u32[]{:S(2)}) collective-permute-start(bf16[16,2432]{1,0:T(8,128)(2,1)} %bitcast.23), channel_id=1, source_target_pairs={{0,8},{4,12},{8,0},{12,4},{16,24},{20,28},{24,16},{28,20},{1,9},{5... | collective-permute-start | bytes 233480 | tf_op jit(solution)/shard_map/ppermute | solution.py:444
  5.2 0.0 collective-permute-start.2
  5.2 5.7 %shard_map.139 = (bf16[2432,1024]{1,0:T(8,128)(2,1)S(1)}, bf16[2432,1024]{1,0:T(8,128)(2,1)S(1)}, bf16[2432,1024]{1,0:T(8,128)(2,1)S(1)}, bf16[2,160,1024]{2,1,0:T(8,128)(2,1)S(1)}) custom-call(bf16[154,2,1024]{2,1,0:T(2,128)(2,1)} %bitcast.29, bf16[7296,1024]{1,0:T(8,128)(2,1)} %bitcast.28), custom_call_target="tpu_custom_call" | custom-call | bytes 29884416 | tf_op jit(solution)/shard_map/pallas_call | solution.py:113
  10.9 0.3 shard_map.140.refs_0_.refs_10_
  11.3 0.1 collective-permute-start.3
  12.0 0.9 %collective-permute-done.3.refs_1_ = bf16[64,2432]{1,0:T(8,128)(2,1)S(1)} collective-permute-done((bf16[64,2432]{1,0:T(8,128)(2,1)S(1)}, bf16[64,2432]{1,0:T(8,128)(2,1)S(1)}, u32[]{:S(2)}, u32[]{:S(2)}) %collective-permute-start.3) | collective-permute-done | bytes 311328 | tf_op jit(solution)/shard_map/ppermute | solution.py:444
  13.0 4.1 %shard_map.141.refs_1_.refs_2_ = bf16[32,2432]{1,0:T(8,128)(2,1)S(1)} custom-call(bf16[64,2432]{1,0:T(8,128)(2,1)S(1)} %shard_map.140.refs_0_.refs_10_, bf16[64,2432]{1,0:T(8,128)(2,1)S(1)} %collective-permute-done.3.refs_1_, s32[1,1]{1,0:T(1,128)} %bitcast.13.refs_2_, f32[8,2432]{1,0:T(8,128)S(1)} %bitcast.18, f32[2,64]{1,0:T(2,128)S(1)} %copy-done.4, ...), custom_call_target="tpu_custom_call" | custom-call | tf_op jit(solution)/shard_map/pallas_call | solution.py:283
  17.1 2.0 %collective-permute-start.4 = (bf16[32,2432]{1,0:T(8,128)(2,1)S(1)}, bf16[32,2432]{1,0:T(8,128)(2,1)S(1)}, u32[]{:S(2)}, u32[]{:S(2)}) collective-permute-start(bf16[32,2432]{1,0:T(8,128)(2,1)S(1)} %shard_map.141.refs_1_.refs_2_), channel_id=1, source_target_pairs={{0,16},{16,0},{1,17},{17,1},{2,18},{18,2},{3,19},{19,3},{4,20},{20... | collective-permute-start | bytes 466952 | tf_op jit(solution)/shard_map/ppermute | solution.py:444
  19.0 4.5 %shard_map.142 = (bf16[768,2432]{1,0:T(8,128)(2,1)S(1)}, bf16[768,2432]{1,0:T(8,128)(2,1)S(1)}, bf16[768,2432]{1,0:T(8,128)(2,1)S(1)}, bf16[128,2432]{1,0:T(8,128)(2,1)S(1)}, f32[8,128]{1,0:T(8,128)S(1)}) custom-call(bf16[2432,4864]{1,0:T(8,128)(2,1)} %refs_0_.2, bf16[32,2432]{1,0:T(8,128)(2,1)S(1)} %shard_map.141.refs_1_.refs_2_), custom_call_target="tpu_custom_call" | custom-call | bytes 23658496 | tf_op jit(solution)/shard_map/pallas_call | solution.py:132
  23.6 0.3 shard_map.143
  23.9 0.1 collective-permute-start.5
  23.9 5.1 %shard_map.144 = (bf16[512,2432]{1,0:T(8,128)(2,1)S(1)}, bf16[512,2432]{1,0:T(8,128)(2,1)S(1)}, bf16[512,2432]{1,0:T(8,128)(2,1)S(1)}, bf16[512,2432]{1,0:T(8,12...) custom-call(bf16[4864,2432]{1,0:T(8,128)(2,1)} %refs_0_.3, ...), custom_call_target="tpu_custom_call" | custom-call | bytes 23658496 | tf_op jit(solution)/shard_map/pallas_call | solution.py:132
  29.0 0.0 copy-start.1
  29.1 4.1 %shard_map.145 = (bf16[16,2432]{1,0:T(8,128)(2,1)S(1)}, bf16[16,2432]{1,0:T(8,128)(2,1)S(1)}, bf16[16,2432]{1,0:T(8,128)(2,1)S(1)}, bf16[16,2432]{1,0:T(8,128)(2,1)S(1)}) custom-call(bf16[32,2432]{1,0:T(8,128)(2,1)S(1)} %get-tuple-element.43.refs_1_.refs_0_, bf16[32,2432]{1,0:T(8,128)(2,1)S(1)} %collective-permute-done.5.refs_1_, ...), custom_call_target="tpu_custom_call" | custom-call | tf_op jit(solution)/shard_map/pallas_call | solution.py:378
  33.1 1.6 %collective-permute-start.6 = (bf16[16,2432]{1,0:T(8,128)(2,1)S(1)}, bf16[16,2432]{1,0:T(8,128)(2,1)S(1)}, u32[]{:S(2)}, u32[]{:S(2)}) collective-permute-start(bf16[16,2432]{1,0:T(8,128)(2,1)S(1)} %get-tuple-element.54), channel_id=1, source_target_pairs={{0,16},{4,20},{8,24},{12,28},{16,0},{20,4},{24,8},{28,12},{1,17},{... | collective-permute-start | bytes 233480 | tf_op jit(solution)/shard_map/ppermute | solution.py:444
  34.7 0.2 collective-permute-start.7
  34.9 0.4 collective-permute-start.8
  35.3 2.6 %collective-permute-done.6.refs_1_ = bf16[16,2432]{1,0:T(8,128)(2,1)S(1)} collective-permute-done((bf16[16,2432]{1,0:T(8,128)(2,1)S(1)}, bf16[16,2432]{1,0:T(8,128)(2,1)S(1)}, u32[]{:S(2)}, u32[]{:S(2)}) %collective-permute-start.6) | collective-permute-done | bytes 77856 | tf_op jit(solution)/shard_map/ppermute | solution.py:444
  37.9 1.2 %collective-permute-done.8.refs_3_ = bf16[16,2432]{1,0:T(8,128)(2,1)S(1)} collective-permute-done((bf16[16,2432]{1,0:T(8,128)(2,1)S(1)}, bf16[16,2432]{1,0:T(8,128)(2,1)S(1)}, u32[]{:S(2)}, u32[]{:S(2)}) %collective-permute-start.8) | collective-permute-done | bytes 77856 | tf_op jit(solution)/shard_map/ppermute | solution.py:444
  39.2 0.7 %shard_map.146 = (bf16[16,2432]{1,0:T(8,128)(2,1)}, f32[1,1024]{1,0:T(1,128)S(1)}) custom-call(f32[32,2432]{1,0:T(8,128)S(1)} %get-tuple-element.42.middle, bf16[16,2432]{1,0:T(8,128)(2,1)S(1)} %get-tuple-element.53.refs_0_, bf16[16,2432]{1,0:T(8,128)(2,1)S(1)} %collective-permute-done.6.refs_1_, bf16[16,2432]{1,0:T(8,128)(2,1)S(1)} %collective-permute-done.7.refs_2_, ...), custom_call_target="tpu_custom_call" | custom-call | tf_op jit(solution)/shard_map/pallas_call | solution.py:410
  39.9 1.6 %collective-permute-start.9 = (f32[1,1024]{1,0:T(1,128)S(1)}, f32[1,1024]{1,0:T(1,128)S(1)}, u32[]{:S(2)}, u32[]{:S(2)}) collective-permute-start(f32[1,1024]{1,0:T(1,128)S(1)} %get-tuple-element.58.raw), channel_id=1, source_target_pairs={{0,1},{1,0},{2,3},{3,2},{4,5},{5,4},{6,7},{7,6},{8,9},{9,8},{10,11... | collective-permute-start | bytes 12296 | tf_op jit(solution)/shard_map/ppermute | solution.py:444
  42.2 1.3 %collective-permute-done.9.partner = f32[1,1024]{1,0:T(1,128)S(1)} collective-permute-done((f32[1,1024]{1,0:T(1,128)S(1)}, f32[1,1024]{1,0:T(1,128)S(1)}, u32[]{:S(2)}, u32[]{:S(2)}) %collective-permute-start.9) | collective-permute-done | bytes 4128 | tf_op jit(solution)/shard_map/ppermute | solution.py:444
  43.5 0.7 %shard_map.147 = (f32[1,1024]{1,0:T(1,128)}, f32[1,1024]{1,0:T(1,128)}) custom-call(f32[1,1024]{1,0:T(1,128)S(1)} %get-tuple-element.58.raw, f32[1,1024]{1,0:T(1,128)S(1)} %collective-permute-done.9.partner, f32[1,1024]{1,0:T(1,128)S(1)} %bitcast.27, s32[1,1]{1,0:T(1,128)} %bitcast.14.index), custom_call_target="tpu_custom_call" | custom-call | tf_op jit(solution)/shard_map/pallas_call | solution.py:434
  (20 shorter events, 0.0 us)
Async XLA Ops:
  0.6 10.3 %collective-permute-start = (bf16[16,2432]{1,0:T(8,128)(2,1)}, bf16[16,2432]{1,0:T(8,128)(2,1)S(1)}, u32[]{:S(2)}, u32[]{:S(2)}) collective-permute-start(bf16[16,2432]{1,0:T(8,128)(2,1)} %bitcast.22), channel_id=1, source_target_pairs={{0,16},{4,20},{8,24},{12,28},{16,0},{20,4},{24,8},{28,12},{1,17},{... | collective-permute-start | bytes 233480 | tf_op jit(solution)/shard_map/ppermute | solution.py:444
  3.6 7.3 %collective-permute-start.1 = (bf16[16,2432]{1,0:T(8,128)(2,1)}, bf16[16,2432]{1,0:T(8,128)(2,1)S(1)}, u32[]{:S(2)}, u32[]{:S(2)}) collective-permute-start(bf16[16,2432]{1,0:T(8,128)(2,1)} %bitcast.23), channel_id=1, source_target_pairs={{0,8},{4,12},{8,0},{12,4},{16,24},{20,28},{24,16},{28,20},{1,9},{5... | collective-permute-start | bytes 233480 | tf_op jit(solution)/shard_map/ppermute | solution.py:444
  5.2 5.8 %collective-permute-start.2 = (bf16[16,2432]{1,0:T(8,128)(2,1)}, bf16[16,2432]{1,0:T(8,128)(2,1)S(1)}, u32[]{:S(2)}, u32[]{:S(2)}) collective-permute-start(bf16[16,2432]{1,0:T(8,128)(2,1)} %bitcast.24), channel_id=1, source_target_pairs={{0,24},{4,28},{8,16},{12,20},{16,8},{20,12},{24,0},{28,4},{1,25},{... | collective-permute-start | bytes 233480 | tf_op jit(solution)/shard_map/ppermute | solution.py:444
  5.2 7.8 %slice-start = ((s8[4980736]{0:T(1024)(128)(4,1)}), s8[4194304]{0:T(1024)(128)(4,1)S(1)}, s32[]{:S(2)}) async-start(s8[4980736]{0:T(1024)(128)(4,1)} %bitcast.15), calls=%async_computation | async-start | bytes 8388608
  5.2 5.7 %copy-start = (f32[1,8,2432]{2,1,0:T(8,128)S(1)}, f32[1,8,2432]{2,1,0:T(8,128)}, u32[]{:S(2)}) copy-start(f32[1,8,2432]{2,1,0:T(8,128)} %param.15) | copy-start | bytes 233476
  5.2 5.8 %copy-start.2 = (bf16[1,1,16,2432]{3,2,1,0:T(8,128)(2,1)S(1)}, bf16[1,1,16,2432]{3,2,1,0:T(8,128)(2,1)}, u32[]{:S(2)}) copy-start(bf16[1,1,16,2432]{3,2,1,0:T(8,128)(2,1)} %param.12) | copy-start | bytes 233476
  5.2 7.8 %slice-start.1 = ((s8[4980736]{0:T(1024)(128)(4,1)}), s8[786432]{0:T(1024)(128)(4,1)S(1)}, s32[]{:S(2)}) async-start(s8[4980736]{0:T(1024)(128)(4,1)} %bitcast.15), calls=%async_computation.1 | async-start | bytes 1572864
  5.2 7.8 %copy-start.4 = (f32[2,64]{1,0:T(2,128)S(1)}, f32[2,64]{1,0:T(2,128)}, u32[]{:S(2)}) copy-start(f32[2,64]{1,0:T(2,128)} %refs_4_.1) | copy-start | bytes 1540
  11.3 1.7 %collective-permute-start.3 = (bf16[64,2432]{1,0:T(8,128)(2,1)S(1)}, bf16[64,2432]{1,0:T(8,128)(2,1)S(1)}, u32[]{:S(2)}, u32[]{:S(2)}) collective-permute-start(bf16[64,2432]{1,0:T(8,128)(2,1)S(1)} %shard_map.140.refs_0_.refs_10_), channel_id=1, source_target_pairs={{0,4},{4,0},{8,12},{12,8},{16,20},{20,16},{24,28},{28,24},{1,5},{5... | collective-permute-start | bytes 933896 | tf_op jit(solution)/shard_map/ppermute | solution.py:444
  17.1 6.5 %collective-permute-start.4 = (bf16[32,2432]{1,0:T(8,128)(2,1)S(1)}, bf16[32,2432]{1,0:T(8,128)(2,1)S(1)}, u32[]{:S(2)}, u32[]{:S(2)}) collective-permute-start(bf16[32,2432]{1,0:T(8,128)(2,1)S(1)} %shard_map.141.refs_1_.refs_2_), channel_id=1, source_target_pairs={{0,16},{16,0},{1,17},{17,1},{2,18},{18,2},{3,19},{19,3},{4,20},{20... | collective-permute-start | bytes 466952 | tf_op jit(solution)/shard_map/ppermute | solution.py:444
  23.9 5.2 %collective-permute-start.5 = (bf16[32,2432]{1,0:T(8,128)(2,1)S(1)}, bf16[32,2432]{1,0:T(8,128)(2,1)S(1)}, u32[]{:S(2)}, u32[]{:S(2)}) collective-permute-start(bf16[32,2432]{1,0:T(8,128)(2,1)S(1)} %get-tuple-element.43.refs_1_.refs_0_), channel_id=1, source_target_pairs={{0,4},{4,0},{8,12},{12,8},{16,20},{20,16},{24,28},{28,24},{1,5},{5... | collective-permute-start | bytes 466952 | tf_op jit(solution)/shard_map/ppermute | solution.py:444
  29.0 10.1 %copy-start.1 = (bf16[2432,64]{0,1:T(8,128)(2,1)S(1)}, bf16[2432,64]{0,1:T(8,128)(2,1)}, u32[]{:S(2)}) copy-start(bf16[2432,64]{0,1:T(8,128)(2,1)} %param.21) | copy-start | bytes 933892
  29.1 14.4 %copy-start.3 = (f32[1,1,1024]{2,1,0:T(1,128)S(1)}, f32[1,1,1024]{2,1,0:T(1,128)}, u32[]{:S(2)}) copy-start(f32[1,1,1024]{2,1,0:T(1,128)} %param.23) | copy-start | bytes 12292
  33.1 4.8 %collective-permute-start.6 = (bf16[16,2432]{1,0:T(8,128)(2,1)S(1)}, bf16[16,2432]{1,0:T(8,128)(2,1)S(1)}, u32[]{:S(2)}, u32[]{:S(2)}) collective-permute-start(bf16[16,2432]{1,0:T(8,128)(2,1)S(1)} %get-tuple-element.54), channel_id=1, source_target_pairs={{0,16},{4,20},{8,24},{12,28},{16,0},{20,4},{24,8},{28,12},{1,17},{... | collective-permute-start | bytes 233480 | tf_op jit(solution)/shard_map/ppermute | solution.py:444
  34.7 3.2 %collective-permute-start.7 = (bf16[16,2432]{1,0:T(8,128)(2,1)S(1)}, bf16[16,2432]{1,0:T(8,128)(2,1)S(1)}, u32[]{:S(2)}, u32[]{:S(2)}) collective-permute-start(bf16[16,2432]{1,0:T(8,128)(2,1)S(1)} %get-tuple-element.55), channel_id=1, source_target_pairs={{0,4},{4,0},{8,12},{12,8},{16,20},{20,16},{24,28},{28,24},{1,5},{5... | collective-permute-start | bytes 233480 | tf_op jit(solution)/shard_map/ppermute | solution.py:444
  34.9 4.3 %collective-permute-start.8 = (bf16[16,2432]{1,0:T(8,128)(2,1)S(1)}, bf16[16,2432]{1,0:T(8,128)(2,1)S(1)}, u32[]{:S(2)}, u32[]{:S(2)}) collective-permute-start(bf16[16,2432]{1,0:T(8,128)(2,1)S(1)} %get-tuple-element.56), channel_id=1, source_target_pairs={{0,20},{4,16},{8,28},{12,24},{16,4},{20,0},{24,12},{28,8},{1,21},{... | collective-permute-start | bytes 233480 | tf_op jit(solution)/shard_map/ppermute | solution.py:444
  39.9 3.6 %collective-permute-start.9 = (f32[1,1024]{1,0:T(1,128)S(1)}, f32[1,1024]{1,0:T(1,128)S(1)}, u32[]{:S(2)}, u32[]{:S(2)}) collective-permute-start(f32[1,1024]{1,0:T(1,128)S(1)} %get-tuple-element.58.raw), channel_id=1, source_target_pairs={{0,1},{1,0},{2,3},{3,2},{4,5},{5,4},{6,7},{7,6},{8,9},{9,8},{10,11... | collective-permute-start | bytes 12296 | tf_op jit(solution)/shard_map/ppermute | solution.py:444

commit v5 on v4

--- a/solution.py
+++ b/solution.py
@@ -190,9 +190,14 @@
     gain = jnp.concatenate([gains[...]] * (tile // HD), axis=1)
     same_head = (head_of_row == head_of_col).astype(jnp.bfloat16)
 
-    def head_norm(values, gain_rows):
-        squares = (values * values).astype(jnp.bfloat16)
-        total = jnp.dot(squares, same_head, preferred_element_type=jnp.float32)
+    def head_norm(values, part):
+        squares = values * values
+        high = squares.astype(jnp.bfloat16)
+        total = jnp.dot(high, same_head, preferred_element_type=jnp.float32)
+        if part == 0:
+            rest = (squares - high.astype(jnp.float32)).astype(jnp.bfloat16)
+            total += jnp.dot(rest, same_head, preferred_element_type=jnp.float32)
+        gain_rows = gain[part : part + 1, :]
         return (values * lax.rsqrt(total * (1.0 / HD) + EPSILON) * gain_rows).astype(jnp.bfloat16)
 
     def project(first, rows, part, cols):
@@ -202,7 +207,7 @@
 
     def project_rows(first, rows, part, target, columns):
         raws = [project(first, rows, part, cols) for cols in columns]
-        normals = [head_norm(raw, gain[part : part + 1, :]) for raw in raws]
+        normals = [head_norm(raw, part) for raw in raws]
         for cols, normal in zip(columns, normals):
             target[pl.ds(first, rows), cols] = normal
 
@@ -306,19 +311,21 @@
     )
 
 
-def middle_kernel(n_blocks, paired, *refs):
-    blocks = refs[:n_blocks]
-    mine, theirs, mod, after, fed, middle = refs[n_blocks:]
-    rows = fed.shape[0]
-    tile = rows // n_blocks
+def middle_kernel(n_blocks, n_sums, paired, *refs):
+    blocks, refs = refs[:n_blocks], refs[n_blocks:]
+    sums, (mod, after, fed, middle) = refs[: 2 * n_sums], refs[2 * n_sums :]
+    rows = sums[0].shape[0]
+    tile = rows * n_sums // n_blocks
     step = tile if tile <= LANES else ROWS
     for at, block in enumerate(blocks):
-
-        def norm_rows(low, at=at, block=block):
+        group, start = divmod(at * tile, rows)
+        mine, theirs = sums[2 * group : 2 * group + 2]
+
+        def norm_rows(low, at=at, block=block, start=start, mine=mine, theirs=theirs):
             here = pl.ds(at * tile + low, step)
-            attention = mine[here, :].astype(jnp.float32)
+            attention = mine[pl.ds(start + low, step), :].astype(jnp.float32)
             if paired:
-                there = pl.ds((at * tile + low + rows // 2) % rows, step)
+                there = pl.ds((start + low + rows // 2) % rows, step)
                 attention += theirs[there, :].astype(jnp.float32)
             values = block[pl.ds(low, step), :].astype(jnp.float32) + mod[2:3, :] * attention
             middle[here, :] = values
@@ -327,18 +334,18 @@
         for_rows(tile, step, norm_rows)
 
 
-def middle_step(blocks, mine, theirs, paired, mod, after):
-    rows, width = mine.shape
-    return pl.pallas_call(
-        functools.partial(middle_kernel, len(blocks), paired),
+def middle_step(blocks, sums, paired, mod, after):
+    rows, width = sum(block.shape[0] for block in blocks), mod.shape[1]
+    return pl.pallas_call(
+        functools.partial(middle_kernel, len(blocks), len(sums) // 2, paired),
         out_shape=[
             jax.ShapeDtypeStruct((rows, width), jnp.bfloat16),
             jax.ShapeDtypeStruct((rows, width), jnp.float32),
         ],
-        in_specs=[IN_VMEM] * (len(blocks) + 3) + [IN_PLACE],
+        in_specs=[IN_VMEM] * (len(blocks) + len(sums) + 1) + [IN_PLACE],
         out_specs=[IN_VMEM] * 2,
         compiler_params=pltpu.CompilerParams(vmem_limit_bytes=SCOPED),
-    )(*blocks, mine, theirs, mod, after)
+    )(*blocks, *sums, mod, after)
 
 
 def feed_kernel(n_fed, n_ups, n_downs, n_outs, *refs):
@@ -410,7 +417,7 @@
     return pl.pallas_call(
         functools.partial(final_kernel, len(feeds)),
         out_shape=[
-            jax.ShapeDtypeStruct((rows, width), jnp.bfloat16),
+            pltpu.VMEM((rows, width), jnp.bfloat16),
             jax.ShapeDtypeStruct((1, rows * final_w.shape[0]), jnp.float32),
         ],
         in_specs=[IN_VMEM] * (3 + len(feeds)),
@@ -502,20 +509,24 @@
         output_weight,
         normed,
     )
-    if paired:
-        theirs = flipped(mine, "row", 1, n_row)
+    if split:
+        sums = [mine] + [flipped(mine, both, mask, count) for mask in (n_col, 1, n_col + 1)]
+        own_blocks = own_blocks + [flipped(part, both, 1, count) for part in own_blocks]
+    elif paired:
+        sums = [mine, flipped(mine, "row", 1, n_row)]
     else:
         mine = lax.psum(mine.astype(jnp.float32), "row")
-        theirs = mine
-    *ups, done = fetch((up_weight,), up_parts, (mine,), shares)
-    fed, middle = middle_step(own_blocks, mine, theirs, paired, mod, done)
-    *downs, done = fetch((down_weight,), down_parts, (fed,), shares)
+        sums = [mine, mine]
+    weights = up_parts + [(1, *part[1:]) for part in down_parts]
+    *fetched, done = fetch((up_weight, down_weight), weights, (mine,), shares)
+    ups, downs = fetched[: len(up_parts)], fetched[len(up_parts) :]
+    fed, middle = middle_step(own_blocks, sums, paired, mod, done)
     if split:
-        feds = [fed, flipped(fed, both, 1, count)]
-        feed, *others = feed_half(feds, ups, downs, 4)
-        feeds = [feed] + [
-            flipped(part, both, mask, count) for part, mask in zip(others, (n_col, 1, n_col + 1))
-        ]
+        feed, *others = feed_half([fed], ups, downs, 4)
+        feeds = [feed]
+        feeds.append(flipped(others[2], both, n_col + 1, count))
+        feeds.append(flipped(others[0], both, n_col, count))
+        feeds.append(flipped(others[1], both, 1, count))
     else:
         (feed,) = feed_half([fed], ups, downs, 1)
         if paired:

time: 44.3 us -> 43.4 us (0.980)
  Pallas kernels: 25.4 us -> 23.8 us
  local copies, waits for them, and re-layouts: 0.03 us -> 0.67 us
  starting transfers between devices: 10.5 us -> 11.1 us
  waiting for transfers between devices: 6.11 us -> 5.52 us
    pallas_call x2 -> x1, Pallas kernels: 9.58 us -> 7.95 us  [fetch(): pl.pallas_call(functools.partial(fetch_kernel, parts, shares, len(sources...]
    unnamed x14 -> x15, local copies, waits for them, and re-layouts: 0.03 us -> 0.67 us
    ppermute x10 -> x13, starting transfers between devices: 10.5 us -> 11.1 us  [flipped(): lax.ppermute(value, axes, [(source, source ^ mask) for source in range(co...]
    ppermute x10 -> x13, waiting for transfers between devices: 6.11 us -> 5.52 us  [flipped(): lax.ppermute(value, axes, [(source, source ^ mask) for source in range(co...]
  transfers between devices with their start and end apart: 10 -> 13, of which waited for: 4 -> 4; matrix products, arithmetic and copies ran while one was open for 0% -> 1% of each run, Pallas kernels for 35% -> 32%
where the time goes in v5:
time: 43.4 us; the launch traced here: 43.2 us
  Pallas kernels  23.8 us (55%)
  starting transfers between devices  11.1 us (26%)
  waiting for transfers between devices  5.52 us (13%)
  between operations  2.11 us (5%)
  local copies, waits for them, and re-layouts  0.67 us (2%)
    ppermute x13, starting transfers between devices, flipped(): lax.ppermute(value, axes, [(source, source ^ mask) for source in range(co...  11.1 us
    pallas_call x1, Pallas kernels, fetch(): pl.pallas_call(functools.partial(fetch_kernel, parts, shares, len(sources...  7.95 us
    pallas_call x1, Pallas kernels, first_step(): pl.pallas_call(functools.partial(first_kernel, parts), out_shape=[pltpu.V...  5.68 us
    ppermute x13, waiting for transfers between devices, flipped(): lax.ppermute(value, axes, [(source, source ^ mask) for source in range(co...  5.52 us
    pallas_call x1, Pallas kernels, attention_half(): pl.pallas_call(functools.partial(attention_kernel, len(ready), len(blocks...  4.16 us
    pallas_call x1, Pallas kernels, feed_half(): pl.pallas_call(functools.partial(feed_kernel, len(feds), len(ups), len(do...  4.06 us
  transfers between devices with their start and end apart: 13, of which 4 were waited for; matrix products, arithmetic and copies ran while one was open for 1% of the time, Pallas kernels for 32%

profile of v5, /device:TPU:0, one launch (start us, length us, event | category | flops | bytes accessed | tf_op | source)
XLA Modules:
  0.0 43.2 jit_solution(5267045748745013923)
XLA Ops:
  0.6 3.0 %collective-permute-start = (bf16[16,2432]{1,0:T(8,128)(2,1)}, bf16[16,2432]{1,0:T(8,128)(2,1)S(1)}, u32[]{:S(2)}, u32[]{:S(2)}) collective-permute-start(bf16[16,2432]{1,0:T(8,128)(2,1)} %bitcast.23), channel_id=1, source_target_pairs={{0,16},{4,20},{8,24},{12,28},{16,0},{20,4},{24,8},{28,12},{1,17},{... | collective-permute-start | bytes 233480 | tf_op jit(solution)/shard_map/ppermute | solution.py:451
  3.6 1.5 %collective-permute-start.1 = (bf16[16,2432]{1,0:T(8,128)(2,1)}, bf16[16,2432]{1,0:T(8,128)(2,1)S(1)}, u32[]{:S(2)}, u32[]{:S(2)}) collective-permute-start(bf16[16,2432]{1,0:T(8,128)(2,1)} %bitcast.24), channel_id=1, source_target_pairs={{0,8},{4,12},{8,0},{12,4},{16,24},{20,28},{24,16},{28,20},{1,9},{5... | collective-permute-start | bytes 233480 | tf_op jit(solution)/shard_map/ppermute | solution.py:451
  5.2 0.0 collective-permute-start.2
  5.2 5.7 %shard_map.139 = (bf16[2432,1024]{1,0:T(8,128)(2,1)S(1)}, bf16[2432,1024]{1,0:T(8,128)(2,1)S(1)}, bf16[2432,1024]{1,0:T(8,128)(2,1)S(1)}, bf16[2,160,1024]{2,1,0:T(8,128)(2,1)S(1)}) custom-call(bf16[154,2,1024]{2,1,0:T(2,128)(2,1)} %bitcast.31, bf16[7296,1024]{1,0:T(8,128)(2,1)} %bitcast.30), custom_call_target="tpu_custom_call" | custom-call | bytes 29884416 | tf_op jit(solution)/shard_map/pallas_call | solution.py:113
  10.9 0.3 shard_map.140.refs_0_.refs_10_
  11.3 0.1 collective-permute-start.5
  12.0 0.9 %collective-permute-done.5.refs_1_ = bf16[64,2432]{1,0:T(8,128)(2,1)S(1)} collective-permute-done((bf16[64,2432]{1,0:T(8,128)(2,1)S(1)}, bf16[64,2432]{1,0:T(8,128)(2,1)S(1)}, u32[]{:S(2)}, u32[]{:S(2)}) %collective-permute-start.5) | collective-permute-done | bytes 311328 | tf_op jit(solution)/shard_map/ppermute | solution.py:451
  13.0 4.2 %shard_map.141.refs_2_.refs_4_ = bf16[32,2432]{1,0:T(8,128)(2,1)S(1)} custom-call(bf16[64,2432]{1,0:T(8,128)(2,1)S(1)} %shard_map.140.refs_0_.refs_10_, bf16[64,2432]{1,0:T(8,128)(2,1)S(1)} %collective-permute-done.5.refs_1_, s32[1,1]{1,0:T(1,128)} %bitcast.13.refs_2_, f32[8,2432]{1,0:T(8,128)S(1)} %bitcast.19, f32[2,64]{1,0:T(2,128)S(1)} %copy-done.4, ...), custom_call_target="tpu_custom_call" | custom-call | tf_op jit(solution)/shard_map/pallas_call | solution.py:288
  17.1 2.0 %collective-permute-start.6 = (bf16[32,2432]{1,0:T(8,128)(2,1)S(1)}, bf16[32,2432]{1,0:T(8,128)(2,1)S(1)}, u32[]{:S(2)}, u32[]{:S(2)}) collective-permute-start(bf16[32,2432]{1,0:T(8,128)(2,1)S(1)} %shard_map.141.refs_2_.refs_4_), channel_id=1, source_target_pairs={{0,16},{4,20},{8,24},{12,28},{16,0},{20,4},{24,8},{28,12},{1,17},{... | collective-permute-start | bytes 466952 | tf_op jit(solution)/shard_map/ppermute | solution.py:451
  19.1 0.2 collective-permute-start.8
  19.3 0.3 collective-permute-start.3
  19.6 0.2 collective-permute-start.4
  19.8 8.0 %shard_map.142 = (bf16[768,2432]{1,0:T(8,128)(2,1)S(1)}, bf16[768,2432]{1,0:T(8,128)(2,1)S(1)}, bf16[768,2432]{1,0:T(8,128)(2,1)S(1)}, bf16[128,2432]{1,0:T(8,12...) custom-call(bf16[2432,4864]{1,0:T(8,128)(2,1)} %refs_0_.1, ...), custom_call_target="tpu_custom_call" | custom-call | bytes 47316992 | tf_op jit(solution)/shard_map/pallas_call | solution.py:132
  27.8 0.4 shard_map.143
  28.2 4.1 %shard_map.144 = (bf16[16,2432]{1,0:T(8,128)(2,1)S(1)}, bf16[16,2432]{1,0:T(8,128)(2,1)S(1)}, bf16[16,2432]{1,0:T(8,128)(2,1)S(1)}, bf16[16,2432]{1,0:T(8,128)(2,1)S(1)}) custom-call(bf16[64,2432]{1,0:T(8,128)(2,1)S(1)} %get-tuple-element.43.refs_0_, bf16[768,2432]{1,0:T(8,128)(2,1)S(1)} %get-tuple-element.44.refs_1_, ...), custom_call_target="tpu_custom_call" | custom-call | tf_op jit(solution)/shard_map/pallas_call | solution.py:385
  32.3 2.0 %collective-permute-start.10 = (bf16[16,2432]{1,0:T(8,128)(2,1)S(1)}, bf16[16,2432]{1,0:T(8,128)(2,1)S(1)}, u32[]{:S(2)}, u32[]{:S(2)}) collective-permute-start(bf16[16,2432]{1,0:T(8,128)(2,1)S(1)} %get-tuple-element.55), channel_id=1, source_target_pairs={{0,16},{4,20},{8,24},{12,28},{16,0},{20,4},{24,8},{28,12},{1,17},{... | collective-permute-start | bytes 233480 | tf_op jit(solution)/shard_map/ppermute | solution.py:451
  34.3 0.2 collective-permute-start.9
  34.5 2.4 %collective-permute-done.10.refs_2_ = bf16[16,2432]{1,0:T(8,128)(2,1)S(1)} collective-permute-done((bf16[16,2432]{1,0:T(8,128)(2,1)S(1)}, bf16[16,2432]{1,0:T(8,128)(2,1)S(1)}, u32[]{:S(2)}, u32[]{:S(2)}) %collective-permute-start.10) | collective-permute-done | bytes 77856 | tf_op jit(solution)/shard_map/ppermute | solution.py:451
  36.9 1.4 %collective-permute-done.9.refs_1_ = bf16[16,2432]{1,0:T(8,128)(2,1)S(1)} collective-permute-done((bf16[16,2432]{1,0:T(8,128)(2,1)S(1)}, bf16[16,2432]{1,0:T(8,128)(2,1)S(1)}, u32[]{:S(2)}, u32[]{:S(2)}) %collective-permute-start.9) | collective-permute-done | bytes 77856 | tf_op jit(solution)/shard_map/ppermute | solution.py:451
  38.3 0.5 %shard_map.145 = (bf16[16,2432]{1,0:T(8,128)(2,1)S(1)}, f32[1,1024]{1,0:T(1,128)S(1)}) custom-call(f32[64,2432]{1,0:T(8,128)S(1)} %get-tuple-element.42.middle, bf16[16,2432]{1,0:T(8,128)(2,1)S(1)} %get-tuple-element.53.refs_0_, bf16[16,2432]{1,0:T(8,128)(2,1)S(1)} %collective-permute-done.9.refs_1_, bf16[16,2432]{1,0:T(8,128)(2,1)S(1)} %collective-permute-done.10.refs_2_, ...), custom_call_target="tpu_custom_call" | custom-call | tf_op jit(solution)/shard_map/pallas_call | solution.py:417
  38.8 1.6 %collective-permute-start.12 = (f32[1,1024]{1,0:T(1,128)S(1)}, f32[1,1024]{1,0:T(1,128)S(1)}, u32[]{:S(2)}, u32[]{:S(2)}) collective-permute-start(f32[1,1024]{1,0:T(1,128)S(1)} %get-tuple-element.58.raw), channel_id=1, source_target_pairs={{0,1},{1,0},{2,3},{3,2},{4,5},{5,4},{6,7},{7,6},{8,9},{9,8},{10,11... | collective-permute-start | bytes 12296 | tf_op jit(solution)/shard_map/ppermute | solution.py:451
  41.1 0.6 %copy.15 = bf16[1,1,16,2432]{3,2,1,0:T(8,128)(2,1)} copy(bf16[1,1,16,2432]{3,2,1,0:T(8,128)(2,1)S(1)} %bitcast.15) | data formatting | bytes 155648
  41.8 0.7 %collective-permute-done.12.partner = f32[1,1024]{1,0:T(1,128)S(1)} collective-permute-done((f32[1,1024]{1,0:T(1,128)S(1)}, f32[1,1024]{1,0:T(1,128)S(1)}, u32[]{:S(2)}, u32[]{:S(2)}) %collective-permute-start.12) | collective-permute-done | bytes 4128 | tf_op jit(solution)/shard_map/ppermute | solution.py:451
  42.5 0.7 %shard_map.146 = (f32[1,1024]{1,0:T(1,128)}, f32[1,1024]{1,0:T(1,128)}) custom-call(f32[1,1024]{1,0:T(1,128)S(1)} %get-tuple-element.58.raw, f32[1,1024]{1,0:T(1,128)S(1)} %collective-permute-done.12.partner, f32[1,1024]{1,0:T(1,128)S(1)} %bitcast.29, s32[1,1]{1,0:T(1,128)} %bitcast.14.index), custom_call_target="tpu_custom_call" | custom-call | tf_op jit(solution)/shard_map/pallas_call | solution.py:441
  (26 shorter events, 0.1 us)
Async XLA Ops:
  0.6 10.3 %collective-permute-start = (bf16[16,2432]{1,0:T(8,128)(2,1)}, bf16[16,2432]{1,0:T(8,128)(2,1)S(1)}, u32[]{:S(2)}, u32[]{:S(2)}) collective-permute-start(bf16[16,2432]{1,0:T(8,128)(2,1)} %bitcast.23), channel_id=1, source_target_pairs={{0,16},{4,20},{8,24},{12,28},{16,0},{20,4},{24,8},{28,12},{1,17},{... | collective-permute-start | bytes 233480 | tf_op jit(solution)/shard_map/ppermute | solution.py:451
  3.6 7.3 %collective-permute-start.1 = (bf16[16,2432]{1,0:T(8,128)(2,1)}, bf16[16,2432]{1,0:T(8,128)(2,1)S(1)}, u32[]{:S(2)}, u32[]{:S(2)}) collective-permute-start(bf16[16,2432]{1,0:T(8,128)(2,1)} %bitcast.24), channel_id=1, source_target_pairs={{0,8},{4,12},{8,0},{12,4},{16,24},{20,28},{24,16},{28,20},{1,9},{5... | collective-permute-start | bytes 233480 | tf_op jit(solution)/shard_map/ppermute | solution.py:451
  5.2 5.8 %collective-permute-start.2 = (bf16[16,2432]{1,0:T(8,128)(2,1)}, bf16[16,2432]{1,0:T(8,128)(2,1)S(1)}, u32[]{:S(2)}, u32[]{:S(2)}) collective-permute-start(bf16[16,2432]{1,0:T(8,128)(2,1)} %bitcast.25), channel_id=1, source_target_pairs={{0,24},{4,28},{8,16},{12,20},{16,8},{20,12},{24,0},{28,4},{1,25},{... | collective-permute-start | bytes 233480 | tf_op jit(solution)/shard_map/ppermute | solution.py:451
  5.2 7.8 %slice-start = ((s8[4980736]{0:T(1024)(128)(4,1)}), s8[4194304]{0:T(1024)(128)(4,1)S(1)}, s32[]{:S(2)}) async-start(s8[4980736]{0:T(1024)(128)(4,1)} %bitcast.16), calls=%async_computation | async-start | bytes 8388608
  5.2 5.7 %copy-start = (f32[1,8,2432]{2,1,0:T(8,128)S(1)}, f32[1,8,2432]{2,1,0:T(8,128)}, u32[]{:S(2)}) copy-start(f32[1,8,2432]{2,1,0:T(8,128)} %param.15) | copy-start | bytes 233476
  5.2 5.8 %copy-start.2 = (bf16[1,1,16,2432]{3,2,1,0:T(8,128)(2,1)S(1)}, bf16[1,1,16,2432]{3,2,1,0:T(8,128)(2,1)}, u32[]{:S(2)}) copy-start(bf16[1,1,16,2432]{3,2,1,0:T(8,128)(2,1)} %param.12) | copy-start | bytes 233476
  5.2 7.8 %slice-start.1 = ((s8[4980736]{0:T(1024)(128)(4,1)}), s8[786432]{0:T(1024)(128)(4,1)S(1)}, s32[]{:S(2)}) async-start(s8[4980736]{0:T(1024)(128)(4,1)} %bitcast.16), calls=%async_computation.1 | async-start | bytes 1572864
  5.2 7.8 %copy-start.4 = (f32[2,64]{1,0:T(2,128)S(1)}, f32[2,64]{1,0:T(2,128)}, u32[]{:S(2)}) copy-start(f32[2,64]{1,0:T(2,128)} %refs_4_.1) | copy-start | bytes 1540
  11.3 1.7 %collective-permute-start.5 = (bf16[64,2432]{1,0:T(8,128)(2,1)S(1)}, bf16[64,2432]{1,0:T(8,128)(2,1)S(1)}, u32[]{:S(2)}, u32[]{:S(2)}) collective-permute-start(bf16[64,2432]{1,0:T(8,128)(2,1)S(1)} %shard_map.140.refs_0_.refs_10_), channel_id=1, source_target_pairs={{0,4},{4,0},{8,12},{12,8},{16,20},{20,16},{24,28},{28,24},{1,5},{5... | collective-permute-start | bytes 933896 | tf_op jit(solution)/shard_map/ppermute | solution.py:451
  17.1 10.7 %collective-permute-start.6 = (bf16[32,2432]{1,0:T(8,128)(2,1)S(1)}, bf16[32,2432]{1,0:T(8,128)(2,1)S(1)}, u32[]{:S(2)}, u32[]{:S(2)}) collective-permute-start(bf16[32,2432]{1,0:T(8,128)(2,1)S(1)} %shard_map.141.refs_2_.refs_4_), channel_id=1, source_target_pairs={{0,16},{4,20},{8,24},{12,28},{16,0},{20,4},{24,8},{28,12},{1,17},{... | collective-permute-start | bytes 466952 | tf_op jit(solution)/shard_map/ppermute | solution.py:451
  19.1 8.7 %collective-permute-start.7 = (bf16[32,2432]{1,0:T(8,128)(2,1)S(1)}, bf16[32,2432]{1,0:T(8,128)(2,1)S(1)}, u32[]{:S(2)}, u32[]{:S(2)}) collective-permute-start(bf16[32,2432]{1,0:T(8,128)(2,1)S(1)} %shard_map.141.refs_2_.refs_4_), channel_id=1, source_target_pairs={{0,4},{4,0},{8,12},{12,8},{16,20},{20,16},{24,28},{28,24},{1,5},{5... | collective-permute-start | bytes 466952 | tf_op jit(solution)/shard_map/ppermute | solution.py:451
  19.1 8.7 %collective-permute-start.8 = (bf16[32,2432]{1,0:T(8,128)(2,1)S(1)}, bf16[32,2432]{1,0:T(8,128)(2,1)S(1)}, u32[]{:S(2)}, u32[]{:S(2)}) collective-permute-start(bf16[32,2432]{1,0:T(8,128)(2,1)S(1)} %shard_map.141.refs_2_.refs_4_), channel_id=1, source_target_pairs={{0,20},{4,16},{8,28},{12,24},{16,4},{20,0},{24,12},{28,8},{1,21},{... | collective-permute-start | bytes 466952 | tf_op jit(solution)/shard_map/ppermute | solution.py:451
  19.3 8.5 %collective-permute-start.3 = (bf16[16,2432]{1,0:T(8,128)(2,1)S(1)}, bf16[16,2432]{1,0:T(8,128)(2,1)S(1)}, u32[]{:S(2)}, u32[]{:S(2)}) collective-permute-start(bf16[16,2432]{1,0:T(8,128)(2,1)S(1)} %bitcast.27), channel_id=1, source_target_pairs={{0,4},{4,0},{8,12},{12,8},{16,20},{20,16},{24,28},{28,24},{1,5},{5... | collective-permute-start | bytes 233480 | tf_op jit(solution)/shard_map/ppermute | solution.py:451
  19.6 8.2 %collective-permute-start.4 = (bf16[16,2432]{1,0:T(8,128)(2,1)S(1)}, bf16[16,2432]{1,0:T(8,128)(2,1)S(1)}, u32[]{:S(2)}, u32[]{:S(2)}) collective-permute-start(bf16[16,2432]{1,0:T(8,128)(2,1)S(1)} %collective-permute-done.refs_1_), channel_id=1, source_target_pairs={{0,4},{4,0},{8,12},{12,8},{16,20},{20,16},{24,28},{28,24},{1,5},{5... | collective-permute-start | bytes 233480 | tf_op jit(solution)/shard_map/ppermute | solution.py:451
  28.2 10.1 %copy-start.1 = (bf16[2432,64]{0,1:T(8,128)(2,1)S(1)}, bf16[2432,64]{0,1:T(8,128)(2,1)}, u32[]{:S(2)}) copy-start(bf16[2432,64]{0,1:T(8,128)(2,1)} %param.21) | copy-start | bytes 933892
  28.2 14.3 %copy-start.3 = (f32[1,1,1024]{2,1,0:T(1,128)S(1)}, f32[1,1,1024]{2,1,0:T(1,128)}, u32[]{:S(2)}) copy-start(f32[1,1,1024]{2,1,0:T(1,128)} %param.23) | copy-start | bytes 12292
  32.3 4.6 %collective-permute-start.10 = (bf16[16,2432]{1,0:T(8,128)(2,1)S(1)}, bf16[16,2432]{1,0:T(8,128)(2,1)S(1)}, u32[]{:S(2)}, u32[]{:S(2)}) collective-permute-start(bf16[16,2432]{1,0:T(8,128)(2,1)S(1)} %get-tuple-element.55), channel_id=1, source_target_pairs={{0,16},{4,20},{8,24},{12,28},{16,0},{20,4},{24,8},{28,12},{1,17},{... | collective-permute-start | bytes 233480 | tf_op jit(solution)/shard_map/ppermute | solution.py:451
  34.3 2.6 %collective-permute-start.11 = (bf16[16,2432]{1,0:T(8,128)(2,1)S(1)}, bf16[16,2432]{1,0:T(8,128)(2,1)S(1)}, u32[]{:S(2)}, u32[]{:S(2)}) collective-permute-start(bf16[16,2432]{1,0:T(8,128)(2,1)S(1)} %get-tuple-element.56), channel_id=1, source_target_pairs={{0,4},{4,0},{8,12},{12,8},{16,20},{20,16},{24,28},{28,24},{1,5},{5... | collective-permute-start | bytes 233480 | tf_op jit(solution)/shard_map/ppermute | solution.py:451
  34.3 4.0 %collective-permute-start.9 = (bf16[16,2432]{1,0:T(8,128)(2,1)S(1)}, bf16[16,2432]{1,0:T(8,128)(2,1)S(1)}, u32[]{:S(2)}, u32[]{:S(2)}) collective-permute-start(bf16[16,2432]{1,0:T(8,128)(2,1)S(1)} %get-tuple-element.54), channel_id=1, source_target_pairs={{0,20},{4,16},{8,28},{12,24},{16,4},{20,0},{24,12},{28,8},{1,21},{... | collective-permute-start | bytes 233480 | tf_op jit(solution)/shard_map/ppermute | solution.py:451
  38.8 3.7 %collective-permute-start.12 = (f32[1,1024]{1,0:T(1,128)S(1)}, f32[1,1024]{1,0:T(1,128)S(1)}, u32[]{:S(2)}, u32[]{:S(2)}) collective-permute-start(f32[1,1024]{1,0:T(1,128)S(1)} %get-tuple-element.58.raw), channel_id=1, source_target_pairs={{0,1},{1,0},{2,3},{3,2},{4,5},{5,4},{6,7},{7,6},{8,9},{9,8},{10,11... | collective-permute-start | bytes 12296 | tf_op jit(solution)/shard_map/ppermute | solution.py:451

commit v6 on v5

--- a/solution.py
+++ b/solution.py
@@ -288,7 +288,7 @@
     return pl.pallas_call(
         functools.partial(attention_kernel, len(ready), len(blocks), own_rows),
         out_shape=jax.ShapeDtypeStruct((own_rows, width), jnp.bfloat16),
-        in_specs=[IN_VMEM] * (len(ready) + len(blocks)) + [IN_VMEM] * 8 + [IN_PLACE],
+        in_specs=[IN_VMEM] * (len(ready) + len(blocks)) + [IN_VMEM] * 8 + [IN_PLACE] * len(after),
         out_specs=IN_VMEM,
         scratch_shapes=[
             pltpu.VMEM((all_rows, width), jnp.bfloat16),
@@ -307,7 +307,7 @@
         text,
         *[in_vmem(part) for part in in_ws],
         in_vmem(out_w),
-        after,
+        *after,
     )
 
 
@@ -491,11 +491,12 @@
         own_blocks = near[:2]
         normed = norm_step(near, mod)
         ready, far = [normed, flipped(normed, both, 1, count)], []
+        peer_blocks = [flipped(part, both, 1, count) for part in own_blocks]
     else:
         gathered = lax.all_gather(tile, ("col", "row"), axis=0, tiled=True)
         far = [jnp.roll(gathered, -lax.axis_index("col") * own_rows, axis=0)]
         own_blocks = [far[0][:own_rows]]
-        ready, normed = [], tile
+        ready, normed, peer_blocks = [], tile, []
         *in_ws, text = first_step(text_keys_values[0], in_w, thirds)
     mine = attention_half(
         ready,
@@ -507,11 +508,11 @@
         text,
         in_ws,
         output_weight,
-        normed,
+        (normed, *peer_blocks),
     )
     if split:
         sums = [mine] + [flipped(mine, both, mask, count) for mask in (n_col, 1, n_col + 1)]
-        own_blocks = own_blocks + [flipped(part, both, 1, count) for part in own_blocks]
+        own_blocks = own_blocks + peer_blocks
     elif paired:
         sums = [mine, flipped(mine, "row", 1, n_row)]
     else:

time: 43.4 us -> 43 us (level)
  transfers between devices with their start and end apart: 13 -> 13, of which waited for: 4 -> 5; matrix products, arithmetic and copies ran while one was open for 1% -> 1% of each run, Pallas kernels for 32% -> 32%
where the time goes in v6:
time: 43 us; the launch traced here: 42.9 us
  Pallas kernels  23.8 us (55%)
  starting transfers between devices  11.2 us (26%)
  waiting for transfers between devices  5.16 us (12%)
  between operations  2.11 us (5%)
  local copies, waits for them, and re-layouts  0.67 us (2%)
    ppermute x13, starting transfers between devices, flipped(): lax.ppermute(value, axes, [(source, source ^ mask) for source in range(co...  11.2 us
    pallas_call x1, Pallas kernels, fetch(): pl.pallas_call(functools.partial(fetch_kernel, parts, shares, len(sources...  7.95 us
    pallas_call x1, Pallas kernels, first_step(): pl.pallas_call(functools.partial(first_kernel, parts), out_shape=[pltpu.V...  5.68 us
    ppermute x13, waiting for transfers between devices, flipped(): lax.ppermute(value, axes, [(source, source ^ mask) for source in range(co...  5.16 us
    pallas_call x1, Pallas kernels, attention_half(): pl.pallas_call(functools.partial(attention_kernel, len(ready), len(blocks...  4.15 us
    pallas_call x1, Pallas kernels, feed_half(): pl.pallas_call(functools.partial(feed_kernel, len(feds), len(ups), len(do...  4.06 us
  transfers between devices with their start and end apart: 13, of which 5 were waited for; matrix products, arithmetic and copies ran while one was open for 1% of the time, Pallas kernels for 32%

profile of v6, /device:TPU:0, one launch (start us, length us, event | category | flops | bytes accessed | tf_op | source)
XLA Modules:
  0.0 42.9 jit_solution(15719151368786452178)
XLA Ops:
  0.6 3.0 %collective-permute-start = (bf16[16,2432]{1,0:T(8,128)(2,1)}, bf16[16,2432]{1,0:T(8,128)(2,1)S(1)}, u32[]{:S(2)}, u32[]{:S(2)}) collective-permute-start(bf16[16,2432]{1,0:T(8,128)(2,1)} %bitcast.23), channel_id=1, source_target_pairs={{0,16},{4,20},{8,24},{12,28},{16,0},{20,4},{24,8},{28,12},{1,17},{... | collective-permute-start | bytes 233480 | tf_op jit(solution)/shard_map/ppermute | solution.py:451
  3.6 1.5 %collective-permute-start.1 = (bf16[16,2432]{1,0:T(8,128)(2,1)}, bf16[16,2432]{1,0:T(8,128)(2,1)S(1)}, u32[]{:S(2)}, u32[]{:S(2)}) collective-permute-start(bf16[16,2432]{1,0:T(8,128)(2,1)} %bitcast.24), channel_id=1, source_target_pairs={{0,8},{4,12},{8,0},{12,4},{16,24},{20,28},{24,16},{28,20},{1,9},{5... | collective-permute-start | bytes 233480 | tf_op jit(solution)/shard_map/ppermute | solution.py:451
  5.2 5.7 %shard_map.139 = (bf16[2432,1024]{1,0:T(8,128)(2,1)S(1)}, bf16[2432,1024]{1,0:T(8,128)(2,1)S(1)}, bf16[2432,1024]{1,0:T(8,128)(2,1)S(1)}, bf16[2,160,1024]{2,1,0:T(8,128)(2,1)S(1)}) custom-call(bf16[154,2,1024]{2,1,0:T(2,128)(2,1)} %bitcast.31, bf16[7296,1024]{1,0:T(8,128)(2,1)} %bitcast.30), custom_call_target="tpu_custom_call" | custom-call | bytes 29884416 | tf_op jit(solution)/shard_map/pallas_call | solution.py:113
  10.9 0.3 shard_map.140.refs_0_.refs_10_
  11.3 0.1 collective-permute-start.5
  11.4 0.5 %collective-permute-start.3 = (bf16[16,2432]{1,0:T(8,128)(2,1)S(1)}, bf16[16,2432]{1,0:T(8,128)(2,1)S(1)}, u32[]{:S(2)}, u32[]{:S(2)}) collective-permute-start(bf16[16,2432]{1,0:T(8,128)(2,1)S(1)} %bitcast.27), channel_id=1, source_target_pairs={{0,4},{4,0},{8,12},{12,8},{16,20},{20,16},{24,28},{28,24},{1,5},{5... | collective-permute-start | bytes 233480 | tf_op jit(solution)/shard_map/ppermute | solution.py:451
  11.9 0.1 collective-permute-start.4
  12.6 0.5 %collective-permute-done.3.refs_11_.refs_2_ = bf16[16,2432]{1,0:T(8,128)(2,1)S(1)} collective-permute-done((bf16[16,2432]{1,0:T(8,128)(2,1)S(1)}, bf16[16,2432]{1,0:T(8,128)(2,1)S(1)}, u32[]{:S(2)}, u32[]{:S(2)}) %collective-permute-start.3) | collective-permute-done | bytes 77856 | tf_op jit(solution)/shard_map/ppermute | solution.py:451
  13.1 0.1 collective-permute-done.4.refs_12_.refs_3_
  13.2 4.2 %shard_map.141.refs_2_.refs_4_ = bf16[32,2432]{1,0:T(8,128)(2,1)S(1)} custom-call(bf16[64,2432]{1,0:T(8,128)(2,1)S(1)} %shard_map.140.refs_0_.refs_10_, bf16[64,2432]{1,0:T(8,128)(2,1)S(1)} %collective-permute-done.5.refs_1_, s32[1,1]{1,0:T(1,128)} %bitcast.13.refs_2_, f32[8,2432]{1,0:T(8,128)S(1)} %bitcast.19, f32[2,64]{1,0:T(2,128)S(1)} %copy-done.4, ...), custom_call_target="tpu_custom_call" | custom-call | tf_op jit(solution)/shard_map/pallas_call | solution.py:288
  17.4 2.0 %collective-permute-start.6 = (bf16[32,2432]{1,0:T(8,128)(2,1)S(1)}, bf16[32,2432]{1,0:T(8,128)(2,1)S(1)}, u32[]{:S(2)}, u32[]{:S(2)}) collective-permute-start(bf16[32,2432]{1,0:T(8,128)(2,1)S(1)} %shard_map.141.refs_2_.refs_4_), channel_id=1, source_target_pairs={{0,16},{4,20},{8,24},{12,28},{16,0},{20,4},{24,8},{28,12},{1,17},{... | collective-permute-start | bytes 466952 | tf_op jit(solution)/shard_map/ppermute | solution.py:451
  19.3 0.2 collective-permute-start.8
  19.5 8.0 %shard_map.142 = (bf16[768,2432]{1,0:T(8,128)(2,1)S(1)}, bf16[768,2432]{1,0:T(8,128)(2,1)S(1)}, bf16[768,2432]{1,0:T(8,128)(2,1)S(1)}, bf16[128,2432]{1,0:T(8,12...) custom-call(bf16[2432,4864]{1,0:T(8,128)(2,1)} %refs_0_.1, ...), custom_call_target="tpu_custom_call" | custom-call | bytes 47316992 | tf_op jit(solution)/shard_map/pallas_call | solution.py:132
  27.5 0.4 shard_map.143
  27.9 4.1 %shard_map.144 = (bf16[16,2432]{1,0:T(8,128)(2,1)S(1)}, bf16[16,2432]{1,0:T(8,128)(2,1)S(1)}, bf16[16,2432]{1,0:T(8,128)(2,1)S(1)}, bf16[16,2432]{1,0:T(8,128)(2,1)S(1)}) custom-call(bf16[64,2432]{1,0:T(8,128)(2,1)S(1)} %get-tuple-element.43.refs_0_, bf16[768,2432]{1,0:T(8,128)(2,1)S(1)} %get-tuple-element.44.refs_1_, ...), custom_call_target="tpu_custom_call" | custom-call | tf_op jit(solution)/shard_map/pallas_call | solution.py:385
  32.0 2.0 %collective-permute-start.10 = (bf16[16,2432]{1,0:T(8,128)(2,1)S(1)}, bf16[16,2432]{1,0:T(8,128)(2,1)S(1)}, u32[]{:S(2)}, u32[]{:S(2)}) collective-permute-start(bf16[16,2432]{1,0:T(8,128)(2,1)S(1)} %get-tuple-element.55), channel_id=1, source_target_pairs={{0,16},{4,20},{8,24},{12,28},{16,0},{20,4},{24,8},{28,12},{1,17},{... | collective-permute-start | bytes 233480 | tf_op jit(solution)/shard_map/ppermute | solution.py:451
  34.0 0.2 collective-permute-start.9
  34.2 2.4 %collective-permute-done.10.refs_2_ = bf16[16,2432]{1,0:T(8,128)(2,1)S(1)} collective-permute-done((bf16[16,2432]{1,0:T(8,128)(2,1)S(1)}, bf16[16,2432]{1,0:T(8,128)(2,1)S(1)}, u32[]{:S(2)}, u32[]{:S(2)}) %collective-permute-start.10) | collective-permute-done | bytes 77856 | tf_op jit(solution)/shard_map/ppermute | solution.py:451
  36.6 1.4 %collective-permute-done.9.refs_1_ = bf16[16,2432]{1,0:T(8,128)(2,1)S(1)} collective-permute-done((bf16[16,2432]{1,0:T(8,128)(2,1)S(1)}, bf16[16,2432]{1,0:T(8,128)(2,1)S(1)}, u32[]{:S(2)}, u32[]{:S(2)}) %collective-permute-start.9) | collective-permute-done | bytes 77856 | tf_op jit(solution)/shard_map/ppermute | solution.py:451
  38.0 0.5 %shard_map.145 = (bf16[16,2432]{1,0:T(8,128)(2,1)S(1)}, f32[1,1024]{1,0:T(1,128)S(1)}) custom-call(f32[64,2432]{1,0:T(8,128)S(1)} %get-tuple-element.42.middle, bf16[16,2432]{1,0:T(8,128)(2,1)S(1)} %get-tuple-element.53.refs_0_, bf16[16,2432]{1,0:T(8,128)(2,1)S(1)} %collective-permute-done.9.refs_1_, bf16[16,2432]{1,0:T(8,128)(2,1)S(1)} %collective-permute-done.10.refs_2_, ...), custom_call_target="tpu_custom_call" | custom-call | tf_op jit(solution)/shard_map/pallas_call | solution.py:417
  38.5 1.6 %collective-permute-start.12 = (f32[1,1024]{1,0:T(1,128)S(1)}, f32[1,1024]{1,0:T(1,128)S(1)}, u32[]{:S(2)}, u32[]{:S(2)}) collective-permute-start(f32[1,1024]{1,0:T(1,128)S(1)} %get-tuple-element.58.raw), channel_id=1, source_target_pairs={{0,1},{1,0},{2,3},{3,2},{4,5},{5,4},{6,7},{7,6},{8,9},{9,8},{10,11... | collective-permute-start | bytes 12296 | tf_op jit(solution)/shard_map/ppermute | solution.py:451
  40.8 0.6 %copy.15 = bf16[1,1,16,2432]{3,2,1,0:T(8,128)(2,1)} copy(bf16[1,1,16,2432]{3,2,1,0:T(8,128)(2,1)S(1)} %bitcast.15) | data formatting | bytes 155648
  41.5 0.7 %collective-permute-done.12.partner = f32[1,1024]{1,0:T(1,128)S(1)} collective-permute-done((f32[1,1024]{1,0:T(1,128)S(1)}, f32[1,1024]{1,0:T(1,128)S(1)}, u32[]{:S(2)}, u32[]{:S(2)}) %collective-permute-start.12) | collective-permute-done | bytes 4128 | tf_op jit(solution)/shard_map/ppermute | solution.py:451
  42.2 0.7 %shard_map.146 = (f32[1,1024]{1,0:T(1,128)}, f32[1,1024]{1,0:T(1,128)}) custom-call(f32[1,1024]{1,0:T(1,128)S(1)} %get-tuple-element.58.raw, f32[1,1024]{1,0:T(1,128)S(1)} %collective-permute-done.12.partner, f32[1,1024]{1,0:T(1,128)S(1)} %bitcast.29, s32[1,1]{1,0:T(1,128)} %bitcast.14.index), custom_call_target="tpu_custom_call" | custom-call | tf_op jit(solution)/shard_map/pallas_call | solution.py:441
  (26 shorter events, 0.1 us)
Async XLA Ops:
  0.6 10.3 %collective-permute-start = (bf16[16,2432]{1,0:T(8,128)(2,1)}, bf16[16,2432]{1,0:T(8,128)(2,1)S(1)}, u32[]{:S(2)}, u32[]{:S(2)}) collective-permute-start(bf16[16,2432]{1,0:T(8,128)(2,1)} %bitcast.23), channel_id=1, source_target_pairs={{0,16},{4,20},{8,24},{12,28},{16,0},{20,4},{24,8},{28,12},{1,17},{... | collective-permute-start | bytes 233480 | tf_op jit(solution)/shard_map/ppermute | solution.py:451
  3.6 7.3 %collective-permute-start.1 = (bf16[16,2432]{1,0:T(8,128)(2,1)}, bf16[16,2432]{1,0:T(8,128)(2,1)S(1)}, u32[]{:S(2)}, u32[]{:S(2)}) collective-permute-start(bf16[16,2432]{1,0:T(8,128)(2,1)} %bitcast.24), channel_id=1, source_target_pairs={{0,8},{4,12},{8,0},{12,4},{16,24},{20,28},{24,16},{28,20},{1,9},{5... | collective-permute-start | bytes 233480 | tf_op jit(solution)/shard_map/ppermute | solution.py:451
  5.2 5.8 %collective-permute-start.2 = (bf16[16,2432]{1,0:T(8,128)(2,1)}, bf16[16,2432]{1,0:T(8,128)(2,1)S(1)}, u32[]{:S(2)}, u32[]{:S(2)}) collective-permute-start(bf16[16,2432]{1,0:T(8,128)(2,1)} %bitcast.25), channel_id=1, source_target_pairs={{0,24},{4,28},{8,16},{12,20},{16,8},{20,12},{24,0},{28,4},{1,25},{... | collective-permute-start | bytes 233480 | tf_op jit(solution)/shard_map/ppermute | solution.py:451
  5.2 8.0 %slice-start = ((s8[4980736]{0:T(1024)(128)(4,1)}), s8[4194304]{0:T(1024)(128)(4,1)S(1)}, s32[]{:S(2)}) async-start(s8[4980736]{0:T(1024)(128)(4,1)} %bitcast.16), calls=%async_computation | async-start | bytes 8388608
  5.2 5.7 %copy-start = (f32[1,8,2432]{2,1,0:T(8,128)S(1)}, f32[1,8,2432]{2,1,0:T(8,128)}, u32[]{:S(2)}) copy-start(f32[1,8,2432]{2,1,0:T(8,128)} %param.15) | copy-start | bytes 233476
  5.2 5.8 %copy-start.2 = (bf16[1,1,16,2432]{3,2,1,0:T(8,128)(2,1)S(1)}, bf16[1,1,16,2432]{3,2,1,0:T(8,128)(2,1)}, u32[]{:S(2)}) copy-start(bf16[1,1,16,2432]{3,2,1,0:T(8,128)(2,1)} %param.12) | copy-start | bytes 233476
  5.2 8.0 %slice-start.1 = ((s8[4980736]{0:T(1024)(128)(4,1)}), s8[786432]{0:T(1024)(128)(4,1)S(1)}, s32[]{:S(2)}) async-start(s8[4980736]{0:T(1024)(128)(4,1)} %bitcast.16), calls=%async_computation.1 | async-start | bytes 1572864
  5.2 8.0 %copy-start.4 = (f32[2,64]{1,0:T(2,128)S(1)}, f32[2,64]{1,0:T(2,128)}, u32[]{:S(2)}) copy-start(f32[2,64]{1,0:T(2,128)} %refs_4_.1) | copy-start | bytes 1540
  11.3 1.9 %collective-permute-start.5 = (bf16[64,2432]{1,0:T(8,128)(2,1)S(1)}, bf16[64,2432]{1,0:T(8,128)(2,1)S(1)}, u32[]{:S(2)}, u32[]{:S(2)}) collective-permute-start(bf16[64,2432]{1,0:T(8,128)(2,1)S(1)} %shard_map.140.refs_0_.refs_10_), channel_id=1, source_target_pairs={{0,4},{4,0},{8,12},{12,8},{16,20},{20,16},{24,28},{28,24},{1,5},{5... | collective-permute-start | bytes 933896 | tf_op jit(solution)/shard_map/ppermute | solution.py:451
  11.4 1.7 %collective-permute-start.3 = (bf16[16,2432]{1,0:T(8,128)(2,1)S(1)}, bf16[16,2432]{1,0:T(8,128)(2,1)S(1)}, u32[]{:S(2)}, u32[]{:S(2)}) collective-permute-start(bf16[16,2432]{1,0:T(8,128)(2,1)S(1)} %bitcast.27), channel_id=1, source_target_pairs={{0,4},{4,0},{8,12},{12,8},{16,20},{20,16},{24,28},{28,24},{1,5},{5... | collective-permute-start | bytes 233480 | tf_op jit(solution)/shard_map/ppermute | solution.py:451
  11.9 1.3 %collective-permute-start.4 = (bf16[16,2432]{1,0:T(8,128)(2,1)S(1)}, bf16[16,2432]{1,0:T(8,128)(2,1)S(1)}, u32[]{:S(2)}, u32[]{:S(2)}) collective-permute-start(bf16[16,2432]{1,0:T(8,128)(2,1)S(1)} %collective-permute-done.refs_1_), channel_id=1, source_target_pairs={{0,4},{4,0},{8,12},{12,8},{16,20},{20,16},{24,28},{28,24},{1,5},{5... | collective-permute-start | bytes 233480 | tf_op jit(solution)/shard_map/ppermute | solution.py:451
  17.4 10.1 %collective-permute-start.6 = (bf16[32,2432]{1,0:T(8,128)(2,1)S(1)}, bf16[32,2432]{1,0:T(8,128)(2,1)S(1)}, u32[]{:S(2)}, u32[]{:S(2)}) collective-permute-start(bf16[32,2432]{1,0:T(8,128)(2,1)S(1)} %shard_map.141.refs_2_.refs_4_), channel_id=1, source_target_pairs={{0,16},{4,20},{8,24},{12,28},{16,0},{20,4},{24,8},{28,12},{1,17},{... | collective-permute-start | bytes 466952 | tf_op jit(solution)/shard_map/ppermute | solution.py:451
  19.3 8.2 %collective-permute-start.7 = (bf16[32,2432]{1,0:T(8,128)(2,1)S(1)}, bf16[32,2432]{1,0:T(8,128)(2,1)S(1)}, u32[]{:S(2)}, u32[]{:S(2)}) collective-permute-start(bf16[32,2432]{1,0:T(8,128)(2,1)S(1)} %shard_map.141.refs_2_.refs_4_), channel_id=1, source_target_pairs={{0,4},{4,0},{8,12},{12,8},{16,20},{20,16},{24,28},{28,24},{1,5},{5... | collective-permute-start | bytes 466952 | tf_op jit(solution)/shard_map/ppermute | solution.py:451
  19.3 8.2 %collective-permute-start.8 = (bf16[32,2432]{1,0:T(8,128)(2,1)S(1)}, bf16[32,2432]{1,0:T(8,128)(2,1)S(1)}, u32[]{:S(2)}, u32[]{:S(2)}) collective-permute-start(bf16[32,2432]{1,0:T(8,128)(2,1)S(1)} %shard_map.141.refs_2_.refs_4_), channel_id=1, source_target_pairs={{0,20},{4,16},{8,28},{12,24},{16,4},{20,0},{24,12},{28,8},{1,21},{... | collective-permute-start | bytes 466952 | tf_op jit(solution)/shard_map/ppermute | solution.py:451
  27.9 10.1 %copy-start.1 = (bf16[2432,64]{0,1:T(8,128)(2,1)S(1)}, bf16[2432,64]{0,1:T(8,128)(2,1)}, u32[]{:S(2)}) copy-start(bf16[2432,64]{0,1:T(8,128)(2,1)} %param.21) | copy-start | bytes 933892
  27.9 14.3 %copy-start.3 = (f32[1,1,1024]{2,1,0:T(1,128)S(1)}, f32[1,1,1024]{2,1,0:T(1,128)}, u32[]{:S(2)}) copy-start(f32[1,1,1024]{2,1,0:T(1,128)} %param.23) | copy-start | bytes 12292
  32.0 4.6 %collective-permute-start.10 = (bf16[16,2432]{1,0:T(8,128)(2,1)S(1)}, bf16[16,2432]{1,0:T(8,128)(2,1)S(1)}, u32[]{:S(2)}, u32[]{:S(2)}) collective-permute-start(bf16[16,2432]{1,0:T(8,128)(2,1)S(1)} %get-tuple-element.55), channel_id=1, source_target_pairs={{0,16},{4,20},{8,24},{12,28},{16,0},{20,4},{24,8},{28,12},{1,17},{... | collective-permute-start | bytes 233480 | tf_op jit(solution)/shard_map/ppermute | solution.py:451
  34.0 2.6 %collective-permute-start.11 = (bf16[16,2432]{1,0:T(8,128)(2,1)S(1)}, bf16[16,2432]{1,0:T(8,128)(2,1)S(1)}, u32[]{:S(2)}, u32[]{:S(2)}) collective-permute-start(bf16[16,2432]{1,0:T(8,128)(2,1)S(1)} %get-tuple-element.56), channel_id=1, source_target_pairs={{0,4},{4,0},{8,12},{12,8},{16,20},{20,16},{24,28},{28,24},{1,5},{5... | collective-permute-start | bytes 233480 | tf_op jit(solution)/shard_map/ppermute | solution.py:451
  34.0 4.0 %collective-permute-start.9 = (bf16[16,2432]{1,0:T(8,128)(2,1)S(1)}, bf16[16,2432]{1,0:T(8,128)(2,1)S(1)}, u32[]{:S(2)}, u32[]{:S(2)}) collective-permute-start(bf16[16,2432]{1,0:T(8,128)(2,1)S(1)} %get-tuple-element.54), channel_id=1, source_target_pairs={{0,20},{4,16},{8,28},{12,24},{16,4},{20,0},{24,12},{28,8},{1,21},{... | collective-permute-start | bytes 233480 | tf_op jit(solution)/shard_map/ppermute | solution.py:451
  38.5 3.7 %collective-permute-start.12 = (f32[1,1024]{1,0:T(1,128)S(1)}, f32[1,1024]{1,0:T(1,128)S(1)}, u32[]{:S(2)}, u32[]{:S(2)}) collective-permute-start(f32[1,1024]{1,0:T(1,128)S(1)} %get-tuple-element.58.raw), channel_id=1, source_target_pairs={{0,1},{1,0},{2,3},{3,2},{4,5},{5,4},{6,7},{7,6},{8,9},{9,8},{10,11... | collective-permute-start | bytes 12296 | tf_op jit(solution)/shard_map/ppermute | solution.py:451
